TPU v7x, 128 devices: a whole 4x4x4 slice. The times are simulated.
128 devices in a mesh: section: 2 (over x_hi), rep: 8 (over z, x_lo), shard: 8 (over y, core).
Axes of the slice: x: 4 (x_hi: 2, x_lo: 2; x = x_hi * 2 + x_lo), y: 4, z: 4, core: 2. Of those that a mesh axis runs over, the one named last changes fastest.
Arguments:
- tokens_in: bfloat16 [2, 8, 512, 1536], P(None, 'rep', 'shard'), may hold values from -6 to 6
- cotangent: bfloat16 [2, 8, 512, 1536], P(None, 'rep', 'shard'), may hold values from -6 to 6
- routes: int32 [2, 2, 8, 512, 4], P('section', None, 'rep', 'shard'), may hold values from 0 to 7, all different within a row; in each aligned block of 64 rows (0 to 63, 64 to 127, ..., all dimensions but the last counted through in order) at most 40 rows name the same one
- gain_attn: bfloat16 [2, 1536], P('section', 'shard'), may hold values from 0.5 to 1.5
- w_query: bfloat16 [2, 1536, 1536], P('section', 'shard'), may hold values from -0.21875 to 0.21875
- w_keyval: bfloat16 [2, 1536, 512], P('section', 'shard'), may hold values from -0.15625 to 0.15625
- w_out: bfloat16 [2, 1536, 1536], P('section', 'shard'), may hold values from -1.25 to 1.25
- gain_moe: bfloat16 [2, 1536], P('section', 'shard'), may hold values from 0.5 to 1.5
- w_router: bfloat16 [2, 1536, 8], P('section', 'shard'), may hold values from -0.078125 to 0.078125
- w_in: bfloat16 [2, 8, 1536, 1536], P('section', 'shard'), may hold values from -0.15625 to 0.15625
- w_down: bfloat16 [2, 8, 768, 1536], P('section', 'shard'), may hold values from -0.4375 to 0.4375
Outputs:
- acts: bfloat16 [2, 2, 8, 512, 1536], P('section', None, 'rep', 'shard')
- input_grads: float32 [2, 2, 8, 512, 1536], P('section', None, 'rep', 'shard')
- grad_gain_attn: float32 [2, 1536], P('section', 'shard')
- grad_query: float32 [2, 1536, 1536], P('section', 'shard', 'rep')
- grad_keyval: float32 [2, 1536, 512], P('section', 'shard', 'rep')
- grad_out: float32 [2, 1536, 1536], P('section', 'shard', 'rep')
- grad_gain_moe: float32 [2, 1536], P('section', 'shard')
- grad_router: float32 [2, 1536, 8], P('section', 'shard')
- grad_in: float32 [2, 8, 1536, 1536], P('section', 'shard', 'rep')
- grad_down: float32 [2, 8, 768, 1536], P('section', 'shard', 'rep')
Inputs may be any that keep to these rules, and one draw needn't show every extreme that they name: `routes`: each token names 4 different experts; within the 64 positions of one device's part of a sequence no expert is named by more than 40 tokens, a bound that some expert reaches in some such block.
All inputs are finite; a program needn't handle non-finite values.
Results may differ from a plain program's by a relative error of at most 0.033.
Values may be sent and summed in bfloat16 or wider, within the bound.
No kernel may reach another device: no remote copies, remote signals or barrier semaphores. Data moves between devices by JAX's collectives and lax.ppermute only.
A program may use at most 256 MiB of HBM per device.

v0:
```python
import jax
import jax.numpy as jnp
from jax import lax
from jax.sharding import PartitionSpec as P

QUERY_HEADS = 12
KEY_VALUE_HEADS = 2
HEAD_SIZE = 128
CAP = 40


EPS = 1e-06
ROPE_BASE = 1000000.0


def shifted(array, axis, by):
    peers = lax.axis_size(axis)
    pairs = [(i, i + by) for i in range(peers) if 0 <= i + by < peers]
    return lax.ppermute(array, axis, pairs)


def rope_tables(count_of_rows, offset):
    half_dim = HEAD_SIZE // 2
    frequency = ROPE_BASE ** (-jnp.arange(half_dim, dtype=jnp.float32) * 2.0 / HEAD_SIZE)
    places = (offset + jnp.arange(count_of_rows, dtype=jnp.int32)).astype(jnp.float32)
    angles = places[:, None] * frequency[None, :]
    return (jnp.cos(angles), jnp.sin(angles))


def rotate_halves(vector, cosine_table, sine_table):
    half_dim = vector.shape[-1] // 2
    first_half = vector[..., :half_dim]
    second_half = vector[..., half_dim:]
    cos_b = cosine_table[:, None, :]
    sin_b = sine_table[:, None, :]
    return jnp.concatenate(
        [first_half * cos_b - second_half * sin_b, second_half * cos_b + first_half * sin_b],
        axis=-1,
    )


def unrotate(grad_vec, cosine_table, sine_table):
    half_dim = grad_vec.shape[-1] // 2
    first_half = grad_vec[..., :half_dim]
    second_half = grad_vec[..., half_dim:]
    cos_b = cosine_table[:, None, :]
    sin_b = sine_table[:, None, :]
    return jnp.concatenate(
        [first_half * cos_b + second_half * sin_b, second_half * cos_b - first_half * sin_b],
        axis=-1,
    )


def score_block(grouped_rows, key_matrix, allowed):
    raw_scores = jnp.einsum(
        "nkgd,lkd->kgnl", grouped_rows, key_matrix, preferred_element_type=jnp.float32
    ) * HEAD_SIZE ** (-0.5)
    return jnp.where(allowed, raw_scores, -1e30)


def norm_back(stream, gain, grad_normed):
    rms_val = lax.rsqrt(jnp.mean(stream * stream, axis=-1, keepdims=True) + EPS)
    normed = stream * rms_val
    grad_gain = jnp.sum(grad_normed * normed, axis=0)
    scaled = grad_normed * gain.astype(jnp.float32)
    return (
        grad_gain,
        rms_val * (scaled - normed * jnp.mean(scaled * normed, axis=-1, keepdims=True)),
    )


def layer_forward(stream, fetched, experts_here, route, tables, offset):
    gain_a, w_q, w_kv, w_o, gain_m, w_r = fetched
    w_inner, w_outer = experts_here
    cosine_table, sine_table = tables
    count_of_rows, model_dim = stream.shape
    groups_per_head = QUERY_HEADS // KEY_VALUE_HEADS
    key_value_width = w_kv.shape[1] // 2
    rms_attn = lax.rsqrt(jnp.mean(stream * stream, axis=-1, keepdims=True) + EPS)
    h_attn = (stream * rms_attn * gain_a.astype(jnp.float32)).astype(jnp.bfloat16)
    q_pre = jnp.dot(h_attn, w_q, preferred_element_type=jnp.float32)
    key_value_projected = jnp.dot(h_attn, w_kv, preferred_element_type=jnp.float32)
    query_rows = rotate_halves(
        q_pre.reshape(count_of_rows, QUERY_HEADS, HEAD_SIZE), cosine_table, sine_table
    ).astype(jnp.bfloat16)
    local_key_rows = rotate_halves(
        key_value_projected[:, :key_value_width].reshape(count_of_rows, KEY_VALUE_HEADS, HEAD_SIZE),
        cosine_table,
        sine_table,
    ).reshape(count_of_rows, key_value_width)
    pair_here = jnp.concatenate(
        [local_key_rows, key_value_projected[:, key_value_width:]], axis=1
    ).astype(jnp.bfloat16)
    pairing_everything = lax.all_gather(pair_here, "shard", axis=0, tiled=True)
    sequence_length = pairing_everything.shape[0]
    key_matrix = pairing_everything[:, :key_value_width].reshape(
        sequence_length, KEY_VALUE_HEADS, HEAD_SIZE
    )
    value_matrix = pairing_everything[:, key_value_width:].reshape(
        sequence_length, KEY_VALUE_HEADS, HEAD_SIZE
    )
    grouped_rows = query_rows.reshape(count_of_rows, KEY_VALUE_HEADS, groups_per_head, HEAD_SIZE)
    allowed = jnp.arange(sequence_length)[None, :] <= (offset + jnp.arange(count_of_rows))[:, None]
    scores = score_block(grouped_rows, key_matrix, allowed)
    row_max = jnp.max(scores, axis=-1, keepdims=True)
    exponent = jnp.exp(scores - row_max)
    totals = jnp.sum(exponent, axis=-1, keepdims=True)
    prob_low = (exponent / totals).astype(jnp.bfloat16)
    log_total = row_max + jnp.log(totals)
    mixed_out = jnp.einsum(
        "kgnl,lkd->nkgd", prob_low, value_matrix, preferred_element_type=jnp.float32
    )
    attended = mixed_out.reshape(count_of_rows, QUERY_HEADS * HEAD_SIZE).astype(jnp.bfloat16)
    mid_stream = stream + jnp.dot(attended, w_o, preferred_element_type=jnp.float32)
    rms_moe = lax.rsqrt(jnp.mean(mid_stream * mid_stream, axis=-1, keepdims=True) + EPS)
    h_moe = (mid_stream * rms_moe * gain_m.astype(jnp.float32)).astype(jnp.bfloat16)
    logits = jnp.dot(h_moe, w_r, preferred_element_type=jnp.float32)
    expert_count = w_r.shape[1]
    chosen_int = (
        route[:, :, None] == jnp.arange(expert_count, dtype=jnp.int32)[None, None, :]
    ).astype(jnp.int32)
    chosen = chosen_int.astype(jnp.float32)
    picked = jnp.sum(chosen * logits[:, None, :], axis=-1)
    gate_vals = jax.nn.softmax(picked, axis=-1)
    flat_hot = chosen_int.reshape(-1, expert_count)
    earlier = jnp.cumsum(flat_hot, axis=0) - flat_hot
    slot_of = jnp.sum(flat_hot * earlier, axis=-1).reshape(route.shape)
    target = route * CAP + slot_of
    flat_target = target.reshape(-1)
    top_count = route.shape[1]
    outgoing = (
        jnp.zeros((expert_count * CAP, model_dim), jnp.bfloat16)
        .at[flat_target]
        .set(jnp.repeat(h_moe, top_count, axis=0))
    )
    arrived = lax.all_to_all(
        outgoing.reshape(expert_count, CAP, model_dim),
        "shard",
        split_axis=0,
        concat_axis=0,
        tiled=True,
    )
    local_count = w_inner.shape[0]
    arrived = arrived.reshape(expert_count // local_count, local_count, CAP, model_dim)
    gate_up = jnp.einsum("jecd,edf->jecf", arrived, w_inner, preferred_element_type=jnp.float32)
    hidden_dim = w_outer.shape[1]
    activated = (jax.nn.silu(gate_up[..., :hidden_dim]) * gate_up[..., hidden_dim:]).astype(
        jnp.bfloat16
    )
    produced = jnp.einsum(
        "jecf,efd->jecd", activated, w_outer, preferred_element_type=jnp.float32
    ).astype(jnp.bfloat16)
    back_rows = lax.all_to_all(
        produced.reshape(expert_count, CAP, model_dim),
        "shard",
        split_axis=0,
        concat_axis=0,
        tiled=True,
    )
    returned = back_rows.reshape(expert_count * CAP, model_dim)[target].astype(jnp.float32)
    result = mid_stream + jnp.sum(gate_vals[:, :, None] * returned, axis=1)
    kept_vals = (
        stream,
        h_attn,
        query_rows,
        pairing_everything,
        log_total,
        attended,
        mid_stream,
        h_moe,
        gate_vals,
        chosen,
        target,
        returned,
        arrived,
        gate_up,
        activated,
    )
    return (result, kept_vals)


def layer_backward(upstream, kept_vals, fetched, experts_here, tables, offset):
    (
        stream,
        h_attn,
        query_rows,
        pairing_everything,
        log_total,
        attended,
        mid_stream,
        h_moe,
        gate_vals,
        chosen,
        target,
        returned,
        arrived,
        gate_up,
        activated,
    ) = kept_vals
    gain_a, w_q, w_kv, w_o, gain_m, w_r = fetched
    w_inner, w_outer = experts_here
    cosine_table, sine_table = tables
    count_of_rows, model_dim = upstream.shape
    expert_count = w_r.shape[1]
    hidden_dim = w_outer.shape[1]
    grad_gates = jnp.sum(upstream[:, None, :] * returned, axis=-1)
    to_experts = (gate_vals[:, :, None] * upstream[:, None, :]).astype(jnp.bfloat16)
    grad_send = (
        jnp.zeros((expert_count * CAP, model_dim), jnp.bfloat16)
        .at[target.reshape(-1)]
        .set(to_experts.reshape(-1, model_dim))
    )
    grad_arrived = lax.all_to_all(
        grad_send.reshape(expert_count, CAP, model_dim),
        "shard",
        split_axis=0,
        concat_axis=0,
        tiled=True,
    )
    grad_arrived = grad_arrived.reshape(arrived.shape)
    grad_act = jnp.einsum(
        "jecd,efd->jecf", grad_arrived, w_outer, preferred_element_type=jnp.float32
    )
    grad_outer = jnp.einsum(
        "jecf,jecd->efd", activated, grad_arrived, preferred_element_type=jnp.float32
    )
    gate_part = gate_up[..., :hidden_dim]
    up_part = gate_up[..., hidden_dim:]
    sigmoid_g = jax.nn.sigmoid(gate_part)
    grad_gate = grad_act * up_part * sigmoid_g * (1.0 + gate_part * (1.0 - sigmoid_g))
    grad_up = grad_act * gate_part * sigmoid_g
    grad_both = jnp.concatenate([grad_gate, grad_up], axis=-1).astype(jnp.bfloat16)
    grad_inner = jnp.einsum(
        "jecd,jecf->edf", arrived, grad_both, preferred_element_type=jnp.float32
    )
    grad_rows = jnp.einsum(
        "jecf,edf->jecd", grad_both, w_inner, preferred_element_type=jnp.float32
    ).astype(jnp.bfloat16)
    grad_home = lax.all_to_all(
        grad_rows.reshape(expert_count, CAP, model_dim),
        "shard",
        split_axis=0,
        concat_axis=0,
        tiled=True,
    )
    grad_hmoe = jnp.sum(
        grad_home.reshape(expert_count * CAP, model_dim)[target].astype(jnp.float32), axis=1
    )
    inner_gate = jnp.sum(gate_vals * grad_gates, axis=-1, keepdims=True)
    grad_picked = gate_vals * (grad_gates - inner_gate)
    grad_logits = jnp.sum(chosen * grad_picked[:, :, None], axis=1).astype(jnp.bfloat16)
    grad_hmoe = grad_hmoe + jnp.dot(grad_logits, w_r.T, preferred_element_type=jnp.float32)
    grad_router = jnp.dot(h_moe.T, grad_logits, preferred_element_type=jnp.float32)
    grad_gain_m, grad_norm_m = norm_back(mid_stream, gain_m, grad_hmoe)
    grad_mid = upstream + grad_norm_m
    grad_attn = grad_mid.astype(jnp.bfloat16)
    grad_w_out = jnp.dot(attended.T, grad_attn, preferred_element_type=jnp.float32)
    gradient_mixed_rows = jnp.dot(grad_attn, w_o.T, preferred_element_type=jnp.float32).astype(
        jnp.bfloat16
    )
    groups_per_head = QUERY_HEADS // KEY_VALUE_HEADS
    key_value_width = w_kv.shape[1] // 2
    sequence_length = pairing_everything.shape[0]
    key_matrix = pairing_everything[:, :key_value_width].reshape(
        sequence_length, KEY_VALUE_HEADS, HEAD_SIZE
    )
    value_matrix = pairing_everything[:, key_value_width:].reshape(
        sequence_length, KEY_VALUE_HEADS, HEAD_SIZE
    )
    grouped_rows = query_rows.reshape(count_of_rows, KEY_VALUE_HEADS, groups_per_head, HEAD_SIZE)
    gradient_grouped_rows = gradient_mixed_rows.reshape(
        count_of_rows, KEY_VALUE_HEADS, groups_per_head, HEAD_SIZE
    )
    allowed = jnp.arange(sequence_length)[None, :] <= (offset + jnp.arange(count_of_rows))[:, None]
    scores = score_block(grouped_rows, key_matrix, allowed)
    prob_full = jnp.exp(scores - log_total)
    grad_probs = jnp.einsum(
        "nkgd,lkd->kgnl", gradient_grouped_rows, value_matrix, preferred_element_type=jnp.float32
    )
    inner_prob = jnp.sum(prob_full * grad_probs, axis=-1, keepdims=True)
    grad_scores = (prob_full * (grad_probs - inner_prob) * HEAD_SIZE ** (-0.5)).astype(jnp.bfloat16)
    grad_query = jnp.einsum(
        "kgnl,lkd->nkgd", grad_scores, key_matrix, preferred_element_type=jnp.float32
    ).reshape(count_of_rows, QUERY_HEADS, HEAD_SIZE)
    grad_key = jnp.einsum(
        "kgnl,nkgd->lkd", grad_scores, grouped_rows, preferred_element_type=jnp.float32
    ).reshape(sequence_length, key_value_width)
    grad_value = jnp.einsum(
        "kgnl,nkgd->lkd",
        prob_full.astype(jnp.bfloat16),
        gradient_grouped_rows,
        preferred_element_type=jnp.float32,
    ).reshape(sequence_length, key_value_width)
    gradient_pairing = lax.psum_scatter(
        jnp.concatenate([grad_key, grad_value], axis=1).astype(jnp.bfloat16),
        "shard",
        scatter_dimension=0,
        tiled=True,
    ).astype(jnp.float32)
    grad_kpre = unrotate(
        gradient_pairing[:, :key_value_width].reshape(count_of_rows, KEY_VALUE_HEADS, HEAD_SIZE),
        cosine_table,
        sine_table,
    ).reshape(count_of_rows, key_value_width)
    grad_kv = jnp.concatenate([grad_kpre, gradient_pairing[:, key_value_width:]], axis=1).astype(
        jnp.bfloat16
    )
    grad_qpre = (
        unrotate(grad_query, cosine_table, sine_table)
        .reshape(count_of_rows, QUERY_HEADS * HEAD_SIZE)
        .astype(jnp.bfloat16)
    )
    grad_hattn = jnp.dot(grad_qpre, w_q.T, preferred_element_type=jnp.float32) + jnp.dot(
        grad_kv, w_kv.T, preferred_element_type=jnp.float32
    )
    grad_w_q = jnp.dot(h_attn.T, grad_qpre, preferred_element_type=jnp.float32)
    grad_w_kv = jnp.dot(h_attn.T, grad_kv, preferred_element_type=jnp.float32)
    grad_gain_a, grad_norm_a = norm_back(stream, gain_a, grad_hattn)
    grad_stream = grad_mid + grad_norm_a
    return (
        grad_stream,
        (grad_gain_a, grad_w_q, grad_w_kv, grad_w_out, grad_gain_m, grad_router),
        (grad_inner, grad_outer),
    )


def body(
    tokens_in,
    cotangent,
    routes,
    gain_attn,
    w_query,
    w_keyval,
    w_out,
    gain_moe,
    w_router,
    w_in,
    w_down,
):
    micro_count = tokens_in.shape[0]
    count_of_rows = tokens_in.shape[2]
    model_dim = tokens_in.shape[3]
    is_first = lax.axis_index("section") == 0
    offset = lax.axis_index("shard") * count_of_rows
    tables = rope_tables(count_of_rows, offset)
    experts_here = (w_in[0], w_down[0])

    def fetch_weights():
        return (
            lax.all_gather(gain_attn[0], "shard", axis=0, tiled=True),
            lax.all_gather(w_query[0], "shard", axis=0, tiled=True),
            lax.all_gather(w_keyval[0], "shard", axis=0, tiled=True),
            lax.all_gather(w_out[0], "shard", axis=0, tiled=True),
            lax.all_gather(gain_moe[0], "shard", axis=0, tiled=True),
            lax.all_gather(w_router[0], "shard", axis=0, tiled=True),
        )

    sent_rows = jnp.zeros((count_of_rows, model_dim), jnp.bfloat16)
    forward_out = []
    kept_list = []
    for step_idx in range(micro_count + 1):
        own_rows = tokens_in[min(step_idx, micro_count - 1), 0].astype(jnp.float32)
        stream = jnp.where(is_first, own_rows, sent_rows.astype(jnp.float32))
        route_now = jnp.where(
            is_first,
            routes[0, min(step_idx, micro_count - 1), 0],
            routes[0, max(step_idx - 1, 0), 0],
        )
        result, kept_vals = layer_forward(
            stream, fetch_weights(), experts_here, route_now, tables, offset
        )
        produced = result.astype(jnp.bfloat16)
        forward_out.append(produced)
        kept_list.append(kept_vals)
        if step_idx < micro_count:
            sent_rows = shifted(produced, "section", 1)
    grad_from_next = jnp.zeros((count_of_rows, model_dim), jnp.float32)
    stream_grads = []
    attn_sums = None
    expert_sums = None
    for step_idx in range(micro_count + 1):
        flag_first = 1.0 if step_idx >= 1 else 0.0
        flag_second = 1.0 if step_idx < micro_count else 0.0
        is_valid = jnp.where(is_first, flag_first, flag_second)
        given_grad = cotangent[max(micro_count - 1 - step_idx, 0), 0].astype(jnp.float32)
        upstream = jnp.where(is_first, grad_from_next, given_grad) * is_valid
        grad_stream, grads_attn, grads_expert = layer_backward(
            upstream,
            kept_list[micro_count - step_idx],
            fetch_weights(),
            experts_here,
            tables,
            offset,
        )
        stream_grads.append(grad_stream)
        if step_idx < micro_count:
            grad_from_next = shifted(grad_stream.astype(jnp.bfloat16), "section", -1).astype(
                grad_stream.dtype
            )
        part_ga, part_wq, part_wkv, part_wo, part_gm, part_router = grads_attn
        grads_attn = (
            lax.psum_scatter(
                part_ga.astype(jnp.bfloat16), "shard", scatter_dimension=0, tiled=True
            ).astype(jnp.float32),
            lax.psum_scatter(
                part_wq.astype(jnp.bfloat16), "shard", scatter_dimension=0, tiled=True
            ).astype(jnp.float32),
            lax.psum_scatter(
                part_wkv.astype(jnp.bfloat16), "shard", scatter_dimension=0, tiled=True
            ).astype(jnp.float32),
            lax.psum_scatter(
                part_wo.astype(jnp.bfloat16), "shard", scatter_dimension=0, tiled=True
            ).astype(jnp.float32),
            lax.psum_scatter(
                part_gm.astype(jnp.bfloat16), "shard", scatter_dimension=0, tiled=True
            ).astype(jnp.float32),
            lax.psum_scatter(
                part_router.astype(jnp.bfloat16), "shard", scatter_dimension=0, tiled=True
            ).astype(jnp.float32),
        )
        if attn_sums is None:
            attn_sums = tuple(grads_attn)
            expert_sums = tuple(grads_expert)
        else:
            attn_sums = tuple(jax.tree.map(jnp.add, attn_sums, tuple(grads_attn)))
            expert_sums = tuple(jax.tree.map(jnp.add, expert_sums, tuple(grads_expert)))
    total_ga, total_wq, total_wkv, total_wo, total_gm, total_router = attn_sums
    total_inner, total_outer = expert_sums
    out_wq, out_wkv, out_wo, out_inner, out_outer = (
        lax.psum_scatter(
            total_wq.astype(jnp.bfloat16), "rep", scatter_dimension=1, tiled=True
        ).astype(jnp.float32),
        lax.psum_scatter(
            total_wkv.astype(jnp.bfloat16), "rep", scatter_dimension=1, tiled=True
        ).astype(jnp.float32),
        lax.psum_scatter(
            total_wo.astype(jnp.bfloat16), "rep", scatter_dimension=1, tiled=True
        ).astype(jnp.float32),
        lax.psum_scatter(
            total_inner.astype(jnp.bfloat16), "rep", scatter_dimension=1, tiled=True
        ).astype(jnp.float32),
        lax.psum_scatter(
            total_outer.astype(jnp.bfloat16), "rep", scatter_dimension=1, tiled=True
        ).astype(jnp.float32),
    )
    out_ga, out_gm, out_router = lax.psum((total_ga, total_gm, total_router), "rep")
    act_rows = [
        jnp.where(is_first, forward_out[micro_idx], forward_out[micro_idx + 1])
        for micro_idx in range(micro_count)
    ]
    grad_rows_out = [
        jnp.where(
            is_first,
            stream_grads[micro_count - micro_idx],
            stream_grads[micro_count - micro_idx - 1],
        )
        for micro_idx in range(micro_count)
    ]
    acts = jnp.stack(act_rows)[None, :, None]
    input_grads = jnp.stack(grad_rows_out)[None, :, None]
    return (
        acts,
        input_grads,
        out_ga[None],
        out_wq[None],
        out_wkv[None],
        out_wo[None],
        out_gm[None],
        out_router[None],
        out_inner[None],
        out_outer[None],
    )


def solution(mesh):
    in_specs = (
        P(None, "rep", "shard", None),
        P(None, "rep", "shard", None),
        P("section", None, "rep", "shard", None),
        P("section", "shard"),
        P("section", "shard", None),
        P("section", "shard", None),
        P("section", "shard", None),
        P("section", "shard"),
        P("section", "shard", None),
        P("section", "shard", None, None),
        P("section", "shard", None, None),
    )
    out_specs = (
        P("section", None, "rep", "shard", None),
        P("section", None, "rep", "shard", None),
        P("section", "shard"),
        P("section", "shard", "rep"),
        P("section", "shard", "rep"),
        P("section", "shard", "rep"),
        P("section", "shard"),
        P("section", "shard", None),
        P("section", "shard", "rep", None),
        P("section", "shard", "rep", None),
    )
    return jax.shard_map(body, mesh=mesh, in_specs=in_specs, out_specs=out_specs, check_vma=False)
```

profile of v0, /device:TPU:0, one launch (start us, length us, event | category | flops | bytes accessed | tf_op | source)
XLA Modules:
  0.0 1499.1 jit_solution(15098020484069795289)
XLA Ops:
  12.6 15.6 %all-reduce.10 = (bf16[1536]{0:T(1024)(128)(2,1)S(1)}, bf16[1536]{0:T(1024)(128)(2,1)S(1)}) all-reduce(bf16[1536]{0:T(1024)(128)(2,1)S(1)} %dynamic-update-slice, bf16[1536]{0:T(1024)(128)(2,1)S(1)} %dynamic-update-slice.1), channel_id=2, replica_groups=mesh['section'=2,'rep'=8,'shard'=8] {'shard'}, use_global_device_ids=true, to_apply=%add | all-reduce | flops 3072 | bytes 12288
  39.0 13.1 all_gather.20
  56.4 16.3 %all-gather.12.cloned.1.call-done = bf16[1,1536,1536]{2,1,0:T(8,128)(2,1)} async-done(((bf16[1,192,1536]{2,1,0:T(8,128)(2,1)}), bf16[1,1536,1536]{2,1,0:T(8,128)(2,1)}) %all-gather.12.cloned.1.call-update) | async-done | bytes 4718608 | tf_op jit(solution)/shard_map/all_gather | solution.py:351
  85.8 23.0 %all-gather.14.cloned.1.call-done = bf16[1,1536,1536]{2,1,0:T(8,128)(2,1)} async-done(((bf16[1,192,1536]{2,1,0:T(8,128)(2,1)}), bf16[1,1536,1536]{2,1,0:T(8,128)(2,1)}) %all-gather.14.cloned.1.call-update) | async-done | bytes 4718608 | tf_op jit(solution)/shard_map/all_gather | solution.py:353
  124.2 12.4 all-to-all-done
  153.1 20.4 %all-gather.5 = bf16[1,1536,8]{2,0,1:T(2,128)(2,1)} all-gather(bf16[1,192,8]{2,0,1:T(2,128)(2,1)} %copy.253), channel_id=7, replica_groups=mesh['section'=2,'rep'=8,'shard'=8] {'shard'}, dimensions={1}, use_global_device_ids=true | all-gather | bytes 27648 | tf_op jit(solution)/shard_map/all_gather | solution.py:355
  205.2 13.5 all_gather.25
  240.2 14.6 all-to-all-done.2
  311.0 13.1 all_gather.26
  396.1 12.3 all-to-all-done.7
  470.4 23.6 %reduce-scatter.61.cloned.1.call-done = bf16[64,512]{1,0:T(8,128)(2,1)} async-done(((bf16[512,512]{1,0:T(8,128)(2,1)}), bf16[64,512]{1,0:T(8,128)(2,1)}) %reduce-scatter.61.cloned.1.call-update) | async-done | bytes 65552
  526.9 18.4 %all_to_all.60 = bf16[8,40,1536]{2,1,0:T(8,128)(2,1)S(1)} all-to-all(bf16[8,40,1536]{2,1,0:T(8,128)(2,1)S(1)} %bitcast.682), channel_id=1, replica_groups=mesh['section'=2,'rep'=8,'shard'=8] {'shard'}, dimensions={0} | all-to-all | bytes 1966080 | tf_op jit(solution)/shard_map/all_to_all | solution.py:213
  609.9 21.0 %reduce-scatter.63.cloned.1.call-done = bf16[64,512]{1,0:T(8,128)(2,1)} async-done(((bf16[512,512]{1,0:T(8,128)(2,1)}), bf16[64,512]{1,0:T(8,128)(2,1)}) %reduce-scatter.63.cloned.1.call-update) | async-done | bytes 65552
  663.7 19.2 %all_to_all.61 = bf16[8,40,1536]{2,1,0:T(8,128)(2,1)S(1)} all-to-all(bf16[8,40,1536]{2,1,0:T(8,128)(2,1)} %bitcast.681), channel_id=1, replica_groups=mesh['section'=2,'rep'=8,'shard'=8] {'shard'}, dimensions={0} | all-to-all | bytes 1966080 | tf_op jit(solution)/shard_map/all_to_all | solution.py:213
  697.1 11.9 all-to-all-done.11
  739.6 25.2 %reduce-scatter.65.cloned.1.call-done = bf16[64,512]{1,0:T(8,128)(2,1)} async-done(((bf16[512,512]{1,0:T(8,128)(2,1)}), bf16[64,512]{1,0:T(8,128)(2,1)}) %reduce-scatter.65.cloned.1.call-update) | async-done | bytes 65552
  833.0 34.1 %reduce-scatter.49.cloned.1.call-done = bf16[192,512]{1,0:T(8,128)(2,1)} async-done(((bf16[1536,512]{1,0:T(8,128)(2,1)}), bf16[192,512]{1,0:T(8,128)(2,1)}) %reduce-scatter.49.cloned.1.call-update) | async-done | bytes 196624 | tf_op jit(solution)/shard_map/reduce_scatter | solution.py:408
  883.5 16.2 %reduce-scatter.73.cloned.1.call-done = bf16[192,8]{1,0:T(8,128)(2,1)} async-done(((bf16[1536,8]{1,0:T(8,128)(2,1)}), bf16[192,8]{1,0:T(8,128)(2,1)}) %reduce-scatter.73.cloned.1.call-update) | async-done | bytes 3088
  900.5 31.6 %reduce-scatter.75.cloned.1.call-done = bf16[192,8]{1,0:T(8,128)(2,1)} async-done(((bf16[1536,8]{1,0:T(8,128)(2,1)}), bf16[192,8]{1,0:T(8,128)(2,1)}) %reduce-scatter.75.cloned.1.call-update) | async-done | bytes 3088
  933.0 31.7 %reduce-scatter.77.cloned.1.call-done = bf16[192,8]{1,0:T(8,128)(2,1)} async-done(((bf16[1536,8]{1,0:T(8,128)(2,1)}), bf16[192,8]{1,0:T(8,128)(2,1)}) %reduce-scatter.77.cloned.1.call-update) | async-done | bytes 3088
  971.2 23.8 %all-reduce.9 = (bf16[1536]{0:T(1024)(128)(2,1)S(1)}, bf16[1536]{0:T(1024)(128)(2,1)S(1)}, bf16[1536]{0:T(1024)(128)(2,1)S(1)}, bf16[1536]{0:T(1024)(128)(2,1)S(...) all-reduce(bf16[1536]{0:T(1024)(128)(2,1)S(1)} %get-tuple-element.8, ...), channel_id=13, replica_groups=mesh['section'=2,'rep'=8,'shard'=8] {'shard'}, use_global_device_ids=true, to_apply=%region_68.69.clone | all-reduce | flops 9216 | bytes 36864
  995.1 34.7 %all-reduce.8 = (f32[1,192]{1,0:T(1,128)}, f32[1,192]{1,0:T(1,128)}, f32[1,192,8]{1,2,0:T(8,128)}) all-reduce(f32[1,192]{1,0:T(1,128)S(1)} %bitcast.742, f32[1,192]{1,0:T(1,128)S(1)} %bitcast.743, f32[1,192,8]{1,2,0:T(8,128)S(1)} %add_bitcast_fusion), channel_id=1, replica_groups=mesh['section'=2,'rep'=8,'shard'=8] {'rep'}, use_global_device_ids=true, to_apply=%region_69.70 | all-reduce | flops 1920 | bytes 15360 | tf_op jit(solution)/shard_map/psum | solution.py:446
  1029.9 15.5 %reduce-scatter.53.cloned.1.call-done = bf16[192,1536]{1,0:T(8,128)(2,1)} async-done(((bf16[1536,1536]{1,0:T(8,128)(2,1)}), bf16[192,1536]{1,0:T(8,128)(2,1)}) %reduce-scatter.53.cloned.1.call-update) | async-done | bytes 589840 | tf_op jit(solution)/shard_map/reduce_scatter | solution.py:411
  1045.3 40.5 %reduce-scatter.55.cloned.1.call-done = bf16[192,1536]{1,0:T(8,128)(2,1)} async-done(((bf16[1536,1536]{1,0:T(8,128)(2,1)}), bf16[192,1536]{1,0:T(8,128)(2,1)}) %reduce-scatter.55.cloned.1.call-update) | async-done | bytes 589840 | tf_op jit(solution)/shard_map/reduce_scatter | solution.py:411
  1089.9 36.3 %reduce-scatter.39.cloned.1.call-done = bf16[192,1536]{1,0:T(8,128)(2,1)} async-done(((bf16[1536,1536]{1,0:T(8,128)(2,1)}), bf16[192,1536]{1,0:T(8,128)(2,1)}) %reduce-scatter.39.cloned.1.call-update) | async-done | bytes 589840 | tf_op jit(solution)/shard_map/reduce_scatter | solution.py:405
  1126.2 40.4 %reduce-scatter.41.cloned.1.call-done = bf16[192,1536]{1,0:T(8,128)(2,1)} async-done(((bf16[1536,1536]{1,0:T(8,128)(2,1)}), bf16[192,1536]{1,0:T(8,128)(2,1)}) %reduce-scatter.41.cloned.1.call-update) | async-done | bytes 589840 | tf_op jit(solution)/shard_map/reduce_scatter | solution.py:405
  1166.7 40.4 %reduce-scatter.43.cloned.1.call-done = bf16[192,1536]{1,0:T(8,128)(2,1)} async-done(((bf16[1536,1536]{1,0:T(8,128)(2,1)}), bf16[192,1536]{1,0:T(8,128)(2,1)}) %reduce-scatter.43.cloned.1.call-update) | async-done | bytes 589840 | tf_op jit(solution)/shard_map/reduce_scatter | solution.py:405
  1210.0 56.2 %reduce-scatter.59.cloned.1.call-done = bf16[1,96,1536]{2,1,0:T(8,128)(2,1)} async-done(((bf16[1,768,1536]{2,1,0:T(8,128)(2,1)}), bf16[1,96,1536]{2,1,0:T(8,128)(2,1)}) %reduce-scatter.59.cloned.1.call-update) | async-done | bytes 294928 | tf_op jit(solution)/shard_map/reduce_scatter | solution.py:442
  1268.0 37.3 %reduce-scatter.69.cloned.1.call-done = bf16[64,192]{1,0:T(8,128)(2,1)} async-done(((bf16[512,192]{1,0:T(8,128)(2,1)}), bf16[64,192]{1,0:T(8,128)(2,1)}) %reduce-scatter.69.cloned.1.call-update) | async-done | bytes 24592
  1307.0 100.3 %reduce-scatter.57.cloned.1.call-done = bf16[1,192,1536]{2,1,0:T(8,128)(2,1)} async-done(((bf16[1,1536,1536]{2,1,0:T(8,128)(2,1)}), bf16[1,192,1536]{2,1,0:T(8,128)(2,1)}) %reduce-scatter.57.cloned.1.call-update) | async-done | bytes 589840 | tf_op jit(solution)/shard_map/reduce_scatter | solution.py:439
  1409.6 40.3 %reduce-scatter.71.cloned.1.call-done = bf16[192,192]{1,0:T(8,128)(2,1)} async-done(((bf16[1536,192]{1,0:T(8,128)(2,1)}), bf16[192,192]{1,0:T(8,128)(2,1)}) %reduce-scatter.71.cloned.1.call-update) | async-done | bytes 73744
  1451.5 39.2 %reduce-scatter.67.cloned.1.call-done = bf16[192,192]{1,0:T(8,128)(2,1)} async-done(((bf16[1536,192]{1,0:T(8,128)(2,1)}), bf16[192,192]{1,0:T(8,128)(2,1)}) %reduce-scatter.67.cloned.1.call-update) | async-done | bytes 73744
  (827 shorter events, 588.4 us)
Async XLA Ops:
  7.2 29.5 %all-gather.10.cloned.1.call-start = ((), (), s32[]{:S(2)}) async-start(), calls=%async_computation.43 | async-start | bytes 1769472 | tf_op jit(solution)/shard_map/all_gather | solution.py:352
  8.0 64.8 %all-gather.12.cloned.1.call-start = ((), (), s32[]{:S(2)}) async-start(), calls=%async_computation.44 | async-start | bytes 5308416 | tf_op jit(solution)/shard_map/all_gather | solution.py:351
  8.7 100.0 %all-gather.14.cloned.1.call-start = ((), (), s32[]{:S(2)}) async-start(), calls=%async_computation.45 | async-start | bytes 5308416 | tf_op jit(solution)/shard_map/all_gather | solution.py:353
  117.7 18.9 %all-to-all-start = ((bf16[8,40,1536]{2,1,0:T(8,128)(2,1)}), bf16[8,40,1536]{2,1,0:T(8,128)(2,1)S(1)}, u32[]{:S(2)}, u32[]{:S(2)}) async-start(bf16[8,40,1536]{2,1,0:T(8,128)(2,1)} %bitcast.21), calls=%async_computation | async-start | bytes 1966080 | tf_op jit(solution)/shard_map/all_to_all | solution.py:136
  145.3 32.2 %all-to-all-start.1 = ((bf16[8,40,1536]{2,1,0:T(8,128)(2,1)}), bf16[8,40,1536]{2,1,0:T(8,128)(2,1)S(1)}, u32[]{:S(2)}, u32[]{:S(2)}) async-start(bf16[8,40,1536]{2,1,0:T(8,128)(2,1)} %convolution_convert_fusion.11), calls=%async_computation.1 | async-start | bytes 1966080 | tf_op jit(solution)/shard_map/all_to_all | solution.py:153
  236.0 18.7 %all-to-all-start.2 = ((bf16[8,40,1536]{2,1,0:T(8,128)(2,1)}), bf16[8,40,1536]{2,1,0:T(8,128)(2,1)S(1)}, u32[]{:S(2)}, u32[]{:S(2)}) async-start(bf16[8,40,1536]{2,1,0:T(8,128)(2,1)} %bitcast.46), calls=%async_computation.2 | async-start | bytes 1966080 | tf_op jit(solution)/shard_map/all_to_all | solution.py:136
  263.5 18.9 %all-to-all-start.3 = ((bf16[8,40,1536]{2,1,0:T(8,128)(2,1)}), bf16[8,40,1536]{2,1,0:T(8,128)(2,1)S(1)}, u32[]{:S(2)}, u32[]{:S(2)}) async-start(bf16[8,40,1536]{2,1,0:T(8,128)(2,1)} %convolution_convert_fusion.10), calls=%async_computation.3 | async-start | bytes 1966080 | tf_op jit(solution)/shard_map/all_to_all | solution.py:153
  341.3 19.5 %all-to-all-start.4 = ((bf16[8,40,1536]{2,1,0:T(8,128)(2,1)}), bf16[8,40,1536]{2,1,0:T(8,128)(2,1)}, u32[]{:S(2)}, u32[]{:S(2)}) async-start(bf16[8,40,1536]{2,1,0:T(8,128)(2,1)} %bitcast.69), calls=%async_computation.4 | async-start | bytes 1966080 | tf_op jit(solution)/shard_map/all_to_all | solution.py:136
  360.8 19.0 %all-to-all-start.6 = ((bf16[8,40,1536]{2,1,0:T(8,128)(2,1)}), bf16[8,40,1536]{2,1,0:T(8,128)(2,1)S(1)}, u32[]{:S(2)}, u32[]{:S(2)}) async-start(bf16[8,40,1536]{2,1,0:T(8,128)(2,1)} %bitcast.82), calls=%async_computation.6 | async-start | bytes 1966080 | tf_op jit(solution)/shard_map/all_to_all | solution.py:213
  408.4 19.5 %all-to-all-start.5 = ((bf16[8,40,1536]{2,1,0:T(8,128)(2,1)}), bf16[8,40,1536]{2,1,0:T(8,128)(2,1)}, u32[]{:S(2)}, u32[]{:S(2)}) async-start(bf16[8,40,1536]{2,1,0:T(8,128)(2,1)} %convolution_convert_fusion.9), calls=%async_computation.5 | async-start | bytes 1966080 | tf_op jit(solution)/shard_map/all_to_all | solution.py:153
  412.6 81.3 %reduce-scatter.61.cloned.1.call-start = ((), (), s32[]{:S(2)}) async-start(), calls=%async_computation.46 | async-start | bytes 589824
  552.5 18.9 %all-to-all-start.9 = ((bf16[8,40,1536]{2,1,0:T(8,128)(2,1)}), bf16[8,40,1536]{2,1,0:T(8,128)(2,1)S(1)}, u32[]{:S(2)}, u32[]{:S(2)}) async-start(bf16[8,40,1536]{2,1,0:T(8,128)(2,1)} %fusion.53), calls=%async_computation.9 | async-start | bytes 1966080 | tf_op jit(solution)/shard_map/all_to_all | solution.py:239
  556.2 74.6 %reduce-scatter.63.cloned.1.call-start = ((), (), s32[]{:S(2)}) async-start(), calls=%async_computation.47 | async-start | bytes 589824
  690.1 18.9 %all-to-all-start.11 = ((bf16[8,40,1536]{2,1,0:T(8,128)(2,1)}), bf16[8,40,1536]{2,1,0:T(8,128)(2,1)S(1)}, u32[]{:S(2)}, u32[]{:S(2)}) async-start(bf16[8,40,1536]{2,1,0:T(8,128)(2,1)} %fusion.56), calls=%async_computation.11 | async-start | bytes 1966080 | tf_op jit(solution)/shard_map/all_to_all | solution.py:239
  693.8 70.9 %reduce-scatter.65.cloned.1.call-start = ((), (), s32[]{:S(2)}) async-start(), calls=%async_computation.48 | async-start | bytes 589824
  735.8 94.0 %reduce-scatter.45.cloned.1.call-start = ((), (), s32[]{:S(2)}) async-start(), calls=%async_computation.35 | async-start | bytes 1769472 | tf_op jit(solution)/shard_map/reduce_scatter | solution.py:408
  737.7 95.3 %reduce-scatter.47.cloned.1.call-start = ((), (), s32[]{:S(2)}) async-start(), calls=%async_computation.36 | async-start | bytes 1769472 | tf_op jit(solution)/shard_map/reduce_scatter | solution.py:408
  739.5 127.5 %reduce-scatter.49.cloned.1.call-start = ((), (), s32[]{:S(2)}) async-start(), calls=%async_computation.37 | async-start | bytes 1769472 | tf_op jit(solution)/shard_map/reduce_scatter | solution.py:408
  768.3 131.4 %reduce-scatter.73.cloned.1.call-start = ((), (), s32[]{:S(2)}) async-start(), calls=%async_computation.52 | async-start | bytes 442368
  770.4 161.7 %reduce-scatter.75.cloned.1.call-start = ((), (), s32[]{:S(2)}) async-start(), calls=%async_computation.53 | async-start | bytes 442368
  772.5 192.2 %reduce-scatter.77.cloned.1.call-start = ((), (), s32[]{:S(2)}) async-start(), calls=%async_computation.54 | async-start | bytes 442368
  774.6 255.3 %reduce-scatter.51.cloned.1.call-start = ((), (), s32[]{:S(2)}) async-start(), calls=%async_computation.38 | async-start | bytes 5308416 | tf_op jit(solution)/shard_map/reduce_scatter | solution.py:411
  779.5 265.8 %reduce-scatter.53.cloned.1.call-start = ((), (), s32[]{:S(2)}) async-start(), calls=%async_computation.39 | async-start | bytes 5308416 | tf_op jit(solution)/shard_map/reduce_scatter | solution.py:411
  784.1 301.7 %reduce-scatter.55.cloned.1.call-start = ((), (), s32[]{:S(2)}) async-start(), calls=%async_computation.40 | async-start | bytes 5308416 | tf_op jit(solution)/shard_map/reduce_scatter | solution.py:411
  788.7 337.5 %reduce-scatter.39.cloned.1.call-start = ((), (), s32[]{:S(2)}) async-start(), calls=%async_computation.32 | async-start | bytes 5308416 | tf_op jit(solution)/shard_map/reduce_scatter | solution.py:405
  793.4 373.2 %reduce-scatter.41.cloned.1.call-start = ((), (), s32[]{:S(2)}) async-start(), calls=%async_computation.33 | async-start | bytes 5308416 | tf_op jit(solution)/shard_map/reduce_scatter | solution.py:405
  798.1 409.0 %reduce-scatter.43.cloned.1.call-start = ((), (), s32[]{:S(2)}) async-start(), calls=%async_computation.34 | async-start | bytes 5308416 | tf_op jit(solution)/shard_map/reduce_scatter | solution.py:405
  808.7 457.4 %reduce-scatter.59.cloned.1.call-start = ((), (), s32[]{:S(2)}) async-start(), calls=%async_computation.42 | async-start | bytes 2654208 | tf_op jit(solution)/shard_map/reduce_scatter | solution.py:442
  816.8 488.5 %reduce-scatter.69.cloned.1.call-start = ((), (), s32[]{:S(2)}) async-start(), calls=%async_computation.50 | async-start | bytes 294912
  869.1 538.2 %reduce-scatter.57.cloned.1.call-start = ((), (), s32[]{:S(2)}) async-start(), calls=%async_computation.41 | async-start | bytes 5308416 | tf_op jit(solution)/shard_map/reduce_scatter | solution.py:439
  879.7 570.2 %reduce-scatter.71.cloned.1.call-start = ((), (), s32[]{:S(2)}) async-start(), calls=%async_computation.51 | async-start | bytes 884736
  1088.7 402.0 %reduce-scatter.67.cloned.1.call-start = ((), (), s32[]{:S(2)}) async-start(), calls=%async_computation.49 | async-start | bytes 884736
  (205 other events, 3398.8 us)
Sparse Core Ops, SparseCore 0:
  9.8 26.9 all-gather.9
  38.4 34.2 all-gather.11
  74.4 34.2 all-gather.13
  462.5 31.3 reduce-scatter.60
  602.2 28.6 reduce-scatter.62
  735.9 28.8 reduce-scatter.64
  767.3 31.4 reduce-scatter.44
  801.4 31.5 reduce-scatter.46
  835.5 31.5 reduce-scatter.48
  870.0 29.6 reduce-scatter.72
  902.6 29.4 reduce-scatter.74
  935.1 29.5 reduce-scatter.76
  967.1 37.8 reduce-scatter.50
  1007.2 38.0 reduce-scatter.52
  1047.6 38.1 reduce-scatter.54
  1088.1 38.1 reduce-scatter.38
  1128.5 38.1 reduce-scatter.40
  1168.9 38.1 reduce-scatter.42
  1209.5 56.6 reduce-scatter.58
  1268.4 36.8 reduce-scatter.68
  1307.8 99.5 reduce-scatter.56
  1409.9 39.9 reduce-scatter.70
  1452.2 38.4 reduce-scatter.66
where the time goes:
time: 1510 us; the launch traced here: 1500 us
  waiting for transfers between devices  802 us (53%)
  matrix products  223 us (15%)
  blocking collectives  172 us (11%)
  local copies, waits for them, and re-layouts  155 us (10%)
  other arithmetic  76.6 us (5%)
  starting transfers between devices  52.9 us (4%)
  between operations  18.6 us (1%)
    unnamed x32, waiting for transfers between devices  268 us
    reduce_scatter x3, waiting for transfers between devices, body(): lax.psum_scatter(part_wq.astype(jnp.bfloat16), 'shard', scatter_dimension...  117 us
    reduce_scatter x1, waiting for transfers between devices, body(): lax.psum_scatter(total_inner.astype(jnp.bfloat16), 'rep', scatter_dimensi...  100 us
    reduce_scatter x1, waiting for transfers between devices, body(): lax.psum_scatter(total_outer.astype(jnp.bfloat16), 'rep', scatter_dimensi...  56.2 us
    reduce_scatter x3, waiting for transfers between devices, body(): lax.psum_scatter(part_wo.astype(jnp.bfloat16), 'shard', scatter_dimension...  56 us
    unnamed x439, local copies, waits for them, and re-layouts  45.3 us
    all_gather x3, blocking collectives, layer_forward(): pairing_everything = lax.all_gather(pair_here, 'shard', axis=0, tiled=True)  39.7 us
    unnamed x2, blocking collectives  39.5 us
  transfers between devices with their start and end apart: 37, of which 34 were waited for; matrix products, arithmetic and copies ran while one was open for 12% of the time, Pallas kernels for 0%

commit v1 on v0

v1 whole, which is shorter than its diff:
```python
import jax
import jax.numpy as jnp
from jax import lax
from jax.experimental import pallas as pl
from jax.experimental.pallas import tpu as pltpu
from jax.sharding import PartitionSpec as P

D = 1536
T = 64
HEADS = 12
KV_HEADS = 2
GROUP = HEADS // KV_HEADS
HS = 128
KW = KV_HEADS * HS
FF = 768
SEQ = 512
N_EXPERTS = 8
LANES = 128
EPS = 1e-06
ROPE_BASE = 1000000.0
SCALE = HS**-0.5
BF = jnp.bfloat16
F32 = jnp.float32

NN = (((1,), (0,)), ((), ()))
NT = (((1,), (1,)), ((), ()))
TN = (((0,), (0,)), ((), ()))


def mm(a, b, dims=NN):
    return lax.dot_general(a, b, dims, preferred_element_type=F32)


def sds(shape, dtype):
    return jax.ShapeDtypeStruct(shape, dtype)


def whole(shape):
    return pl.BlockSpec(shape, lambda *_: (0,) * len(shape))


def call(kernel, name, grid, in_specs, out_specs, out_shape, scratch, flops, nbytes, *args):
    return pl.pallas_call(
        kernel,
        name=name,
        grid=grid,
        in_specs=in_specs,
        out_specs=out_specs,
        out_shape=out_shape,
        scratch_shapes=scratch,
        compiler_params=pltpu.CompilerParams(
            dimension_semantics=("arbitrary",) * len(grid), vmem_limit_bytes=40 * 2**20
        ),
        cost_estimate=pl.CostEstimate(flops=flops, bytes_accessed=nbytes, transcendentals=0),
    )(*args)


def swap(x):
    return lax.ppermute(x, "shard", [(i, i ^ 1) for i in range(8)])


def along_y(x, k):
    return lax.ppermute(x, "shard", [(i, (i + 2 * k) % 8) for i in range(8)])


def gather_blocks(x):
    same = [x, along_y(x, 1), along_y(x, 2), along_y(x, 3)]
    return same + [swap(b) for b in same]


def scatter_sum_blocks(same, other):
    rows = same.shape[0] // 4
    got = swap(other)
    sums = []
    for k in range(4):
        part = slice(k * rows, (k + 1) * rows)
        sums.append((same[part].astype(F32) + got[part].astype(F32)).astype(BF))
    return [sums[0]] + [along_y(sums[k], -k) for k in (1, 2, 3)]


def rope(x, cos, sin):
    return x * cos + pltpu.roll(x, HS // 2, 1) * sin


def rope_back(x, cos, sin):
    return x * cos - pltpu.roll(x, HS // 2, 1) * sin


def qkv_kernel(x_ref, gain_ref, w_ref, cos_ref, sin_ref, q_ref, kv_ref, h_ref):
    j = pl.program_id(0)

    @pl.when(j == 0)
    def _():
        x = x_ref[...].astype(F32)
        r = lax.rsqrt(jnp.mean(x * x, axis=-1, keepdims=True) + EPS)
        h_ref[...] = (x * r * gain_ref[0:1, :]).astype(BF)

    y = mm(h_ref[...], w_ref[...])
    cos, sin = cos_ref[...], sin_ref[...]

    @pl.when(j < 3)
    def _():
        for i in range(4):
            at = slice(i * HS, (i + 1) * HS)
            q_ref[:, at] = rope(y[:, at], cos, sin).astype(BF)

    @pl.when(j == 3)
    def _():
        for i in range(2):
            at = slice(i * HS, (i + 1) * HS)
            kv_ref[:, at] = rope(y[:, at], cos, sin).astype(BF)
        kv_ref[:, KW:] = y[:, KW:].astype(BF)


def qkv(x, gains, w_packed, cos, sin):
    return call(
        qkv_kernel, "qkv", (4,),
        [whole((T, D)), whole((8, D)), pl.BlockSpec((D, 512), lambda j: (0, j)), whole((T, HS)), whole((T, HS))],
        [pl.BlockSpec((T, 512), lambda j: (0, jnp.minimum(j, 2))), whole((T, 512)), whole((T, D))],
        [sds((T, D), BF), sds((T, 512), BF), sds((T, D), BF)],
        [], 2 * T * D * 2048, 7 * 10**6,
        x, gains, w_packed, cos, sin,
    )


def stack_rows(blocks, dst, width):
    for i, b in enumerate(blocks):
        dst[i * T : (i + 1) * T, :] = b[:, :width]


def heads_of(ref, k):
    return jnp.concatenate([ref[:, h * HS : (h + 1) * HS] for h in range(k * GROUP, (k + 1) * GROUP)], axis=0)


def probs_of(q6, keys, allowed):
    s = mm(q6, keys, NT) * SCALE
    s = jnp.where(allowed[None] > 0, s.reshape(GROUP, T, SEQ), -1e30)
    e = jnp.exp(s - jnp.max(s, axis=-1, keepdims=True))
    p = e * (1.0 / jnp.sum(e, axis=-1, keepdims=True))
    return p.reshape(GROUP * T, SEQ)


def attend_kernel(*refs):
    q_ref, kv_refs, rest = refs[0], refs[1:9], refs[9:]
    allowed_ref, x_ref, w_ref, gain_ref, wr_ref, chosen_ref, att_ref, mid_ref, hm_ref, kv_s, mid_s = rest
    j = pl.program_id(0)

    @pl.when(j == 0)
    def _():
        stack_rows(kv_refs, kv_s, 512)
        allowed = allowed_ref[...]
        for k in range(KV_HEADS):
            p = probs_of(heads_of(q_ref, k), kv_s[:, k * HS : (k + 1) * HS], allowed).astype(BF)
            o = mm(p, kv_s[:, KW + k * HS : KW + (k + 1) * HS])
            for g in range(GROUP):
                h = k * GROUP + g
                att_ref[:, h * HS : (h + 1) * HS] = o[g * T : (g + 1) * T].astype(BF)

    mid_s[j] = mm(att_ref[...], w_ref[...])

    @pl.when(j == 3)
    def _():
        mids = [x_ref[:, i * 384 : (i + 1) * 384].astype(F32) + mid_s[i] for i in range(4)]
        square = sum(jnp.sum(v * v, axis=-1, keepdims=True) for v in mids)
        r = lax.rsqrt(square * (1.0 / D) + EPS)
        logits = jnp.zeros((T, LANES), F32)
        for i in range(4):
            at = slice(i * 384, (i + 1) * 384)
            mid_ref[:, at] = mids[i]
            h = (mids[i] * r * gain_ref[1:2, at]).astype(BF)
            hm_ref[:, at] = h
            logits = logits + mm(h, wr_ref[at, :])
        chosen = chosen_ref[...] > 0
        top = jnp.max(jnp.where(chosen, logits, -jnp.inf), axis=-1, keepdims=True)
        e = jnp.where(chosen, jnp.exp(jnp.minimum(logits - top, 0.0)), 0.0)
        gate = e / jnp.sum(e, axis=-1, keepdims=True)
        high = gate.astype(BF).astype(F32)
        hm_ref[:, D:] = (high + pltpu.roll(gate - high, N_EXPERTS, 1)).astype(BF)


def attend(q, kvs, allowed, x, w_out, gains, w_r, chosen):
    return call(
        attend_kernel, "attend", (4,),
        [whole((T, D))] + [whole((T, 512))] * 8
        + [whole((T, SEQ)), whole((T, D)), pl.BlockSpec((D, 384), lambda j: (0, j)), whole((8, D)), whole((D, LANES)), whole((T, LANES))],
        [whole((T, D)), whole((T, D)), whole((T, D + LANES))],
        [sds((T, D), BF), sds((T, D), F32), sds((T, D + LANES), BF)],
        [pltpu.VMEM((SEQ, 512), BF), pltpu.VMEM((4, T, 384), F32)],
        2 * T * D * D + 4 * T * D * SEQ, 8 * 10**6,
        q, *kvs, allowed, x, w_out, gains, w_r, chosen,
    )


def expert_kernel(save, *refs):
    hm_refs, (mine_ref, wg_ref, wu_ref, wd_ref), rest = refs[:8], refs[8:12], refs[12:]
    if save:
        same_ref, other_ref, h_ref, g_ref, gate_ref, up_ref, act_ref, prod_ref, acc = rest
    else:
        same_ref, other_ref, h_ref, g_ref, acc = rest
    j = pl.program_id(0)

    @pl.when(j == 0)
    def _():
        stack_rows(hm_refs, h_ref, D)
        mine = mine_ref[0:1, :]
        for i, b in enumerate(hm_refs):
            g = jnp.sum(b[:, D:].astype(F32) * mine, axis=-1, keepdims=True)
            g_ref[i * T : (i + 1) * T, :] = jnp.broadcast_to(g, (T, LANES))

    h = h_ref[...]
    gate = mm(h, wg_ref[...])
    up = mm(h, wu_ref[...])
    act = (gate / (1.0 + jnp.exp(-gate)) * up).astype(BF)
    if save:
        gate_ref[...] = gate
        up_ref[...] = up
        act_ref[...] = act
    add = mm(act, wd_ref[...])

    @pl.when(j == 0)
    def _():
        acc[...] = add

    @pl.when(j > 0)
    def _():
        acc[...] += add

    @pl.when(j == 2)
    def _():
        prod = acc[...].astype(BF)
        if save:
            prod_ref[...] = prod
        part = (prod.astype(F32) * g_ref[:, 0:1]).astype(BF)
        same_ref[...] = part[:256]
        other_ref[...] = part[256:]


def expert(hms, mine, w_in, w_down, save):
    f_block = pl.BlockSpec((SEQ, 256), lambda j: (0, j))
    out_specs = [whole((256, D)), whole((256, D))]
    out_shape = [sds((256, D), BF), sds((256, D), BF)]
    extra_specs = [whole((SEQ, D)), whole((SEQ, LANES))]
    extra_shape = [sds((SEQ, D), BF), sds((SEQ, LANES), F32)]
    scratch = [pltpu.VMEM((SEQ, D), F32)]
    if save:
        out_specs += extra_specs + [f_block, f_block, f_block, whole((SEQ, D))]
        out_shape += extra_shape + [sds((SEQ, FF), F32), sds((SEQ, FF), F32), sds((SEQ, FF), BF), sds((SEQ, D), BF)]
    else:
        scratch = [pltpu.VMEM((SEQ, D), BF), pltpu.VMEM((SEQ, LANES), F32)] + scratch
    return call(
        lambda *refs: expert_kernel(save, *refs), "expert", (3,),
        [whole((T, D + LANES))] * 8
        + [whole((8, LANES)), pl.BlockSpec((D, 256), lambda j: (0, j)), pl.BlockSpec((D, 256), lambda j: (0, j + 3)),
           pl.BlockSpec((256, D), lambda j: (j, 0))],
        out_specs, out_shape, scratch, 6 * SEQ * D * FF, 12 * 10**6,
        *hms, mine, w_in, w_in, w_down,
    )


def expert_back_kernel(save, *refs):
    gs, (g_ref, gate_ref, up_ref, prod_ref, put_ref, wd_ref, wg_ref, wu_ref), rest = refs[:8], refs[8:16], refs[16:]
    if save:
        same_ref, other_ref, dprod, dg_ref, du_ref, acc = rest
    else:
        same_ref, other_ref, dprod, acc = rest
    j = pl.program_id(0)

    @pl.when(j == 0)
    def _():
        put = put_ref[...]
        for i, b in enumerate(gs):
            at = slice(i * T, (i + 1) * T)
            g = b[...].astype(F32)
            dprod[at, :] = (g * g_ref[at, 0:1]).astype(BF)
            d = jnp.sum(g * prod_ref[at, :].astype(F32), axis=-1, keepdims=True)
            high = d.astype(BF).astype(F32)
            lanes = (high * put[0:1, :] + (d - high) * put[1:2, :]).astype(BF)
            dst = same_ref if i < 4 else other_ref
            dst[(i % 4) * T : (i % 4 + 1) * T, D:] = lanes

    d_act = mm(dprod[...], wd_ref[...], NT)
    gate, up = gate_ref[...], up_ref[...]
    s = 1.0 / (1.0 + jnp.exp(-gate))
    dg = (d_act * up * (s * (1.0 + gate * (1.0 - s)))).astype(BF)
    du = (d_act * (gate * s)).astype(BF)
    if save:
        dg_ref[...] = dg
        du_ref[...] = du
    add = mm(dg, wg_ref[...], NT) + mm(du, wu_ref[...], NT)

    @pl.when(j == 0)
    def _():
        acc[...] = add

    @pl.when(j > 0)
    def _():
        acc[...] += add

    @pl.when(j == 2)
    def _():
        same_ref[:, :D] = acc[:256].astype(BF)
        other_ref[:, :D] = acc[256:].astype(BF)


def expert_back(gs, kept, put, w_in, w_down, save):
    g_share, gate, up, produced = kept
    f_block = pl.BlockSpec((SEQ, 256), lambda j: (0, j))
    out_specs = [whole((256, D + LANES)), whole((256, D + LANES))]
    out_shape = [sds((256, D + LANES), BF), sds((256, D + LANES), BF)]
    scratch = [pltpu.VMEM((SEQ, D), F32)]
    if save:
        out_specs += [whole((SEQ, D)), f_block, f_block]
        out_shape += [sds((SEQ, D), BF), sds((SEQ, FF), BF), sds((SEQ, FF), BF)]
    else:
        scratch = [pltpu.VMEM((SEQ, D), BF)] + scratch
    return call(
        lambda *refs: expert_back_kernel(save, *refs), "expert_back", (3,),
        [whole((T, D))] * 8
        + [whole((SEQ, LANES)), f_block, f_block, whole((SEQ, D)), whole((8, LANES)),
           pl.BlockSpec((256, D), lambda j: (j, 0)), pl.BlockSpec((D, 256), lambda j: (0, j)), pl.BlockSpec((D, 256), lambda j: (0, j + 3))],
        out_specs, out_shape, scratch, 6 * SEQ * D * FF, 14 * 10**6,
        *gs, g_share, gate, up, produced, put, w_down, w_in, w_in,
    )


def norm_back(x, gain, grad):
    r = lax.rsqrt(jnp.mean(x * x, axis=-1, keepdims=True) + EPS)
    n = x * r
    scaled = grad * gain
    back = r * (scaled - n * jnp.mean(scaled * n, axis=-1, keepdims=True))
    return jnp.sum(grad * n, axis=0, keepdims=True), back


def attend_back_kernel(*refs):
    rets, (g_ref, mid_ref, hm_ref, gain_ref, wr_ref, w_ref, q_ref), kv_refs, rest = refs[:4], refs[4:11], refs[11:19], refs[19:]
    allowed_ref, cos_ref, sin_ref, dmid_ref, datt_ref, dq_ref, same_ref, other_ref, dl_ref, gain_out, da, kv_s, kv_acc = rest
    j = pl.program_id(0)

    @pl.when(j == 0)
    def _():
        total = sum(r[...].astype(F32) for r in rets)
        lanes = total[:, D:]
        d_gate = lanes + pltpu.roll(lanes, LANES - N_EXPERTS, 1)
        share = hm_ref[:, D:].astype(F32)
        gate = share + pltpu.roll(share, LANES - N_EXPERTS, 1)
        gate = jnp.where(lax.broadcasted_iota(jnp.int32, (T, LANES), 1) < N_EXPERTS, gate, 0.0)
        inner = jnp.sum(gate * d_gate, axis=-1, keepdims=True)
        d_logits = (gate * (d_gate - inner)).astype(BF)
        dl_ref[...] = d_logits
        d_hm = total[:, :D] + mm(d_logits, wr_ref[...], NT)
        grad_gain, back = norm_back(mid_ref[...], gain_ref[1:2, :], d_hm)
        gain_out[...] = jnp.broadcast_to(grad_gain, (8, D))
        d_mid = g_ref[...].astype(F32) + back
        dmid_ref[...] = d_mid
        datt_ref[...] = d_mid.astype(BF)
        stack_rows(kv_refs, kv_s, 512)

    piece = mm(datt_ref[...], w_ref[...], NT).astype(BF)
    for i in range(3):
        da[j * 3 + i] = piece[:, i * HS : (i + 1) * HS]

    @pl.when(j == 3)
    def _():
        allowed = allowed_ref[...]
        cos, sin = cos_ref[...], sin_ref[...]
        for k in range(KV_HEADS):
            keys = kv_s[:, k * HS : (k + 1) * HS]
            values = kv_s[:, KW + k * HS : KW + (k + 1) * HS]
            q6 = heads_of(q_ref, k)
            d6 = da[k * GROUP : (k + 1) * GROUP].reshape(GROUP * T, HS)
            p = probs_of(q6, keys, allowed)
            dp = mm(d6, values, NT)
            ds = (p * (dp - jnp.sum(p * dp, axis=-1, keepdims=True)) * SCALE).astype(BF)
            dq = mm(ds, keys)
            for g in range(GROUP):
                h = k * GROUP + g
                dq_ref[:, h * HS : (h + 1) * HS] = rope_back(dq[g * T : (g + 1) * T], cos, sin).astype(BF)
            kv_acc[:, k * HS : (k + 1) * HS] = mm(ds, q6, TN)
            kv_acc[:, KW + k * HS : KW + (k + 1) * HS] = mm(p.astype(BF), d6, TN)
        same_ref[...] = kv_acc[:256].astype(BF)
        other_ref[...] = kv_acc[256:].astype(BF)


def attend_back(rets, g, mid, hm, gains, w_r, w_out, q, kvs, allowed, cos, sin):
    return call(
        attend_back_kernel, "attend_back", (4,),
        [whole((T, D + LANES))] * 4
        + [whole((T, D)), whole((T, D)), whole((T, D + LANES)), whole((8, D)), whole((D, LANES)), pl.BlockSpec((384, D), lambda j: (j, 0)), whole((T, D))]
        + [whole((T, 512))] * 8 + [whole((T, SEQ)), whole((T, HS)), whole((T, HS))],
        [whole((T, D)), whole((T, D)), whole((T, D)), whole((256, 512)), whole((256, 512)), whole((T, LANES)), whole((8, D))],
        [sds((T, D), F32), sds((T, D), BF), sds((T, D), BF), sds((256, 512), BF), sds((256, 512), BF), sds((T, LANES), BF), sds((8, D), F32)],
        [pltpu.VMEM((HEADS, T, HS), BF), pltpu.VMEM((SEQ, 512), BF), pltpu.VMEM((SEQ, 512), F32)],
        2 * T * D * D + 10 * T * D * SEQ, 8 * 10**6,
        *rets, g, mid, hm, gains, w_r, w_out, q, *kvs, allowed, cos, sin,
    )


MSG = 2048 + LANES


def qkv_back_kernel(*refs):
    rets, (dq_ref, dl_ref, gm_ref, x_ref, gain_ref, w_ref, cos_ref, sin_ref, dmid_ref), rest = refs[:4], refs[4:13], refs[13:]
    gin_ref, glow_ref, msg_ref, dh = rest
    j = pl.program_id(0)

    @pl.when(j == 0)
    def _():
        d_kv = sum(r[...].astype(F32) for r in rets)
        cos, sin = cos_ref[...], sin_ref[...]
        msg_ref[:T, :D] = dq_ref[...]
        for i in range(KV_HEADS):
            msg_ref[:T, D + i * HS : D + (i + 1) * HS] = rope_back(d_kv[:, i * HS : (i + 1) * HS], cos, sin).astype(BF)
        msg_ref[:T, D + KW : 2048] = d_kv[:, KW:].astype(BF)
        msg_ref[:T, 2048:] = dl_ref[...]

    dh[j] = mm(msg_ref[:T, :2048], w_ref[...], NT)

    @pl.when(j == 3)
    def _():
        d_h = jnp.concatenate([dh[i] for i in range(4)], axis=1)
        grad_gain, back = norm_back(x_ref[...].astype(F32), gain_ref[0:1, :], d_h)
        g_in = dmid_ref[...] + back
        gin_ref[...] = g_in
        glow_ref[...] = g_in.astype(BF)
        row = lax.broadcasted_iota(jnp.int32, (16, D), 0)
        gm = jnp.broadcast_to(gm_ref[0:1, :], (16, D))
        both = jnp.where(row == 0, jnp.broadcast_to(grad_gain, (16, D)), jnp.where(row == 1, gm, 0.0))
        msg_ref[T:, :D] = both.astype(BF)
        msg_ref[T:, D:] = jnp.zeros((16, MSG - D), BF)


def qkv_back(rets, dq, dl, gm, x, gains, w_packed, cos, sin, d_mid):
    return call(
        qkv_back_kernel, "qkv_back", (4,),
        [whole((T, 512))] * 4
        + [whole((T, D)), whole((T, LANES)), whole((8, D)), whole((T, D)), whole((8, D)), pl.BlockSpec((384, 2048), lambda j: (j, 0)),
           whole((T, HS)), whole((T, HS)), whole((T, D))],
        [whole((T, D)), whole((T, D)), whole((T + 16, MSG))],
        [sds((T, D), F32), sds((T, D), BF), sds((T + 16, MSG), BF)],
        [pltpu.VMEM((4, T, 384), F32)],
        2 * T * D * 2048, 9 * 10**6,
        *rets, dq, dl, gm, x, gains, w_packed, cos, sin, d_mid,
    )


SLICE = D // 8


def attn_grad_kernel(*refs):
    order_ref, left_ref = refs[0], refs[1]
    msgs, datts = refs[2:18], refs[18:34]
    gq_ref, go_ref, gr_ref, gain_ref = refs[34:38]
    lh, rq, ro = refs[38:41]
    gains = jnp.zeros((16, D), F32)
    for m in range(2):
        for i in range(8):
            at = slice((m * 8 + i) * T, (m * 8 + i + 1) * T)
            lh[at, :] = left_ref[order_ref[i], m * T : (m + 1) * T, :]
            rq[at, :] = msgs[m * 8 + i][:T, :]
            ro[at, :] = datts[m * 8 + i][...]
            gains = gains + msgs[m * 8 + i][T:, :D].astype(F32)
    gain_ref[...] = gains
    for c in range(4):
        at = slice(c * 512, (c + 1) * 512)
        gq_ref[:, at] = mm(lh[:, :256], rq[:, at], TN)[:SLICE].astype(BF)
    for c in range(3):
        at = slice(c * 512, (c + 1) * 512)
        go_ref[:, at] = mm(lh[:, 256:512], ro[:, at], TN)[:SLICE].astype(BF)
    gr_ref[...] = mm(lh[:, 512:], rq[:, 2048:], TN)[:SLICE]


def attn_grad(order, left, msgs, datts):
    vm = pl.BlockSpec(memory_space=pltpu.VMEM)
    return pl.pallas_call(
        attn_grad_kernel,
        name="attn_grad",
        in_specs=[pl.BlockSpec(memory_space=pltpu.SMEM)] + [vm] * 33,
        out_specs=[vm] * 4,
        out_shape=[sds((SLICE, 2048), BF), sds((SLICE, D), BF), sds((SLICE, LANES), F32), sds((16, D), F32)],
        scratch_shapes=[pltpu.VMEM((1024, 768), BF), pltpu.VMEM((1024, MSG), BF), pltpu.VMEM((1024, D), BF)],
        compiler_params=pltpu.CompilerParams(vmem_limit_bytes=40 * 2**20),
        cost_estimate=pl.CostEstimate(flops=2 * 1024 * 256 * 3584, bytes_accessed=10 * 10**6, transcendentals=0),
    )(order, left, *msgs, *datts)


def body(tokens_in, cotangent, routes, gain_attn, w_query, w_keyval, w_out, gain_moe, w_router, w_in, w_down):
    is_first = lax.axis_index("section") == 0
    shard = lax.axis_index("shard")
    chip, core = shard // 2, shard % 2

    extra = jnp.concatenate([w_router[0], gain_attn[0][:, None], gain_moe[0][:, None]], axis=1)
    extra = jnp.pad(extra, ((0, 0), (0, LANES - extra.shape[1])))
    packed = jnp.concatenate([w_query[0], w_keyval[0], extra], axis=1)
    w_packed = lax.all_gather(packed, "shard", axis=0, tiled=True)
    w_o = lax.all_gather(w_out[0], "shard", axis=0, tiled=True)
    w_r = w_packed[:, 2048:]
    pick = (jnp.arange(LANES)[None, :] == (jnp.arange(8)[:, None] + N_EXPERTS)) & (jnp.arange(8)[:, None] < 2)
    gains = mm(pick.astype(BF), w_r, NT)
    inner, outer = w_in[0, 0], w_down[0, 0]

    half = HS // 2
    frequency = ROPE_BASE ** (-jnp.arange(half, dtype=F32) * 2.0 / HS)
    place = shard * T + jnp.arange(T, dtype=jnp.int32)
    angles = place.astype(F32)[:, None] * frequency[None, :]
    cos = jnp.concatenate([jnp.cos(angles)] * 2, axis=1)
    sin = jnp.concatenate([-jnp.sin(angles), jnp.sin(angles)], axis=1)
    order = jnp.stack([((chip - k) % 4) * 2 + c for c in (core, 1 - core) for k in range(4)]).astype(jnp.int32)
    key_place = (order[:, None] * T + jnp.arange(T, dtype=jnp.int32)[None, :]).reshape(1, SEQ)
    allowed = (key_place <= place[:, None]).astype(F32)
    lane = jnp.arange(LANES, dtype=jnp.int32)
    mine = ((lane == shard) | (lane == shard + N_EXPERTS)).astype(F32)
    mine = jnp.broadcast_to(mine[None, :], (8, LANES))
    put = jnp.stack([lane == shard, lane == shard + N_EXPERTS]).astype(F32)
    put = jnp.pad(put, ((0, 6), (0, 0)))

    def layer(x, route, save):
        chosen = jnp.any(route[:, :, None] == lane[None, None, :], axis=1).astype(F32)
        q, kv, h_attn = qkv(x, gains, w_packed, cos, sin)
        kvs = gather_blocks(kv)
        att, mid, hm = attend(q, kvs, allowed, x, w_o, gains, w_r, chosen)
        hms = gather_blocks(hm)
        out = expert(hms, mine, inner, outer, save)
        rets = scatter_sum_blocks(out[0], out[1])
        y = (mid + sum(r.astype(F32) for r in rets)).astype(BF)
        return y, (x, q, h_attn, kvs, att, mid, hm) + tuple(out[2:])

    def layer_back(g, kept, save):
        x, q, h_attn, kvs, att, mid, hm, h_all, g_share, gate, up, act, produced = kept
        gs = gather_blocks(g)
        out = expert_back(gs, (g_share, gate, up, produced), put, inner, outer, save)
        rets = scatter_sum_blocks(out[0], out[1])
        d_mid, d_att, dq, kv_same, kv_other, dl, gm = attend_back(
            rets, g, mid, hm, gains, w_r, w_o, q, kvs, allowed, cos, sin
        )
        kv_rets = scatter_sum_blocks(kv_same, kv_other)
        g_in, g_low, msg = qkv_back(kv_rets, dq, dl, gm, x, gains, w_packed, cos, sin, d_mid)
        return g_in, g_low, msg, d_att, out[2:]

    micros = range(2)
    first = [layer(tokens_in[m, 0], routes[0, m, 0], False)[0] for m in micros]
    arrived = [lax.ppermute(first[m], "section", [(0, 1)]) for m in micros]
    inputs = [jnp.where(is_first, tokens_in[m, 0], arrived[m]) for m in micros]
    second = [layer(inputs[m], routes[0, m, 0], True) for m in micros]
    acts = [second[m][0] for m in micros]
    kept = [second[m][1] for m in micros]

    back = [layer_back(cotangent[m, 0], kept[m], False)[1] for m in micros]
    arrived = [lax.ppermute(back[m], "section", [(1, 0)]) for m in micros]
    given = [jnp.where(is_first, arrived[m], cotangent[m, 0]) for m in micros]
    final = [layer_back(given[m], kept[m], True) for m in micros]

    h_all = [kept[m][7] for m in micros]
    act = [kept[m][11] for m in micros]
    d_prod = [final[m][4][0] for m in micros]
    d_gate = [final[m][4][1] for m in micros]
    d_up = [final[m][4][2] for m in micros]

    def both(left, right):
        return sum(mm(left[m], right[m], TN) for m in micros).astype(BF)

    send_in = jnp.concatenate([both(h_all, d_gate), both(h_all, d_up)], axis=1)
    send_down = both(act, d_prod)
    send = jnp.concatenate([send_in.reshape(8, SLICE, D), send_down.reshape(8, SLICE // 2, D)], axis=1)
    got = lax.all_to_all(send, "rep", split_axis=0, concat_axis=0, tiled=True)
    expert_sums = jnp.sum(got.astype(F32), axis=0)

    def columns(rows):
        cut = rows[:, :D].reshape(T, 8, SLICE).transpose(1, 0, 2)
        return jnp.pad(cut, ((0, 0), (0, 0), (0, 256 - SLICE)))

    left = jnp.concatenate(
        [jnp.concatenate([columns(kept[m][2]), columns(kept[m][4]), columns(kept[m][6])], axis=2) for m in micros], axis=1
    )
    left = lax.all_to_all(left, "shard", split_axis=0, concat_axis=0, tiled=True)
    msgs = [b for m in micros for b in gather_blocks(final[m][2])]
    datts = [b for m in micros for b in gather_blocks(final[m][3])]
    gq, go, gr, gg = attn_grad(order, left, msgs, datts)
    gg = lax.dynamic_slice(gg[:2], (0, shard * SLICE), (2, SLICE))
    small = jnp.concatenate([gr[:, :N_EXPERTS], gg.T], axis=1).astype(BF)
    small = jnp.pad(small, ((0, 0), (0, 64 - small.shape[1])))

    def pieces(rows):
        return rows.reshape(SLICE, 8, -1).transpose(1, 0, 2)

    send = jnp.concatenate(
        [pieces(gq[:, :D]), pieces(gq[:, D:]), jnp.broadcast_to(small[None], (8, SLICE, 64)), pieces(go)], axis=2
    )
    got = lax.all_to_all(send, "rep", split_axis=0, concat_axis=0, tiled=True)
    sums = jnp.sum(got.astype(F32), axis=0)
    g_q, g_kv, g_small, g_o = sums[:, :SLICE], sums[:, SLICE : SLICE + 64], sums[:, SLICE + 64 : SLICE + 128], sums[:, SLICE + 128 :]

    return (
        jnp.stack(acts)[None, :, None],
        jnp.stack([final[m][0] for m in micros])[None, :, None],
        g_small[None, :, N_EXPERTS],
        g_q[None],
        g_kv[None],
        g_o[None],
        g_small[None, :, N_EXPERTS + 1],
        g_small[None, :, :N_EXPERTS],
        expert_sums[None, None, :SLICE],
        expert_sums[None, None, SLICE:],
    )


def solution(mesh):
    in_specs = (
        P(None, "rep", "shard", None),
        P(None, "rep", "shard", None),
        P("section", None, "rep", "shard", None),
        P("section", "shard"),
        P("section", "shard", None),
        P("section", "shard", None),
        P("section", "shard", None),
        P("section", "shard"),
        P("section", "shard", None),
        P("section", "shard", None, None),
        P("section", "shard", None, None),
    )
    out_specs = (
        P("section", None, "rep", "shard", None),
        P("section", None, "rep", "shard", None),
        P("section", "shard"),
        P("section", "shard", "rep"),
        P("section", "shard", "rep"),
        P("section", "shard", "rep"),
        P("section", "shard"),
        P("section", "shard", None),
        P("section", "shard", "rep", None),
        P("section", "shard", "rep", None),
    )
    return jax.shard_map(body, mesh=mesh, in_specs=in_specs, out_specs=out_specs, check_vma=False)
```

time: 1510 us -> 722 us (0.48)
  waiting for transfers between devices: 802 us -> 243 us
  matrix products: 223 us -> 14.4 us
  blocking collectives: 172 us -> 0 us
  Pallas kernels: 0 us -> 145 us
  starting transfers between devices: 52.9 us -> 163 us
  local copies, waits for them, and re-layouts: 155 us -> 97.4 us
  other arithmetic: 76.6 us -> 31.5 us
    reduce_scatter x11 -> x0, waiting for transfers between devices: 367 us -> none  [the longest x3 117 us: body(): lax.psum_scatter(part_wq.astype(jnp.bfloat16), 'shard', scatter_dimension...]
    unnamed x32 -> x2, waiting for transfers between devices: 268 us -> 0.71 us
    dot_general x72 -> x7, matrix products: 223 us -> 14.4 us  [mm(): return lax.dot_general(a, b, dims, preferred_element_type=F32)]
    pallas_call x0 -> x25, Pallas kernels: none -> 145 us  [the longest x24 141 us: call(): pl.pallas_call(kernel, name=name, grid=grid, in_specs=in_specs, out_specs...]
    ppermute x4 -> x164, starting transfers between devices: 13.5 us -> 147 us  [the longest x84 116 us: along_y(): return lax.ppermute(x, 'shard', [(i, (i + 2 * k) % 8) for i in range(8)])]
    ppermute x4 -> x164, waiting for transfers between devices: 24.2 us -> 126 us  [the longest x84 114 us: along_y(): return lax.ppermute(x, 'shard', [(i, (i + 2 * k) % 8) for i in range(8)])]
    all_gather x4 -> x0, blocking collectives: 60.2 us -> none  [the longest x3 39.7 us: layer_forward(): pairing_everything = lax.all_gather(pair_here, 'shard', axis=0, tiled=True)]
    unnamed x2 -> x0, blocking collectives: 39.5 us -> none
  transfers between devices with their start and end apart: 37 -> 169, of which waited for: 34 -> 47; matrix products, arithmetic and copies ran while one was open for 12% -> 9% of each run, Pallas kernels for 0% -> 20%
where the time goes in v1:
time: 722 us; the launch traced here: 712 us
  waiting for transfers between devices  243 us (34%)
  starting transfers between devices  163 us (23%)
  Pallas kernels  145 us (20%)
  local copies, waits for them, and re-layouts  97.4 us (13%)
  other arithmetic  31.5 us (4%)
  between operations  17.3 us (2%)
  matrix products  14.4 us (2%)
    pallas_call x24, Pallas kernels, call(): pl.pallas_call(kernel, name=name, grid=grid, in_specs=in_specs, out_specs...  141 us
    ppermute x84, starting transfers between devices, along_y(): return lax.ppermute(x, 'shard', [(i, (i + 2 * k) % 8) for i in range(8)])  116 us
    ppermute x84, waiting for transfers between devices, along_y(): return lax.ppermute(x, 'shard', [(i, (i + 2 * k) % 8) for i in range(8)])  114 us
    unnamed x491, local copies, waits for them, and re-layouts  66 us
    all_to_all x2, waiting for transfers between devices, body(): got = lax.all_to_all(send, 'rep', split_axis=0, concat_axis=0, tiled=True)  61.9 us
    all_gather x1, waiting for transfers between devices, body(): w_packed = lax.all_gather(packed, 'shard', axis=0, tiled=True)  43.6 us
    ppermute x76, starting transfers between devices, swap(): return lax.ppermute(x, 'shard', [(i, i ^ 1) for i in range(8)])  17.1 us
    reshape x12, local copies, waits for them, and re-layouts, columns(): cut = rows[:, :D].reshape(T, 8, SLICE).transpose(1, 0, 2)  15.5 us
  transfers between devices with their start and end apart: 169, of which 47 were waited for; matrix products, arithmetic and copies ran while one was open for 9% of the time, Pallas kernels for 20%

profile of v1, /device:TPU:0, one launch (start us, length us, event | category | flops | bytes accessed | tf_op | source)
XLA Modules:
  0.0 711.6 jit_solution(1399195412100437818)
XLA Ops:
  11.9 43.6 %all-gather.4.cloned.1.call-done.w_ref.refs_9_ = bf16[1536,2176]{1,0:T(8,128)(2,1)} async-done(((bf16[192,2176]{1,0:T(8,128)(2,1)}), bf16[1536,2176]{1,0:T(8,128)(2,1)}) %all-gather.4.cloned.1.call-update) | async-done | bytes 6684688 | tf_op jit(solution)/shard_map/all_gather | solution.py:494
  83.4 11.0 %all-gather.6.cloned.1.call-done = bf16[1,1536,1536]{2,1,0:T(8,128)(2,1)} async-done(((bf16[1,192,1536]{2,1,0:T(8,128)(2,1)}), bf16[1,1536,1536]{2,1,0:T(8,128)(2,1)}) %all-gather.6.cloned.1.call-update) | async-done | bytes 4718608 | tf_op jit(solution)/shard_map/all_gather | solution.py:495
  126.5 7.6 %collective-permute-done.44.refs_1_ = bf16[64,1664]{1,0:T(8,128)(2,1)} collective-permute-done((bf16[64,1664]{1,0:T(8,128)(2,1)}, bf16[64,1664]{1,0:T(8,128)(2,1)}, u32[]{:S(2)}, u32[]{:S(2)}) %collective-permute-start.44) | collective-permute-done | bytes 213024 | tf_op jit(solution)/shard_map/ppermute | solution.py:63
  140.2 7.3 %expert.4 = (bf16[256,1536]{1,0:T(8,128)(2,1)S(1)}, bf16[256,1536]{1,0:T(8,128)(2,1)S(1)}) custom-call(bf16[64,1664]{1,0:T(8,128)(2,1)S(1)} %copy-done.140, bf16[64,1664]{1,0:T(8,128)(2,1)} %collective-permute-done.7.refs_1_, bf16[64,1664]{1,0:T(8,128)(2,1)} %collective-permute-done.8.refs_2_, bf16[64,1664]{1,0:T(8,128)(2,1)} %collective-permute-done.9.refs_3_, ...), custom_call_target="tpu_custom_call" | custom-call | flops 3623878656 | bytes 12000000 | tf_op jit(solution)/shard_map/expert/pallas_call | solution.py:43
  148.0 7.1 expert.6
  170.4 5.5 collective-permute-start.18
  178.3 5.5 collective-permute-start.55
  228.9 5.3 collective-permute-done.26.refs_1_
  244.1 7.3 %expert.5 = (bf16[256,1536]{1,0:T(8,128)(2,1)S(1)}, bf16[256,1536]{1,0:T(8,128)(2,1)S(1)}, bf16[512,1536]{1,0:T(8,128)(2,1)S(1)}, f32[512,128]{1,0:T(8,128)S(1)}...) custom-call(bf16[64,1664]{1,0:T(8,128)(2,1)S(1)} %get-tuple-element., ...), custom_call_target="tpu_custom_call" | custom-call | flops 3623878656 | bytes 12000000 | tf_op jit(solution)/shard_map/expert/pallas_call | solution.py:43
  256.1 11.4 %expert_back.4 = (bf16[256,1664]{1,0:T(8,128)(2,1)S(1)}, bf16[256,1664]{1,0:T(8,128)(2,1)}) custom-call(bf16[64,1536]{1,0:T(8,128)(2,1)} %get-tuple-element.290.refs_0_.refs_4_, bf16[64,1536]{1,0:T(8,128)(2,1)} %collective-permute-done.74.refs_1_, bf16[64,1536]{1,0:T(8,128)(2,1)} %collective-permute-done.75.refs_2_, ...), custom_call_target="tpu_custom_call" | custom-call | flops 3623878656 | bytes 14000000 | tf_op jit(solution)/shard_map/expert_back/pallas_call | solution.py:43
  269.1 7.3 %expert.7 = (bf16[256,1536]{1,0:T(8,128)(2,1)S(1)}, bf16[256,1536]{1,0:T(8,128)(2,1)S(1)}, bf16[512,1536]{1,0:T(8,128)(2,1)S(1)}, f32[512,128]{1,0:T(8,128)S(1)}...) custom-call(bf16[64,1664]{1,0:T(8,128)(2,1)S(1)} %get-tuple-element., ...), custom_call_target="tpu_custom_call" | custom-call | flops 3623878656 | bytes 12000000 | tf_op jit(solution)/shard_map/expert/pallas_call | solution.py:43
  278.3 11.4 %expert_back.6 = (bf16[256,1664]{1,0:T(8,128)(2,1)S(1)}, bf16[256,1664]{1,0:T(8,128)(2,1)S(1)}) custom-call(bf16[64,1536]{1,0:T(8,128)(2,1)S(1)} %copy-done.35, bf16[64,1536]{1,0:T(8,128)(2,1)S(1)} %collective-permute-done.105.refs_1_, bf16[64,1536]{1,0:T(8,128)(2,1)S(1)} %collective-permute-done.106.refs_2_, ...), custom_call_target="tpu_custom_call" | custom-call | flops 3623878656 | bytes 14000000 | tf_op jit(solution)/shard_map/expert_back/pallas_call | solution.py:43
  299.8 6.1 collective-permute-start.115
  307.9 6.3 attend_back.4
  315.6 5.2 attend_back.6
  343.9 5.5 collective-permute-done.120
  361.0 6.9 collective-permute-done.90.refs_1_
  369.4 10.3 %expert_back.7 = (bf16[256,1664]{1,0:T(8,128)(2,1)S(1)}, bf16[256,1664]{1,0:T(8,128)(2,1)S(1)}, bf16[512,1536]{1,0:T(8,128)(2,1)S(1)}, bf16[512,768]{1,0:T(8,128)(2,1)S(1)}, bf16[512,768]{1,0:T(8,128)(2,1)S(1)}) custom-call(bf16[64,1536]{1,0:T(8,128)(2,1)S(1)} %get-tuple-element.289.refs_0_.refs_4_, bf16[64,1536]{1,0:T(8,128)(2,1)S(1)} %collective-permute-done.121.refs_1_, ...), custom_call_target="tpu_custom_call" | custom-call | flops 3623878656 | bytes 14000000 | tf_op jit(solution)/shard_map/expert_back/pallas_call | solution.py:43
  382.6 10.3 %expert_back.5 = (bf16[256,1664]{1,0:T(8,128)(2,1)S(1)}, bf16[256,1664]{1,0:T(8,128)(2,1)S(1)}, bf16[512,1536]{1,0:T(8,128)(2,1)S(1)}, bf16[512,768]{1,0:T(8,128)(2,1)S(1)}, bf16[512,768]{1,0:T(8,128)(2,1)S(1)}) custom-call(bf16[64,1536]{1,0:T(8,128)(2,1)S(1)} %get-tuple-element.288.refs_0_.refs_4_, bf16[64,1536]{1,0:T(8,128)(2,1)S(1)} %collective-permute-done.90.refs_1_, ...), custom_call_target="tpu_custom_call" | custom-call | flops 3623878656 | bytes 14000000 | tf_op jit(solution)/shard_map/expert_back/pallas_call | solution.py:43
  429.5 6.2 attend_back.7
  437.3 6.3 attend_back.5
  448.3 6.7 all-to-all-start
  462.3 18.3 %collective-permute-done.150.refs_19_ = bf16[64,1536]{1,0:T(8,128)(2,1)S(1)} collective-permute-done((bf16[64,1536]{1,0:T(8,128)(2,1)}, bf16[64,1536]{1,0:T(8,128)(2,1)S(1)}, u32[]{:S(2)}, u32[]{:S(2)}) %collective-permute-start.150) | collective-permute-done | bytes 196640 | tf_op jit(solution)/shard_map/ppermute | solution.py:63
  480.7 4.9 collective-permute-done.151.refs_20_
  523.2 7.7 %collective-permute-done.136.refs_3_ = bf16[80,2176]{1,0:T(8,128)(2,1)S(1)} collective-permute-done((bf16[80,2176]{1,0:T(8,128)(2,1)S(1)}, bf16[80,2176]{1,0:T(8,128)(2,1)S(1)}, u32[]{:S(2)}, u32[]{:S(2)}) %collective-permute-start.136) | collective-permute-done | bytes 348192 | tf_op jit(solution)/shard_map/ppermute | solution.py:63
  535.6 10.7 %collective-permute-done.143.refs_11_ = bf16[80,2176]{1,0:T(8,128)(2,1)S(1)} collective-permute-done((bf16[80,2176]{1,0:T(8,128)(2,1)S(1)}, bf16[80,2176]{1,0:T(8,128)(2,1)S(1)}, u32[]{:S(2)}, u32[]{:S(2)}) %collective-permute-start.143) | collective-permute-done | bytes 348192 | tf_op jit(solution)/shard_map/ppermute | solution.py:63
  551.5 6.8 copy.99
  595.2 5.1 pad_maximum_fusion
  600.3 12.6 %all-to-all-done.1 = bf16[8,192,512]{2,1,0:T(8,128)(2,1)} async-done(((bf16[8,192,512]{2,1,0:T(8,128)(2,1)}), bf16[8,192,512]{2,1,0:T(8,128)(2,1)}, u32[]{:S(2)}, u32[]{:S(2)}) %all-to-all-start.1) | async-done | bytes 1572896 | tf_op jit(solution)/shard_map/all_to_all | solution.py:588
  612.8 5.1 all-to-all-start.2
  637.1 5.1 collective-permute-done.35
  648.8 49.4 %all-to-all-done.2 = bf16[8,288,1536]{2,1,0:T(8,128)(2,1)} async-done(((bf16[8,288,1536]{2,1,0:T(8,128)(2,1)}), bf16[8,288,1536]{2,1,0:T(8,128)(2,1)}, u32[]{:S(2)}, u32[]{:S(2)}) %all-to-all-start.2) | async-done | bytes 7077920 | tf_op jit(solution)/shard_map/all_to_all | solution.py:564
  (926 shorter events, 368.6 us)
Async XLA Ops:
  7.2 48.3 %all-gather.4.cloned.1.call-start = ((), (), s32[]{:S(2)}) async-start(), calls=%async_computation.3 | async-start | bytes 7520256 | tf_op jit(solution)/shard_map/all_gather | solution.py:494
  10.3 84.1 %all-gather.6.cloned.1.call-start = ((), (), s32[]{:S(2)}) async-start(), calls=%async_computation.4 | async-start | bytes 5308416 | tf_op jit(solution)/shard_map/all_gather | solution.py:495
  80.5 21.9 %collective-permute-start.40 = (bf16[64,512]{1,0:T(8,128)(2,1)S(1)}, bf16[64,512]{1,0:T(8,128)(2,1)S(1)}, u32[]{:S(2)}, u32[]{:S(2)}) collective-permute-start(bf16[64,512]{1,0:T(8,128)(2,1)S(1)} %get-tuple-element.113.refs_1_), channel_id=1, source_target_pairs={{0,1},{1,0},{2,3},{3,2},{4,5},{5,4},{6,7},{7,6},{8,9},{9,8},{10,11... | collective-permute-start | bytes 196616 | tf_op jit(solution)/shard_map/ppermute | solution.py:59
  82.7 23.3 %collective-permute-start.41 = (bf16[64,512]{1,0:T(8,128)(2,1)S(1)}, bf16[64,512]{1,0:T(8,128)(2,1)S(1)}, u32[]{:S(2)}, u32[]{:S(2)}) collective-permute-start(bf16[64,512]{1,0:T(8,128)(2,1)S(1)} %collective-permute-done.37.refs_2_), channel_id=1, source_target_pairs={{0,1},{1,0},{2,3},{3,2},{4,5},{5,4},{6,7},{7,6},{8,9},{9,8},{10,11... | collective-permute-start | bytes 196616 | tf_op jit(solution)/shard_map/ppermute | solution.py:59
  82.7 24.7 %collective-permute-start.42 = (bf16[64,512]{1,0:T(8,128)(2,1)S(1)}, bf16[64,512]{1,0:T(8,128)(2,1)S(1)}, u32[]{:S(2)}, u32[]{:S(2)}) collective-permute-start(bf16[64,512]{1,0:T(8,128)(2,1)S(1)} %collective-permute-done.38.refs_3_), channel_id=1, source_target_pairs={{0,1},{1,0},{2,3},{3,2},{4,5},{5,4},{6,7},{7,6},{8,9},{9,8},{10,11... | collective-permute-start | bytes 196616 | tf_op jit(solution)/shard_map/ppermute | solution.py:59
  83.2 24.8 %collective-permute-start.43 = (bf16[64,512]{1,0:T(8,128)(2,1)S(1)}, bf16[64,512]{1,0:T(8,128)(2,1)S(1)}, u32[]{:S(2)}, u32[]{:S(2)}) collective-permute-start(bf16[64,512]{1,0:T(8,128)(2,1)S(1)} %collective-permute-done.39.refs_4_), channel_id=1, source_target_pairs={{0,1},{1,0},{2,3},{3,2},{4,5},{5,4},{6,7},{7,6},{8,9},{9,8},{10,11... | collective-permute-start | bytes 196616 | tf_op jit(solution)/shard_map/ppermute | solution.py:59
  101.7 19.9 %collective-permute-start.7 = (bf16[64,1664]{1,0:T(8,128)(2,1)S(1)}, bf16[64,1664]{1,0:T(8,128)(2,1)}, u32[]{:S(2)}, u32[]{:S(2)}) collective-permute-start(bf16[64,1664]{1,0:T(8,128)(2,1)S(1)} %get-tuple-element.103.refs_0_), channel_id=1, source_target_pairs={{0,2},{1,3},{2,4},{3,5},{4,6},{5,7},{6,0},{7,1},{8,10},{9,11},{10,... | collective-permute-start | bytes 638984 | tf_op jit(solution)/shard_map/ppermute | solution.py:63
  103.1 19.7 %collective-permute-start.8 = (bf16[64,1664]{1,0:T(8,128)(2,1)S(1)}, bf16[64,1664]{1,0:T(8,128)(2,1)}, u32[]{:S(2)}, u32[]{:S(2)}) collective-permute-start(bf16[64,1664]{1,0:T(8,128)(2,1)S(1)} %get-tuple-element.103.refs_0_), channel_id=1, source_target_pairs={{0,4},{1,5},{2,6},{3,7},{4,0},{5,1},{6,2},{7,3},{8,12},{9,13},{10,... | collective-permute-start | bytes 638984 | tf_op jit(solution)/shard_map/ppermute | solution.py:63
  106.6 18.7 %collective-permute-start.9 = (bf16[64,1664]{1,0:T(8,128)(2,1)S(1)}, bf16[64,1664]{1,0:T(8,128)(2,1)}, u32[]{:S(2)}, u32[]{:S(2)}) collective-permute-start(bf16[64,1664]{1,0:T(8,128)(2,1)S(1)} %get-tuple-element.103.refs_0_), channel_id=1, source_target_pairs={{0,6},{1,7},{2,0},{3,1},{4,2},{5,3},{6,4},{7,5},{8,14},{9,15},{10,... | collective-permute-start | bytes 638984 | tf_op jit(solution)/shard_map/ppermute | solution.py:63
  170.4 18.4 %collective-permute-start.18 = (bf16[64,1536]{1,0:T(8,128)(2,1)}, bf16[64,1536]{1,0:T(8,128)(2,1)}, u32[]{:S(2)}, u32[]{:S(2)}) collective-permute-start(bf16[64,1536]{1,0:T(8,128)(2,1)} %add_convert_fusion.34), channel_id=1, source_target_pairs={{0,64},{1,65},{2,66},{3,67},{4,68},{5,69},{6,70},{7,71},{8,72},{9,... | collective-permute-start | bytes 589832 | tf_op jit(solution)/shard_map/ppermute | solution.py:541
  197.6 24.5 %collective-permute-start.105 = (bf16[64,1536]{1,0:T(8,128)(2,1)S(1)}, bf16[64,1536]{1,0:T(8,128)(2,1)S(1)}, u32[]{:S(2)}, u32[]{:S(2)}) collective-permute-start(bf16[64,1536]{1,0:T(8,128)(2,1)S(1)} %copy-done.35), channel_id=1, source_target_pairs={{0,2},{1,3},{2,4},{3,5},{4,6},{5,7},{6,0},{7,1},{8,10},{9,11},{10,... | collective-permute-start | bytes 589832 | tf_op jit(solution)/shard_map/ppermute | solution.py:63
  200.7 22.4 %collective-permute-start.106 = (bf16[64,1536]{1,0:T(8,128)(2,1)S(1)}, bf16[64,1536]{1,0:T(8,128)(2,1)S(1)}, u32[]{:S(2)}, u32[]{:S(2)}) collective-permute-start(bf16[64,1536]{1,0:T(8,128)(2,1)S(1)} %copy-done.35), channel_id=1, source_target_pairs={{0,4},{1,5},{2,6},{3,7},{4,0},{5,1},{6,2},{7,3},{8,12},{9,13},{10,... | collective-permute-start | bytes 589832 | tf_op jit(solution)/shard_map/ppermute | solution.py:63
  268.6 21.5 %collective-permute-start.81 = (bf16[256,1664]{1,0:T(8,128)(2,1)}, bf16[256,1664]{1,0:T(8,128)(2,1)}, u32[]{:S(2)}, u32[]{:S(2)}) collective-permute-start(bf16[256,1664]{1,0:T(8,128)(2,1)} %get-tuple-element.129), channel_id=1, source_target_pairs={{0,1},{1,0},{2,3},{3,2},{4,5},{5,4},{6,7},{7,6},{8,9},{9,8},{10,11... | collective-permute-start | bytes 2555912 | tf_op jit(solution)/shard_map/ppermute | solution.py:59
  296.4 17.9 %collective-permute-start.113 = (bf16[64,1664]{1,0:T(8,128)(2,1)S(1)}, bf16[64,1664]{1,0:T(8,128)(2,1)S(1)}, u32[]{:S(2)}, u32[]{:S(2)}) collective-permute-start(bf16[64,1664]{1,0:T(8,128)(2,1)S(1)} %get-tuple-element.256), channel_id=1, source_target_pairs={{0,6},{1,7},{2,0},{3,1},{4,2},{5,3},{6,4},{7,5},{8,14},{9,15},{10,... | collective-permute-start | bytes 638984 | tf_op jit(solution)/shard_map/ppermute | solution.py:63
  396.9 27.5 %collective-permute-start.130 = (bf16[64,1664]{1,0:T(8,128)(2,1)}, bf16[64,1664]{1,0:T(8,128)(2,1)S(1)}, u32[]{:S(2)}, u32[]{:S(2)}) collective-permute-start(bf16[64,1664]{1,0:T(8,128)(2,1)} %get-tuple-element.251), channel_id=1, source_target_pairs={{0,4},{1,5},{2,6},{3,7},{4,0},{5,1},{6,2},{7,3},{8,12},{9,13},{10,... | collective-permute-start | bytes 638984 | tf_op jit(solution)/shard_map/ppermute | solution.py:63
  397.6 27.5 %collective-permute-start.131 = (bf16[64,1664]{1,0:T(8,128)(2,1)}, bf16[64,1664]{1,0:T(8,128)(2,1)}, u32[]{:S(2)}, u32[]{:S(2)}) collective-permute-start(bf16[64,1664]{1,0:T(8,128)(2,1)} %get-tuple-element.250), channel_id=1, source_target_pairs={{0,2},{1,3},{2,4},{3,5},{4,6},{5,7},{6,0},{7,1},{8,10},{9,11},{10,... | collective-permute-start | bytes 638984 | tf_op jit(solution)/shard_map/ppermute | solution.py:63
  398.8 38.3 %collective-permute-start.98 = (bf16[64,1664]{1,0:T(8,128)(2,1)}, bf16[64,1664]{1,0:T(8,128)(2,1)S(1)}, u32[]{:S(2)}, u32[]{:S(2)}) collective-permute-start(bf16[64,1664]{1,0:T(8,128)(2,1)} %get-tuple-element.244), channel_id=1, source_target_pairs={{0,6},{1,7},{2,0},{3,1},{4,2},{5,3},{6,4},{7,5},{8,14},{9,15},{10,... | collective-permute-start | bytes 638984 | tf_op jit(solution)/shard_map/ppermute | solution.py:63
  401.9 35.2 %collective-permute-start.99 = (bf16[64,1664]{1,0:T(8,128)(2,1)}, bf16[64,1664]{1,0:T(8,128)(2,1)S(1)}, u32[]{:S(2)}, u32[]{:S(2)}) collective-permute-start(bf16[64,1664]{1,0:T(8,128)(2,1)} %get-tuple-element.243), channel_id=1, source_target_pairs={{0,4},{1,5},{2,6},{3,7},{4,0},{5,1},{6,2},{7,3},{8,12},{9,13},{10,... | collective-permute-start | bytes 638984 | tf_op jit(solution)/shard_map/ppermute | solution.py:63
  406.9 30.2 %collective-permute-start.100 = (bf16[64,1664]{1,0:T(8,128)(2,1)}, bf16[64,1664]{1,0:T(8,128)(2,1)}, u32[]{:S(2)}, u32[]{:S(2)}) collective-permute-start(bf16[64,1664]{1,0:T(8,128)(2,1)} %get-tuple-element.242), channel_id=1, source_target_pairs={{0,2},{1,3},{2,4},{3,5},{4,6},{5,7},{6,0},{7,1},{8,10},{9,11},{10,... | collective-permute-start | bytes 638984 | tf_op jit(solution)/shard_map/ppermute | solution.py:63
  437.1 24.1 %collective-permute-start.132 = (bf16[256,512]{1,0:T(8,128)(2,1)}, bf16[256,512]{1,0:T(8,128)(2,1)}, u32[]{:S(2)}, u32[]{:S(2)}) collective-permute-start(bf16[256,512]{1,0:T(8,128)(2,1)} %get-tuple-element.162), channel_id=1, source_target_pairs={{0,1},{1,0},{2,3},{3,2},{4,5},{5,4},{6,7},{7,6},{8,9},{9,8},{10,11... | collective-permute-start | bytes 786440 | tf_op jit(solution)/shard_map/ppermute | solution.py:59
  446.3 39.5 %collective-permute-start.101 = (bf16[256,512]{1,0:T(8,128)(2,1)}, bf16[256,512]{1,0:T(8,128)(2,1)}, u32[]{:S(2)}, u32[]{:S(2)}) collective-permute-start(bf16[256,512]{1,0:T(8,128)(2,1)} %get-tuple-element.140), channel_id=1, source_target_pairs={{0,1},{1,0},{2,3},{3,2},{4,5},{5,4},{6,7},{7,6},{8,9},{9,8},{10,11... | collective-permute-start | bytes 786440 | tf_op jit(solution)/shard_map/ppermute | solution.py:59
  448.3 109.9 %all-to-all-start = ((bf16[8,128,768]{2,1,0:T(8,128)(2,1)}), bf16[8,128,768]{2,1,0:T(8,128)(2,1)S(1)}, u32[]{:S(2)}, u32[]{:S(2)}) async-start(bf16[8,128,768]{2,1,0:T(8,128)(2,1)} %fusion.23), calls=%async_computation | async-start | bytes 3145728 | tf_op jit(solution)/shard_map/all_to_all | solution.py:574
  455.0 25.6 %collective-permute-start.150 = (bf16[64,1536]{1,0:T(8,128)(2,1)}, bf16[64,1536]{1,0:T(8,128)(2,1)S(1)}, u32[]{:S(2)}, u32[]{:S(2)}) collective-permute-start(bf16[64,1536]{1,0:T(8,128)(2,1)} %copy-done.157), channel_id=1, source_target_pairs={{0,2},{1,3},{2,4},{3,5},{4,6},{5,7},{6,0},{7,1},{8,10},{9,11},{10,... | collective-permute-start | bytes 589832 | tf_op jit(solution)/shard_map/ppermute | solution.py:63
  457.1 28.5 %collective-permute-start.151 = (bf16[64,1536]{1,0:T(8,128)(2,1)}, bf16[64,1536]{1,0:T(8,128)(2,1)S(1)}, u32[]{:S(2)}, u32[]{:S(2)}) collective-permute-start(bf16[64,1536]{1,0:T(8,128)(2,1)} %copy-done.157), channel_id=1, source_target_pairs={{0,4},{1,5},{2,6},{3,7},{4,0},{5,1},{6,2},{7,3},{8,12},{9,13},{10,... | collective-permute-start | bytes 589832 | tf_op jit(solution)/shard_map/ppermute | solution.py:63
  459.7 25.9 %collective-permute-start.152 = (bf16[64,1536]{1,0:T(8,128)(2,1)}, bf16[64,1536]{1,0:T(8,128)(2,1)S(1)}, u32[]{:S(2)}, u32[]{:S(2)}) collective-permute-start(bf16[64,1536]{1,0:T(8,128)(2,1)} %copy-done.157), channel_id=1, source_target_pairs={{0,6},{1,7},{2,0},{3,1},{4,2},{5,3},{6,4},{7,5},{8,14},{9,15},{10,... | collective-permute-start | bytes 589832 | tf_op jit(solution)/shard_map/ppermute | solution.py:63
  461.2 24.5 %collective-permute-start.153 = (bf16[64,1536]{1,0:T(8,128)(2,1)}, bf16[64,1536]{1,0:T(8,128)(2,1)S(1)}, u32[]{:S(2)}, u32[]{:S(2)}) collective-permute-start(bf16[64,1536]{1,0:T(8,128)(2,1)} %copy-done.157), channel_id=1, source_target_pairs={{0,1},{1,0},{2,3},{3,2},{4,5},{5,4},{6,7},{7,6},{8,9},{9,8},{10,11... | collective-permute-start | bytes 589832 | tf_op jit(solution)/shard_map/ppermute | solution.py:59
  512.5 18.3 %collective-permute-start.136 = (bf16[80,2176]{1,0:T(8,128)(2,1)S(1)}, bf16[80,2176]{1,0:T(8,128)(2,1)S(1)}, u32[]{:S(2)}, u32[]{:S(2)}) collective-permute-start(bf16[80,2176]{1,0:T(8,128)(2,1)S(1)} %get-tuple-element.172.refs_2_), channel_id=1, source_target_pairs={{0,2},{1,3},{2,4},{3,5},{4,6},{5,7},{6,0},{7,1},{8,10},{9,11},{10,... | collective-permute-start | bytes 1044488 | tf_op jit(solution)/shard_map/ppermute | solution.py:63
  513.5 18.6 %collective-permute-start.137 = (bf16[80,2176]{1,0:T(8,128)(2,1)S(1)}, bf16[80,2176]{1,0:T(8,128)(2,1)}, u32[]{:S(2)}, u32[]{:S(2)}) collective-permute-start(bf16[80,2176]{1,0:T(8,128)(2,1)S(1)} %get-tuple-element.172.refs_2_), channel_id=1, source_target_pairs={{0,4},{1,5},{2,6},{3,7},{4,0},{5,1},{6,2},{7,3},{8,12},{9,13},{10,... | collective-permute-start | bytes 1044488 | tf_op jit(solution)/shard_map/ppermute | solution.py:63
  515.5 17.8 %collective-permute-start.138 = (bf16[80,2176]{1,0:T(8,128)(2,1)S(1)}, bf16[80,2176]{1,0:T(8,128)(2,1)}, u32[]{:S(2)}, u32[]{:S(2)}) collective-permute-start(bf16[80,2176]{1,0:T(8,128)(2,1)S(1)} %get-tuple-element.172.refs_2_), channel_id=1, source_target_pairs={{0,6},{1,7},{2,0},{3,1},{4,2},{5,3},{6,4},{7,5},{8,14},{9,15},{10,... | collective-permute-start | bytes 1044488 | tf_op jit(solution)/shard_map/ppermute | solution.py:63
  522.1 24.1 %collective-permute-start.143 = (bf16[80,2176]{1,0:T(8,128)(2,1)S(1)}, bf16[80,2176]{1,0:T(8,128)(2,1)S(1)}, u32[]{:S(2)}, u32[]{:S(2)}) collective-permute-start(bf16[80,2176]{1,0:T(8,128)(2,1)S(1)} %get-tuple-element.173.refs_10_), channel_id=1, source_target_pairs={{0,2},{1,3},{2,4},{3,5},{4,6},{5,7},{6,0},{7,1},{8,10},{9,11},{10,... | collective-permute-start | bytes 1044488 | tf_op jit(solution)/shard_map/ppermute | solution.py:63
  586.1 26.8 %all-to-all-start.1 = ((bf16[8,192,512]{2,1,0:T(8,128)(2,1)}), bf16[8,192,512]{2,1,0:T(8,128)(2,1)}, u32[]{:S(2)}, u32[]{:S(2)}) async-start(bf16[8,192,512]{2,1,0:T(8,128)(2,1)} %pad_maximum_fusion.2), calls=%async_computation.1 | async-start | bytes 3145728 | tf_op jit(solution)/shard_map/all_to_all | solution.py:588
  612.8 85.4 %all-to-all-start.2 = ((bf16[8,288,1536]{2,1,0:T(8,128)(2,1)}), bf16[8,288,1536]{2,1,0:T(8,128)(2,1)}, u32[]{:S(2)}, u32[]{:S(2)}) async-start(bf16[8,288,1536]{2,1,0:T(8,128)(2,1)} %pad_maximum_fusion), calls=%async_computation.2 | async-start | bytes 14155776 | tf_op jit(solution)/shard_map/all_to_all | solution.py:564
  (381 other events, 5010.7 us)
Sparse Core Ops, SparseCore 0:
  10.4 45.0 all-gather.3
  57.2 37.1 all-gather.5

commit v2 on v1

v2 whole, which is shorter than its diff:
```python
import jax
import jax.numpy as jnp
from jax import lax
from jax.experimental import pallas as pl
from jax.experimental.pallas import tpu as pltpu
from jax.sharding import PartitionSpec as P

D = 1536
T = 64
R = 2 * T
C = 4 * T
HEADS = 12
KV_HEADS = 2
GROUP = HEADS // KV_HEADS
HS = 128
KW = KV_HEADS * HS
SLICE = D // 8
FF = 768
SEQ = 512
N_EXPERTS = 8
LANES = 128
EPS = 1e-06
ROPE_BASE = 1000000.0
SCALE = HS**-0.5
BF = jnp.bfloat16
VMEM = 24 * 2**20
F32 = jnp.float32

NN = (((1,), (0,)), ((), ()))
NT = (((1,), (1,)), ((), ()))
TN = (((0,), (0,)), ((), ()))


def mm(a, b, dims=NN):
    return lax.dot_general(a, b, dims, preferred_element_type=F32)


def sds(shape, dtype):
    return jax.ShapeDtypeStruct(shape, dtype)


def whole(shape):
    return pl.BlockSpec(shape, lambda *_: (0,) * len(shape))


def call(kernel, name, grid, in_specs, out_specs, out_shape, scratch, flops, nbytes, *args):
    return pl.pallas_call(
        kernel,
        name=name,
        grid=grid,
        in_specs=in_specs,
        out_specs=out_specs,
        out_shape=out_shape,
        scratch_shapes=scratch,
        compiler_params=pltpu.CompilerParams(
            dimension_semantics=("arbitrary",) * len(grid), vmem_limit_bytes=VMEM
        ),
        cost_estimate=pl.CostEstimate(flops=flops, bytes_accessed=nbytes, transcendentals=0),
    )(*args)


def swap(x):
    return lax.ppermute(x, "shard", [(i, i ^ 1) for i in range(8)])


def along_y(x, k):
    return lax.ppermute(x, "shard", [(i, (i + 2 * k) % 8) for i in range(8)])


def from_chips(x):
    return [x, along_y(x, 1), along_y(x, 2), along_y(x, 3)]


def to_chips(blocks):
    return [blocks[0]] + [along_y(blocks[k], -k) for k in (1, 2, 3)]


def gather_blocks(x):
    same = from_chips(x)
    return same + [swap(b) for b in same]


def z_near(x):
    return lax.ppermute(x, "rep", [(i, (i // 2 ^ 1) * 2 + i % 2) for i in range(8)])


def z_far(x):
    return lax.ppermute(x, "rep", [(i, (3 - i // 2) * 2 + i % 2) for i in range(8)])


def x_pair(x):
    return lax.ppermute(x, "rep", [(i, i ^ 1) for i in range(8)])


def plus(a, b):
    return (a.astype(F32) + b.astype(F32)).astype(BF)


def rope(x, cos, sin):
    return x * cos + pltpu.roll(x, HS // 2, 1) * sin


def rope_back(x, cos, sin):
    return x * cos - pltpu.roll(x, HS // 2, 1) * sin


def qkv_kernel(x0_ref, x1_ref, gain_ref, w_ref, cos_ref, sin_ref, q_ref, kv_ref, h_ref):
    j = pl.program_id(0)

    @pl.when(j == 0)
    def _():
        for m, x_ref in enumerate((x0_ref, x1_ref)):
            x = x_ref[...].astype(F32)
            r = lax.rsqrt(jnp.mean(x * x, axis=-1, keepdims=True) + EPS)
            h_ref[m * T : (m + 1) * T, :] = (x * r * gain_ref[0:1, :]).astype(BF)

    y = mm(h_ref[...], w_ref[...])
    cos, sin = cos_ref[...], sin_ref[...]

    @pl.when(j < 3)
    def _():
        for i in range(4):
            at = slice(i * HS, (i + 1) * HS)
            q_ref[:, at] = rope(y[:, at], cos, sin).astype(BF)

    @pl.when(j == 3)
    def _():
        for i in range(2):
            at = slice(i * HS, (i + 1) * HS)
            kv_ref[:, at] = rope(y[:, at], cos, sin).astype(BF)
        kv_ref[:, KW:] = y[:, KW:].astype(BF)


def qkv(x0, x1, gains, w, cos, sin):
    return call(
        qkv_kernel, "qkv", (4,),
        [whole((T, D)), whole((T, D)), whole((8, D)), pl.BlockSpec((D, 512), lambda j: (0, j)), whole((R, HS)), whole((R, HS))],
        [pl.BlockSpec((R, 512), lambda j: (0, jnp.minimum(j, 2))), whole((R, 512)), whole((R, D))],
        [sds((R, D), BF), sds((R, 512), BF), sds((R, D), BF)],
        [], 2 * R * D * 2048, 7 * 10**6,
        x0, x1, gains, w, cos, sin,
    )


def stack_keys(kv_refs, kv_s):
    for m in range(2):
        for i, b in enumerate(kv_refs):
            kv_s[m, i * T : (i + 1) * T, :] = b[m * T : (m + 1) * T, :]


def heads_of(ref, m, k):
    rows = slice(m * T, (m + 1) * T)
    return jnp.concatenate([ref[rows, h * HS : (h + 1) * HS] for h in range(k * GROUP, (k + 1) * GROUP)], axis=0)


def probs_of(q6, keys, allowed):
    s = mm(q6, keys, NT) * SCALE
    s = jnp.where(allowed[None] > 0, s.reshape(GROUP, T, SEQ), -1e30)
    e = jnp.exp(s - jnp.max(s, axis=-1, keepdims=True))
    p = e * (1.0 / jnp.sum(e, axis=-1, keepdims=True))
    return p.reshape(GROUP * T, SEQ)


def attend_kernel(save, *refs):
    q_ref, kv_refs, rest = refs[0], refs[1:9], refs[9:]
    allowed_ref, x0_ref, x1_ref, w_ref, gain_ref, wr_ref, chosen_ref = rest[:7]
    if save:
        h_ref, att_ref, mid_ref, hm0_ref, hm1_ref, left_ref, kv_s, mid_s = rest[7:]
    else:
        att_ref, mid_ref, hm0_ref, hm1_ref, kv_s, mid_s = rest[7:]
    j = pl.program_id(0)

    @pl.when(j == 0)
    def _():
        stack_keys(kv_refs, kv_s)
        allowed = allowed_ref[...]
        for m in range(2):
            for k in range(KV_HEADS):
                p = probs_of(heads_of(q_ref, m, k), kv_s[m, :, k * HS : (k + 1) * HS], allowed).astype(BF)
                o = mm(p, kv_s[m, :, KW + k * HS : KW + (k + 1) * HS])
                for g in range(GROUP):
                    h = k * GROUP + g
                    att_ref[m * T : (m + 1) * T, h * HS : (h + 1) * HS] = o[g * T : (g + 1) * T].astype(BF)

    mid_s[j] = mm(att_ref[...], w_ref[...])

    @pl.when(j == 2)
    def _():
        for m, (x_ref, hm_ref) in enumerate(((x0_ref, hm0_ref), (x1_ref, hm1_ref))):
            rows = slice(m * T, (m + 1) * T)
            mids = [x_ref[:, i * 512 : (i + 1) * 512].astype(F32) + mid_s[i, rows] for i in range(3)]
            square = sum(jnp.sum(v * v, axis=-1, keepdims=True) for v in mids)
            r = lax.rsqrt(square * (1.0 / D) + EPS)
            logits = jnp.zeros((T, LANES), F32)
            for i in range(3):
                at = slice(i * 512, (i + 1) * 512)
                mid_ref[rows, at] = mids[i]
                h = (mids[i] * r * gain_ref[1:2, at]).astype(BF)
                hm_ref[:, at] = h
                logits = logits + mm(h, wr_ref[at, :])
            chosen = chosen_ref[rows, :] > 0
            top = jnp.max(jnp.where(chosen, logits, -jnp.inf), axis=-1, keepdims=True)
            e = jnp.where(chosen, jnp.exp(jnp.minimum(logits - top, 0.0)), 0.0)
            gate = e / jnp.sum(e, axis=-1, keepdims=True)
            high = gate.astype(BF).astype(F32)
            hm_ref[:, D:] = (high + pltpu.roll(gate - high, N_EXPERTS, 1)).astype(BF)
            if save:
                for a in range(3):
                    for i in range(8):
                        cut = slice(i * SLICE, (i + 1) * SLICE)
                        rows_of = hm_ref[:, cut] if a == 2 else (h_ref, att_ref)[a][rows, cut]
                        left_ref[i, rows, a * 256 : a * 256 + SLICE] = rows_of
                        left_ref[i, rows, a * 256 + SLICE : (a + 1) * 256] = jnp.zeros((T, 256 - SLICE), BF)


def attend(q, kvs, allowed, x0, x1, w, gains, chosen, h_attn, save):
    more = [h_attn] if save else []
    return call(
        lambda *refs: attend_kernel(save, *refs), "attend", (3,),
        [whole((R, D))] + [whole((R, 512))] * 8
        + [whole((T, SEQ)), whole((T, D)), whole((T, D)), pl.BlockSpec((D, 512), lambda j: (0, 4 + j)), whole((8, D)),
           pl.BlockSpec((D, LANES), lambda j: (0, 28)), whole((R, LANES))]
        + [whole((R, D)) for _ in more],
        [whole((R, D)), whole((R, D)), whole((T, D + LANES)), whole((T, D + LANES))] + [whole((8, R, 768)) for _ in more],
        [sds((R, D), BF), sds((R, D), F32), sds((T, D + LANES), BF), sds((T, D + LANES), BF)] + [sds((8, R, 768), BF) for _ in more],
        [pltpu.VMEM((2, SEQ, 512), BF), pltpu.VMEM((3, R, 512), F32)],
        2 * R * D * D + 4 * R * D * SEQ, 8 * 10**6,
        q, *kvs, allowed, x0, x1, w, gains, w, chosen, *more,
    )


FW = D + FF
GW = 2 * D


def expert_kernel(save, *refs):
    hm_refs, (mine_ref, wg_ref, wu_ref, wd_ref), outs, rest = refs[:4], refs[4:8], refs[8:12], refs[12:]
    if save:
        f_refs, (g_ref, gate_ref, up_ref, prod_ref, acc, total) = rest[:2], rest[2:]
        h_ref = f_refs[0]
    else:
        h_ref, g_ref, acc, total = rest
    j = pl.program_id(0)

    @pl.when(j == 0)
    def _():
        for i, b in enumerate(hm_refs):
            at = slice(i * T, (i + 1) * T)
            h_ref[at, :D] = b[:, :D]
            lanes = b[:, D:].astype(F32)
            for e in range(2):
                g = jnp.sum(lanes * mine_ref[e : e + 1, :], axis=-1, keepdims=True)
                g_ref[e, at, :] = jnp.broadcast_to(g, (T, LANES))
        if save:
            f_refs[1][:, :D] = f_refs[0][:, :D]

    h = h_ref[:, :D]
    gate = mm(h, wg_ref[0])
    up = mm(h, wu_ref[0])
    act = (gate / (1.0 + jnp.exp(-gate)) * up).astype(BF)
    if save:
        gate_ref[0] = gate
        up_ref[0] = up
        for step in range(6):

            @pl.when(j == step)
            def _(step=step):
                at = D + (step % 3) * 256
                f_refs[step // 3][:, at : at + 256] = act

    add = mm(act, wd_ref[0])

    @pl.when(j % 3 == 0)
    def _():
        acc[...] = add

    @pl.when(j % 3 > 0)
    def _():
        acc[...] += add

    @pl.when(j == 2)
    def _():
        prod = acc[...].astype(BF)
        if save:
            prod_ref[0] = prod
        total[...] = prod.astype(F32) * g_ref[0, :, 0:1]

    @pl.when(j == 5)
    def _():
        prod = acc[...].astype(BF)
        if save:
            prod_ref[1] = prod
        part = (total[...] + prod.astype(F32) * g_ref[1, :, 0:1]).astype(BF)
        for i, o in enumerate(outs):
            o[...] = part[i * T : (i + 1) * T]


def expert(hms, mine, w_in, w_down, save):
    f_block = pl.BlockSpec((1, C, 256), lambda j: (j // 3, 0, j % 3))
    out_specs = [whole((T, D))] * 4
    out_shape = [sds((T, D), BF)] * 4
    scratch = [pltpu.VMEM((C, D), F32), pltpu.VMEM((C, D), F32)]
    if save:
        out_specs += [whole((C, FW)), whole((C, FW)), whole((2, C, LANES)), f_block, f_block, whole((2, C, D))]
        out_shape += [sds((C, FW), BF), sds((C, FW), BF), sds((2, C, LANES), F32), sds((2, C, FF), F32), sds((2, C, FF), F32), sds((2, C, D), BF)]
    else:
        scratch = [pltpu.VMEM((C, D), BF), pltpu.VMEM((2, C, LANES), F32)] + scratch
    return call(
        lambda *refs: expert_kernel(save, *refs), "expert", (6,),
        [whole((T, D + LANES))] * 4
        + [whole((8, LANES)), pl.BlockSpec((1, D, 256), lambda j: (j // 3, 0, j % 3)), pl.BlockSpec((1, D, 256), lambda j: (j // 3, 0, j % 3 + 3)),
           pl.BlockSpec((1, 256, D), lambda j: (j // 3, j % 3, 0))],
        out_specs, out_shape, scratch, 12 * C * D * FF, 18 * 10**6,
        *hms, mine, w_in, w_in, w_down,
    )


def expert_back_kernel(save, *refs):
    gs, (g_ref, gate_ref, up_ref, prod_ref, put_ref, wd_ref, wg_ref, wu_ref), outs, rest = refs[:4], refs[4:12], refs[12:16], refs[16:]
    if save:
        d_refs, (lanes_s, dprod, acc, total) = rest[:2], rest[2:]
    else:
        lanes_s, dprod, acc, total = rest
    j = pl.program_id(0)

    for e in range(2):

        @pl.when(j == 3 * e)
        def _(e=e):
            put = put_ref[...]
            for i, b in enumerate(gs):
                at = slice(i * T, (i + 1) * T)
                g = b[...].astype(F32)
                d_prod = (g * g_ref[e, at, 0:1]).astype(BF)
                dprod[at, :] = d_prod
                if save:
                    d_refs[e][at, D:] = d_prod
                d = jnp.sum(g * prod_ref[e, at, :].astype(F32), axis=-1, keepdims=True)
                high = d.astype(BF).astype(F32)
                lanes = high * put[2 * e : 2 * e + 1, :] + (d - high) * put[2 * e + 1 : 2 * e + 2, :]
                lanes_s[at, :] = lanes if e == 0 else lanes_s[at, :] + lanes

    d_act = mm(dprod[...], wd_ref[0], NT)
    gate, up = gate_ref[0], up_ref[0]
    s = 1.0 / (1.0 + jnp.exp(-gate))
    dg = (d_act * up * (s * (1.0 + gate * (1.0 - s)))).astype(BF)
    du = (d_act * (gate * s)).astype(BF)
    if save:
        for step in range(6):

            @pl.when(j == step)
            def _(step=step):
                at = (step % 3) * 256
                d_refs[step // 3][:, at : at + 256] = dg
                d_refs[step // 3][:, FF + at : FF + at + 256] = du

    add = mm(dg, wg_ref[0], NT) + mm(du, wu_ref[0], NT)

    @pl.when(j % 3 == 0)
    def _():
        acc[...] = add

    @pl.when(j % 3 > 0)
    def _():
        acc[...] += add

    @pl.when(j == 2)
    def _():
        total[...] = acc[...].astype(BF).astype(F32)

    @pl.when(j == 5)
    def _():
        part = (total[...] + acc[...].astype(BF).astype(F32)).astype(BF)
        for i, o in enumerate(outs):
            at = slice(i * T, (i + 1) * T)
            o[:, :D] = part[at]
            o[:, D:] = lanes_s[at, :].astype(BF)


def expert_back(gs, kept, put, w_in, w_down, save):
    g_share, gate, up, produced = kept
    f_block = pl.BlockSpec((1, C, 256), lambda j: (j // 3, 0, j % 3))
    out_specs = [whole((T, D + LANES))] * 4
    out_shape = [sds((T, D + LANES), BF)] * 4
    if save:
        out_specs += [whole((C, GW))] * 2
        out_shape += [sds((C, GW), BF)] * 2
    return call(
        lambda *refs: expert_back_kernel(save, *refs), "expert_back", (6,),
        [whole((T, D))] * 4
        + [whole((2, C, LANES)), f_block, f_block, whole((2, C, D)), whole((8, LANES)),
           pl.BlockSpec((1, 256, D), lambda j: (j // 3, j % 3, 0)), pl.BlockSpec((1, D, 256), lambda j: (j // 3, 0, j % 3)),
           pl.BlockSpec((1, D, 256), lambda j: (j // 3, 0, j % 3 + 3))],
        out_specs, out_shape,
        [pltpu.VMEM((C, LANES), F32), pltpu.VMEM((C, D), BF), pltpu.VMEM((C, D), F32), pltpu.VMEM((C, D), F32)],
        12 * C * D * FF, 20 * 10**6,
        *gs, g_share, gate, up, produced, put, w_down, w_in, w_in,
    )


def norm_back(x, gain, grad):
    r = lax.rsqrt(jnp.mean(x * x, axis=-1, keepdims=True) + EPS)
    n = x * r
    scaled = grad * gain
    back = r * (scaled - n * jnp.mean(scaled * n, axis=-1, keepdims=True))
    return jnp.sum(grad * n, axis=0, keepdims=True), back


def attend_back_kernel(*refs):
    rets, g_refs, mid_ref, hm_refs, rest = refs[:8], refs[8:10], refs[10], refs[11:13], refs[13:]
    gain_ref, wr_ref, w0_ref, w1_ref, w2_ref, q_ref = rest[:6]
    kv_refs, rest = rest[6:14], rest[14:]
    allowed_ref, cos_ref, sin_ref, dmid_ref, datt_ref, dq_ref, same_ref, other_ref, dl_ref, gain_out, da, kv_s, kv_acc = rest
    j = pl.program_id(0)

    @pl.when(j == 0)
    def _():
        grads = jnp.zeros((1, D), F32)
        for m in range(2):
            rows = slice(m * T, (m + 1) * T)
            total = sum(r[...].astype(F32) for r in rets[4 * m : 4 * m + 4])
            lanes = total[:, D:]
            d_gate = lanes + pltpu.roll(lanes, LANES - N_EXPERTS, 1)
            share = hm_refs[m][:, D:].astype(F32)
            gate = share + pltpu.roll(share, LANES - N_EXPERTS, 1)
            gate = jnp.where(lax.broadcasted_iota(jnp.int32, (T, LANES), 1) < N_EXPERTS, gate, 0.0)
            inner = jnp.sum(gate * d_gate, axis=-1, keepdims=True)
            d_logits = (gate * (d_gate - inner)).astype(BF)
            dl_ref[rows, :] = d_logits
            d_hm = total[:, :D] + mm(d_logits, wr_ref[...], NT)
            grad_gain, back = norm_back(mid_ref[rows, :], gain_ref[1:2, :], d_hm)
            grads = grads + grad_gain
            d_mid = g_refs[m][...].astype(F32) + back
            dmid_ref[rows, :] = d_mid
            datt_ref[rows, :] = d_mid.astype(BF)
        gain_out[...] = jnp.broadcast_to(grads, (8, D))
        stack_keys(kv_refs, kv_s)

    piece = mm(datt_ref[:, 0:512], w0_ref[...], NT) + mm(datt_ref[:, 512:1024], w1_ref[...], NT) + mm(datt_ref[:, 1024:], w2_ref[...], NT)
    piece = piece.astype(BF)
    for m in range(2):
        for i in range(3):
            da[m, j * 3 + i] = piece[m * T : (m + 1) * T, i * HS : (i + 1) * HS]

    @pl.when(j == 3)
    def _():
        allowed = allowed_ref[...]
        cos, sin = cos_ref[:T, :], sin_ref[:T, :]
        for m in range(2):
            rows = slice(m * T, (m + 1) * T)
            for k in range(KV_HEADS):
                keys = kv_s[m, :, k * HS : (k + 1) * HS]
                values = kv_s[m, :, KW + k * HS : KW + (k + 1) * HS]
                q6 = heads_of(q_ref, m, k)
                d6 = da[m, k * GROUP : (k + 1) * GROUP].reshape(GROUP * T, HS)
                p = probs_of(q6, keys, allowed)
                dp = mm(d6, values, NT)
                ds = (p * (dp - jnp.sum(p * dp, axis=-1, keepdims=True)) * SCALE).astype(BF)
                dq = mm(ds, keys)
                for g in range(GROUP):
                    h = k * GROUP + g
                    dq_ref[rows, h * HS : (h + 1) * HS] = rope_back(dq[g * T : (g + 1) * T], cos, sin).astype(BF)
                kv_acc[:, k * HS : (k + 1) * HS] = mm(ds, q6, TN)
                kv_acc[:, KW + k * HS : KW + (k + 1) * HS] = mm(p.astype(BF), d6, TN)
            for i in range(4):
                at = slice(i * R + m * T, i * R + (m + 1) * T)
                same_ref[at, :] = kv_acc[i * T : (i + 1) * T].astype(BF)
                other_ref[at, :] = kv_acc[C + i * T : C + (i + 1) * T].astype(BF)


def attend_back(rets, gs, mid, hms, gains, w, q, kvs, allowed, cos, sin):
    return call(
        attend_back_kernel, "attend_back", (4,),
        [whole((T, D + LANES))] * 8 + [whole((T, D))] * 2 + [whole((R, D))] + [whole((T, D + LANES))] * 2
        + [whole((8, D)), pl.BlockSpec((D, LANES), lambda j: (0, 28))]
        + [pl.BlockSpec((384, 512), lambda j, c=c: (j, 4 + c)) for c in range(3)]
        + [whole((R, D))] + [whole((R, 512))] * 8 + [whole((T, SEQ)), whole((R, HS)), whole((R, HS))],
        [whole((R, D)), whole((R, D)), whole((R, D)), whole((4 * R, 512)), whole((4 * R, 512)), whole((R, LANES)), whole((8, D))],
        [sds((R, D), F32), sds((R, D), BF), sds((R, D), BF), sds((4 * R, 512), BF), sds((4 * R, 512), BF), sds((R, LANES), BF), sds((8, D), F32)],
        [pltpu.VMEM((2, HEADS, T, HS), BF), pltpu.VMEM((2, SEQ, 512), BF), pltpu.VMEM((SEQ, 512), F32)],
        2 * R * D * D + 10 * R * D * SEQ, 8 * 10**6,
        *rets, *gs, mid, *hms, gains, w, w, w, w, q, *kvs, allowed, cos, sin,
    )


MSG = 512 + LANES


def qkv_back_kernel(*refs):
    rets, (dq_ref, dl_ref, gm_ref, x0_ref, x1_ref, gain_ref, w_ref, cos_ref, sin_ref, dmid_ref), rest = refs[:4], refs[4:14], refs[14:]
    gin_ref, low0_ref, low1_ref, msg_ref, dh = rest
    j = pl.program_id(0)

    @pl.when(j == 0)
    def _():
        d_kv = sum(r[...].astype(F32) for r in rets)
        cos, sin = cos_ref[...], sin_ref[...]
        for i in range(KV_HEADS):
            at = slice(i * HS, (i + 1) * HS)
            msg_ref[:R, at] = rope_back(d_kv[:, at], cos, sin).astype(BF)
        msg_ref[:R, KW:512] = d_kv[:, KW:].astype(BF)
        msg_ref[:R, 512:] = dl_ref[...]

    dh[j] = mm(dq_ref[...], w_ref[:, :D], NT) + mm(msg_ref[:R, :512], w_ref[:, D:], NT)

    @pl.when(j == 3)
    def _():
        d_h = jnp.concatenate([dh[i] for i in range(4)], axis=1)
        grads = jnp.zeros((1, D), F32)
        for m, (x_ref, low_ref) in enumerate(((x0_ref, low0_ref), (x1_ref, low1_ref))):
            rows = slice(m * T, (m + 1) * T)
            grad_gain, back = norm_back(x_ref[...].astype(F32), gain_ref[0:1, :], d_h[rows])
            grads = grads + grad_gain
            g_in = dmid_ref[rows, :] + back
            gin_ref[rows, :] = g_in
            low_ref[...] = g_in.astype(BF)
        for c in range(3):
            at = slice(c * 512, (c + 1) * 512)
            row = lax.broadcasted_iota(jnp.int32, (16, 512), 0)
            both = jnp.where(row == c, jnp.broadcast_to(grads[:, at], (16, 512)), 0.0)
            both = both + jnp.where(row == 3 + c, jnp.broadcast_to(gm_ref[0:1, at], (16, 512)), 0.0)
            msg_ref[R:, :512] = both.astype(BF) if c == 0 else msg_ref[R:, :512] + both.astype(BF)
        msg_ref[R:, 512:] = jnp.zeros((16, LANES), BF)


def qkv_back(rets, dq, dl, gm, x0, x1, gains, w, cos, sin, d_mid):
    return call(
        qkv_back_kernel, "qkv_back", (4,),
        [whole((R, 512))] * 4
        + [whole((R, D)), whole((R, LANES)), whole((8, D)), whole((T, D)), whole((T, D)), whole((8, D)), pl.BlockSpec((384, 2048), lambda j: (j, 0)),
           whole((R, HS)), whole((R, HS)), whole((R, D))],
        [whole((R, D)), whole((T, D)), whole((T, D)), whole((R + 16, MSG))],
        [sds((R, D), F32), sds((T, D), BF), sds((T, D), BF), sds((R + 16, MSG), BF)],
        [pltpu.VMEM((4, R, 384), F32)],
        2 * R * D * 2048, 9 * 10**6,
        *rets, dq, dl, gm, x0, x1, gains, w, cos, sin, d_mid,
    )


def attn_grad_kernel(*refs):
    order_ref, left_ref = refs[0], refs[1]
    msgs, dqs, datts = refs[2:10], refs[10:18], refs[18:26]
    gq_ref, gkv_ref, go_ref, gr_ref, gain_ref = refs[26:31]
    lh, rq, ro, rm = refs[31:35]
    gains = jnp.zeros((16, 512), F32)
    for i in range(8):
        at = slice(i * R, (i + 1) * R)
        lh[at, :] = left_ref[order_ref[i]]
        rq[at, :] = dqs[i][...]
        ro[at, :] = datts[i][...]
        rm[at, :] = msgs[i][:R, :]
        gains = gains + msgs[i][R:, :512].astype(F32)
    gain_ref[...] = gains
    for c in range(3):
        at = slice(c * 512, (c + 1) * 512)
        gq_ref[:, at] = mm(lh[:, :256], rq[:, at], TN)[:SLICE].astype(BF)
        go_ref[:, at] = mm(lh[:, 256:512], ro[:, at], TN)[:SLICE].astype(BF)
    gkv_ref[...] = mm(lh[:, :256], rm[:, :512], TN)[:SLICE].astype(BF)
    gr_ref[...] = mm(lh[:, 512:], rm[:, 512:], TN)[:SLICE]


def attn_grad(order, left, msgs, dqs, datts):
    return pl.pallas_call(
        attn_grad_kernel,
        name="attn_grad",
        grid=(1,),
        in_specs=[pl.BlockSpec(memory_space=pltpu.SMEM)] + [whole(a.shape) for a in (left, *msgs, *dqs, *datts)],
        out_specs=[whole((SLICE, D)), whole((SLICE, 512)), whole((SLICE, D)), whole((SLICE, LANES)), whole((16, 512))],
        out_shape=[sds((SLICE, D), BF), sds((SLICE, 512), BF), sds((SLICE, D), BF), sds((SLICE, LANES), F32), sds((16, 512), F32)],
        scratch_shapes=[pltpu.VMEM((8 * R, 768), BF), pltpu.VMEM((8 * R, D), BF), pltpu.VMEM((8 * R, D), BF), pltpu.VMEM((8 * R, MSG), BF)],
        compiler_params=pltpu.CompilerParams(vmem_limit_bytes=32 * 2**20),
        cost_estimate=pl.CostEstimate(flops=2 * 1024 * 256 * 3584, bytes_accessed=10 * 10**6, transcendentals=0),
    )(order, left, *msgs, *dqs, *datts)


def expert_grad_kernel(part, places, order_ref, *refs):
    lefts, rights, out_ref, turned, result = refs[:4], refs[4:8], refs[8], refs[9], refs[10]
    j = pl.program_id(0)
    rows = out_ref.shape[1]

    @pl.when(j == 0)
    def _():
        for i, left in enumerate(lefts):
            turned[:, i * C : (i + 1) * C] = left[:, part].T

    result[...] = sum(mm(turned[:, i * C : (i + 1) * C], rights[i][...]) for i in range(4))
    for i in range(8):
        out_ref[i] = result[pl.ds(pl.multiple_of(order_ref[i] * rows, rows), rows), :].astype(BF)


def expert_grad(order, lefts, rights, part, first, blocks):
    width = part.stop - part.start
    return pl.pallas_call(
        lambda *refs: expert_grad_kernel(part, None, *refs),
        name="expert_grad",
        grid_spec=pltpu.PrefetchScalarGridSpec(
            num_scalar_prefetch=1,
            grid=(blocks,),
            in_specs=[pl.BlockSpec((C, FW), lambda j, o: (0, 0))] * 4 + [pl.BlockSpec((C, 256), lambda j, o: (0, first + j))] * 4,
            out_specs=pl.BlockSpec((8, width // 8, 256), lambda j, o: (0, 0, j)),
            scratch_shapes=[pltpu.VMEM((width, 4 * C), BF), pltpu.VMEM((width, 256), F32)],
        ),
        out_shape=sds((8, width // 8, 256 * blocks), BF),
        compiler_params=pltpu.CompilerParams(dimension_semantics=("arbitrary",), vmem_limit_bytes=VMEM),
        cost_estimate=pl.CostEstimate(flops=2 * 4 * C * width * 256 * blocks, bytes_accessed=8 * 10**6, transcendentals=0),
    )(order, *lefts, *rights)


def body(tokens_in, cotangent, routes, gain_attn, w_query, w_keyval, w_out, gain_moe, w_router, w_in, w_down):
    is_first = lax.axis_index("section") == 0
    shard = lax.axis_index("shard")
    rep = lax.axis_index("rep")
    chip, core = shard // 2, shard % 2
    micros = range(2)

    extra = jnp.concatenate([w_router[0], gain_attn[0][:, None], gain_moe[0][:, None]], axis=1)
    extra = jnp.pad(extra, ((0, 0), (0, LANES - extra.shape[1])))
    packed = jnp.concatenate([w_query[0], w_keyval[0], w_out[0], extra], axis=1)
    w = lax.all_gather(packed, "shard", axis=0, tiled=True)
    pick = (jnp.arange(LANES)[None, :] == (jnp.arange(8)[:, None] + N_EXPERTS)) & (jnp.arange(8)[:, None] < 2)
    gains = mm(pick.astype(BF), w[:, 3584:], NT)
    inner = jnp.stack([w_in[0, 0], swap(w_in[0, 0])])
    outer = jnp.stack([w_down[0, 0], swap(w_down[0, 0])])

    w, gains, inner, outer = lax.optimization_barrier((w, gains, inner, outer))

    half = HS // 2
    frequency = ROPE_BASE ** (-jnp.arange(half, dtype=F32) * 2.0 / HS)
    place = shard * T + jnp.arange(T, dtype=jnp.int32)
    angles = place.astype(F32)[:, None] * frequency[None, :]
    angles = jnp.concatenate([angles, angles], axis=0)
    cos = jnp.concatenate([jnp.cos(angles)] * 2, axis=1)
    sin = jnp.concatenate([-jnp.sin(angles), jnp.sin(angles)], axis=1)
    order = jnp.stack([((chip - k) % 4) * 2 + c for c in (core, 1 - core) for k in range(4)]).astype(jnp.int32)
    key_place = (order[:, None] * T + jnp.arange(T, dtype=jnp.int32)[None, :]).reshape(1, SEQ)
    allowed = (key_place <= place[:, None]).astype(F32)
    lane = jnp.arange(LANES, dtype=jnp.int32)
    other = shard ^ 1
    mine = jnp.stack([(lane == e) | (lane == e + N_EXPERTS) for e in (shard, other)]).astype(F32)
    mine = jnp.pad(mine, ((0, 6), (0, 0)))
    put = jnp.stack([lane == shard, lane == shard + N_EXPERTS, lane == other, lane == other + N_EXPERTS]).astype(F32)
    put = jnp.pad(put, ((0, 4), (0, 0)))
    chosen = jnp.any(routes[0, :, 0].reshape(R, -1)[:, :, None] == lane[None, None, :], axis=1).astype(F32)

    def layer(x, save):
        q, kv, h_attn = qkv(x[0], x[1], gains, w, cos, sin)
        kvs = gather_blocks(kv)
        att, mid, hm0, hm1, *left = attend(q, kvs, allowed, x[0], x[1], w, gains, chosen, h_attn, save)
        hms = (hm0, hm1)
        y, more = [], []
        for m in micros:
            out = expert(from_chips(hms[m]), mine, inner, outer, save)
            rets = to_chips(out[:4])
            y.append((mid[m * T : (m + 1) * T] + sum(r.astype(F32) for r in rets)).astype(BF))
            more.append(out[4:])
        return y, (x, q, kvs, mid, hms), more, left

    def layer_back(g, kept, more, save, beside):
        x, q, kvs, mid, hms = kept
        rets, saved = [], []
        for m in micros:
            g_share, gate, up, produced = more[m][2:]
            out = expert_back(from_chips(g[m]), (g_share, gate, up, produced), put, inner, outer, save)
            rets += to_chips(out[:4])
            saved.append(out[4:])
        rets, sends = lax.optimization_barrier((rets, beside(saved)))
        d_mid, d_att, dq, kv_same, kv_other, dl, gm = attend_back(rets, g, mid, hms, gains, w, q, kvs, allowed, cos, sin)
        got = swap(kv_other)
        kv_rets = to_chips([plus(kv_same[k * R : (k + 1) * R], got[k * R : (k + 1) * R]) for k in range(4)])
        kv_rets, dq, d_att = lax.optimization_barrier((kv_rets, dq, d_att))
        g_in, low0, low1, msg = qkv_back(kv_rets, dq, dl, gm, x[0], x[1], gains, w, cos, sin, d_mid)
        return g_in, (low0, low1), msg, dq, d_att, sends

    tokens = [tokens_in[m, 0] for m in micros]
    given = [cotangent[m, 0] for m in micros]
    first, *_ = layer(tokens, False)
    arrived = [lax.ppermute(first[m], "section", [(0, 1)]) for m in micros]
    inputs = [jnp.where(is_first, tokens[m], arrived[m]) for m in micros]
    acts, kept, more, left = layer(inputs, True)
    left = lax.all_to_all(left[0], "shard", split_axis=0, concat_axis=0, tiled=True)
    f_own = [more[m][0] for m in micros]
    f_got = [swap(more[m][1]) for m in micros]

    z, x_lo = rep // 2, rep % 2
    rep_order = jnp.stack([zz * 2 + xx for zz in (z, 3 - z, z ^ 1, (3 - z) ^ 1) for xx in (x_lo, 1 - x_lo)]).astype(jnp.int32)

    def weights(saved):
        rights = [saved[m][0] for m in micros] + [swap(saved[m][1]) for m in micros]
        send_in = expert_grad(rep_order, lefts, rights, slice(0, D), 0, 6)
        send_down = expert_grad(rep_order, lefts, rights, slice(D, FW), 6, 6)
        return send_in.reshape(4, 2, SLICE, D), send_down.reshape(4, 2, SLICE // 2, D)

    def reduce_first(sends):
        send_in, send_down = sends
        near = send_in[..., :FF]
        far = send_in[..., FF:]
        near = plus(near[0:2], z_near(near[2:4]))
        got = z_far(jnp.concatenate([far[1:2], far[3:4]], axis=0))
        far = plus(jnp.concatenate([far[0:1], far[2:3]], axis=0), got)
        down = plus(send_down[:, 0], x_pair(send_down[:, 1]))
        return near, far, down

    def reduce_second(sends):
        near, far, down = sends
        near = near[0].astype(F32) + z_far(near[1]).astype(F32)
        far = far[0].astype(F32) + z_near(far[1]).astype(F32)
        down_near, down_far = down[..., :FF], down[..., FF:]
        down_near = plus(down_near[0:2], z_near(down_near[2:4]))
        got = z_far(jnp.concatenate([down_far[1:2], down_far[3:4]], axis=0))
        down_far = plus(jnp.concatenate([down_far[0:1], down_far[2:3]], axis=0), got)
        return near, far, down_near, down_far

    def reduce_third(sends):
        near, far, down_near, down_far = sends
        halves = [v[0] + x_pair(v[1].astype(BF)).astype(F32) for v in (near, far)]
        downs = [
            down_near[0].astype(F32) + z_far(down_near[1]).astype(F32),
            down_far[0].astype(F32) + z_near(down_far[1]).astype(F32),
        ]
        return jnp.concatenate(halves, axis=1), jnp.concatenate(downs, axis=1)

    _, back, *_, (left, f_got) = layer_back(given, kept, more, False, lambda saved: (left, f_got))
    lefts = f_own + f_got
    arrived = [lax.ppermute(back[m], "section", [(1, 0)]) for m in micros]
    given = [jnp.where(is_first, arrived[m], given[m]) for m in micros]
    g_in, _, msg, dq, d_att, sends = layer_back(given, kept, more, True, weights)

    msg, sends = lax.optimization_barrier((msg, reduce_first(sends)))
    msgs, dqs, datts = gather_blocks(msg), gather_blocks(dq), gather_blocks(d_att)
    msgs, sends = lax.optimization_barrier((msgs, reduce_second(sends)))
    grad_in, grad_down = reduce_third(sends)
    gq, gkv, go, gr, gg = attn_grad(order, left, msgs, dqs, datts)
    gg = lax.dynamic_slice(gg[:6].reshape(2, D), (0, shard * SLICE), (2, SLICE))
    small = jnp.concatenate([gr[:, :N_EXPERTS], gg.T], axis=1).astype(BF)
    small = jnp.pad(small, ((0, 0), (0, 64 - small.shape[1])))

    def pieces(rows):
        return rows.reshape(SLICE, 8, -1).transpose(1, 0, 2)

    send = jnp.concatenate([pieces(gq), pieces(gkv), jnp.broadcast_to(small[None], (8, SLICE, 64)), pieces(go)], axis=2)
    got = lax.all_to_all(send, "rep", split_axis=0, concat_axis=0, tiled=True)
    sums = jnp.sum(got.astype(F32), axis=0)
    g_q, g_kv, g_small, g_o = sums[:, :SLICE], sums[:, SLICE : SLICE + 64], sums[:, SLICE + 64 : SLICE + 128], sums[:, SLICE + 128 :]

    return (
        jnp.stack(acts)[None, :, None],
        g_in.reshape(1, 2, 1, T, D),
        g_small[None, :, N_EXPERTS],
        g_q[None],
        g_kv[None],
        g_o[None],
        g_small[None, :, N_EXPERTS + 1],
        g_small[None, :, :N_EXPERTS],
        grad_in[None, None],
        grad_down[None, None],
    )


def solution(mesh):
    in_specs = (
        P(None, "rep", "shard", None),
        P(None, "rep", "shard", None),
        P("section", None, "rep", "shard", None),
        P("section", "shard"),
        P("section", "shard", None),
        P("section", "shard", None),
        P("section", "shard", None),
        P("section", "shard"),
        P("section", "shard", None),
        P("section", "shard", None, None),
        P("section", "shard", None, None),
    )
    out_specs = (
        P("section", None, "rep", "shard", None),
        P("section", None, "rep", "shard", None),
        P("section", "shard"),
        P("section", "shard", "rep"),
        P("section", "shard", "rep"),
        P("section", "shard", "rep"),
        P("section", "shard"),
        P("section", "shard", None),
        P("section", "shard", "rep", None),
        P("section", "shard", "rep", None),
    )
    return jax.shard_map(body, mesh=mesh, in_specs=in_specs, out_specs=out_specs, check_vma=False)
```

time: 722 us -> 626 us (0.87)
  waiting for transfers between devices: 243 us -> 199 us
  starting transfers between devices: 163 us -> 132 us
  matrix products: 14.4 us -> 1.23 us
  local copies, waits for them, and re-layouts: 97.4 us -> 90.1 us
    all_to_all x2 -> x1, waiting for transfers between devices: 61.9 us -> 14.3 us  [body(): got = lax.all_to_all(send, 'rep', split_axis=0, concat_axis=0, tiled=True)]
    ppermute x84 -> x69, waiting for transfers between devices: 114 us -> 95.7 us  [along_y(): return lax.ppermute(x, 'shard', [(i, (i + 2 * k) % 8) for i in range(8)])]
    ppermute x84 -> x69, starting transfers between devices: 116 us -> 98 us  [along_y(): return lax.ppermute(x, 'shard', [(i, (i + 2 * k) % 8) for i in range(8)])]
    pallas_call x1 -> x3, Pallas kernels: 4.16 us -> 21.2 us  [the longest x2 18.4 us: expert_grad(): pl.pallas_call(lambda *refs: expert_grad_kernel(part, None, *refs), name=...]
    ppermute x0 -> x11, waiting for transfers between devices: none -> 17 us  [the longest x4 11.9 us: z_far(): lax.ppermute(x, 'rep', [(i, (3 - i // 2) * 2 + i % 2) for i in range(8)])]
    pallas_call x24 -> x16, Pallas kernels: 141 us -> 124 us  [call(): pl.pallas_call(kernel, name=name, grid=grid, in_specs=in_specs, out_specs...]
    ppermute x0 -> x11, starting transfers between devices: none -> 15.6 us  [the longest x4 10.1 us: z_far(): lax.ppermute(x, 'rep', [(i, (3 - i // 2) * 2 + i % 2) for i in range(8)])]
    reshape x12 -> x1, local copies, waits for them, and re-layouts: 15.5 us -> 0.02 us  [body(): gg = lax.dynamic_slice(gg[:6].reshape(2, D), (0, shard * SLICE), (2, SLICE))]
  transfers between devices with their start and end apart: 169 -> 115, of which waited for: 47 -> 50; matrix products, arithmetic and copies ran while one was open for 9% -> 6% of each run, Pallas kernels for 20% -> 18%
where the time goes in v2:
time: 626 us; the launch traced here: 616 us
  waiting for transfers between devices  199 us (32%)
  Pallas kernels  145 us (23%)
  starting transfers between devices  132 us (21%)
  local copies, waits for them, and re-layouts  90.1 us (14%)
  other arithmetic  32.6 us (5%)
  between operations  16.2 us (3%)
    pallas_call x16, Pallas kernels, call(): pl.pallas_call(kernel, name=name, grid=grid, in_specs=in_specs, out_specs...  124 us
    ppermute x69, starting transfers between devices, along_y(): return lax.ppermute(x, 'shard', [(i, (i + 2 * k) % 8) for i in range(8)])  98 us
    ppermute x69, waiting for transfers between devices, along_y(): return lax.ppermute(x, 'shard', [(i, (i + 2 * k) % 8) for i in range(8)])  95.7 us
    unnamed x316, local copies, waits for them, and re-layouts  76.6 us
    all_gather x1, waiting for transfers between devices, body(): w = lax.all_gather(packed, 'shard', axis=0, tiled=True)  39.4 us
    pallas_call x2, Pallas kernels, expert_grad(): pl.pallas_call(lambda *refs: expert_grad_kernel(part, None, *refs), name=...  18.4 us
    ppermute x28, waiting for transfers between devices, swap(): return lax.ppermute(x, 'shard', [(i, i ^ 1) for i in range(8)])  14.9 us
    all_to_all x1, waiting for transfers between devices, body(): got = lax.all_to_all(send, 'rep', split_axis=0, concat_axis=0, tiled=True)  14.3 us
  transfers between devices with their start and end apart: 115, of which 50 were waited for; matrix products, arithmetic and copies ran while one was open for 6% of the time, Pallas kernels for 18%

profile of v2, /device:TPU:0, one launch (start us, length us, event | category | flops | bytes accessed | tf_op | source)
XLA Modules:
  0.0 616.2 jit_solution(16982932806004231899)
XLA Ops:
  12.0 10.3 %collective-permute-done.1 = bf16[768,1536]{1,0:T(8,128)(2,1)} collective-permute-done((bf16[768,1536]{1,0:T(8,128)(2,1)}, bf16[768,1536]{1,0:T(8,128)(2,1)}, u32[]{:S(2)}, u32[]{:S(2)}) %collective-permute-start.1) | collective-permute-done | bytes 2359328 | tf_op jit(solution)/shard_map/ppermute | solution.py:63
  22.3 5.7 pad_maximum_fusion.1.refs_7_.refs_9_
  28.0 8.2 %pad_maximum_fusion.refs_5_.refs_6_.refs_10_.refs_11_ = bf16[2,1536,1536]{2,1,0:T(8,128)(2,1)} fusion(bf16[1,1536,1536]{2,1,0:T(8,128)(2,1)} %bitcast.10, bf16[1,1536,1536]{2,1,0:T(8,128)(2,1)} %bitcast.133), kind=kLoop, calls=%fused_computation | loop fusion | flops 4718592 | bytes 18874368 | tf_op jit(solution)/shard_map/stack | solution.py:622
  36.2 39.4 %all-gather.2.cloned.1.call-done.w_ref.refs_12_.refs_14_.refs_15_.refs_16_.refs_17_.refs_10_ = bf16[1536,3712]{1,0:T(8,128)(2,1)} async-done(((bf16[192,3712]{1,0:T(8,128)(2,1)}), bf16[1536,3712]{1,0:T(8,128)(2,1)}) %all-gather.2.cloned.1.call-update) | async-done | bytes 11403280 | tf_op jit(solution)/shard_map/all_gather | solution.py:619
  115.3 4.9 collective-permute-start.16
  124.6 7.6 %expert.4 = (bf16[64,1536]{1,0:T(8,128)(2,1)S(1)}, bf16[64,1536]{1,0:T(8,128)(2,1)S(1)}, bf16[64,1536]{1,0:T(8,128)(2,1)S(1)}, bf16[64,1536]{1,0:T(8,128)(2,1)S(1)}) custom-call(bf16[64,1664]{1,0:T(8,128)(2,1)S(1)} %get-tuple-element.149.refs_0_, bf16[64,1664]{1,0:T(8,128)(2,1)S(1)} %collective-permute-done.9.refs_1_, ...), custom_call_target="tpu_custom_call" | custom-call | flops 3623878656 | bytes 18000000 | tf_op jit(solution)/shard_map/expert/pallas_call | solution.py:47
  135.6 7.6 %expert.5 = (bf16[64,1536]{1,0:T(8,128)(2,1)S(1)}, bf16[64,1536]{1,0:T(8,128)(2,1)S(1)}, bf16[64,1536]{1,0:T(8,128)(2,1)S(1)}, bf16[64,1536]{1,0:T(8,128)(2,1)S(1)}) custom-call(bf16[64,1664]{1,0:T(8,128)(2,1)S(1)} %get-tuple-element.156.refs_0_, bf16[64,1664]{1,0:T(8,128)(2,1)S(1)} %collective-permute-done.16.refs_1_, ...), custom_call_target="tpu_custom_call" | custom-call | flops 3623878656 | bytes 18000000 | tf_op jit(solution)/shard_map/expert/pallas_call | solution.py:47
  147.6 5.4 collective-permute-done.19
  156.9 4.9 collective-permute-start.22
  187.0 5.0 attend.3
  214.7 10.5 %expert.7 = (bf16[64,1536]{1,0:T(8,128)(2,1)S(1)}, bf16[64,1536]{1,0:T(8,128)(2,1)S(1)}, bf16[64,1536]{1,0:T(8,128)(2,1)S(1)}, bf16[64,1536]{1,0:T(8,128)(2,1)S(...) custom-call(bf16[64,1664]{1,0:T(8,128)(2,1)S(1)} %get-tuple-element., ...), custom_call_target="tpu_custom_call" | custom-call | flops 3623878656 | bytes 18000000 | tf_op jit(solution)/shard_map/expert/pallas_call | solution.py:47
  229.0 6.0 collective-permute-done.32.refs_3_
  237.0 9.5 %expert.6 = (bf16[64,1536]{1,0:T(8,128)(2,1)S(1)}, bf16[64,1536]{1,0:T(8,128)(2,1)S(1)}, bf16[64,1536]{1,0:T(8,128)(2,1)S(1)}, bf16[64,1536]{1,0:T(8,128)(2,1)S(...) custom-call(bf16[64,1664]{1,0:T(8,128)(2,1)S(1)} %get-tuple-element., ...), custom_call_target="tpu_custom_call" | custom-call | flops 3623878656 | bytes 18000000 | tf_op jit(solution)/shard_map/expert/pallas_call | solution.py:47
  249.7 4.9 collective-permute-start.44
  255.7 11.8 %expert_back.5 = (bf16[64,1664]{1,0:T(8,128)(2,1)S(1)}, bf16[64,1664]{1,0:T(8,128)(2,1)S(1)}, bf16[64,1664]{1,0:T(8,128)(2,1)S(1)}, bf16[64,1664]{1,0:T(8,128)(2,1)S(1)}) custom-call(bf16[64,1536]{1,0:T(8,128)(2,1)S(1)} %get-tuple-element.354.refs_0_.refs_9_, bf16[64,1536]{1,0:T(8,128)(2,1)S(1)} %collective-permute-done.48.refs_1_, ...), custom_call_target="tpu_custom_call" | custom-call | flops 3623878656 | bytes 20000000 | tf_op jit(solution)/shard_map/expert_back/pallas_call | solution.py:47
  273.0 10.9 %expert_back.4 = (bf16[64,1664]{1,0:T(8,128)(2,1)S(1)}, bf16[64,1664]{1,0:T(8,128)(2,1)S(1)}, bf16[64,1664]{1,0:T(8,128)(2,1)S(1)}, bf16[64,1664]{1,0:T(8,128)(2,1)S(1)}) custom-call(bf16[64,1536]{1,0:T(8,128)(2,1)S(1)} %copy-done.43, bf16[64,1536]{1,0:T(8,128)(2,1)S(1)} %collective-permute-done.42.refs_1_, ...), custom_call_target="tpu_custom_call" | custom-call | flops 3623878656 | bytes 20000000 | tf_op jit(solution)/shard_map/expert_back/pallas_call | solution.py:47
  290.7 5.4 collective-permute-done.45.refs_1_
  326.6 7.9 %attend_back.2 = (f32[128,1536]{1,0:T(8,128)S(1)}, bf16[128,1536]{1,0:T(8,128)(2,1)}, bf16[128,1536]{1,0:T(8,128)(2,1)S(1)}, bf16[512,512]{1,0:T(8,128)(2,1)S(1)...) custom-call(bf16[64,1664]{1,0:T(8,128)(2,1)S(1)} %copy-done.103, ...), custom_call_target="tpu_custom_call" | custom-call | flops 1610612736 | bytes 8000000 | tf_op jit(solution)/shard_map/attend_back/pallas_call | solution.py:47
  339.9 6.3 %collective-permute-done.59.refs_3_ = bf16[128,512]{1,0:T(8,128)(2,1)S(1)} collective-permute-done((bf16[128,512]{1,0:T(8,128)(2,1)S(1)}, bf16[128,512]{1,0:T(8,128)(2,1)S(1)}, u32[]{:S(2)}, u32[]{:S(2)}) %collective-permute-start.59) | collective-permute-done | bytes 131104 | tf_op jit(solution)/shard_map/ppermute | solution.py:67
  353.8 8.6 %collective-permute-done.60 = bf16[64,1536]{1,0:T(8,128)(2,1)S(1)} collective-permute-done((bf16[64,1536]{1,0:T(8,128)(2,1)S(1)}, bf16[64,1536]{1,0:T(8,128)(2,1)S(1)}, u32[]{:S(2)}, u32[]{:S(2)}) %collective-permute-start.60) | collective-permute-done | bytes 196640 | tf_op jit(solution)/shard_map/ppermute | solution.py:724
  383.2 12.9 %expert_back.6 = (bf16[64,1664]{1,0:T(8,128)(2,1)S(1)}, bf16[64,1664]{1,0:T(8,128)(2,1)S(1)}, bf16[64,1664]{1,0:T(8,128)(2,1)S(1)}, bf16[64,1664]{1,0:T(8,128)(2...) custom-call(bf16[64,1536]{1,0:T(8,128)(2,1)S(1)} %get-tuple-element.353.refs_0_.refs_8_, ...), custom_call_target="tpu_custom_call" | custom-call | flops 3623878656 | bytes 20000000 | tf_op jit(solution)/shard_map/expert_back/pallas_call | solution.py:47
  398.7 13.0 %expert_back.7 = (bf16[64,1664]{1,0:T(8,128)(2,1)S(1)}, bf16[64,1664]{1,0:T(8,128)(2,1)S(1)}, bf16[64,1664]{1,0:T(8,128)(2,1)S(1)}, bf16[64,1664]{1,0:T(8,128)(2...) custom-call(bf16[64,1536]{1,0:T(8,128)(2,1)S(1)} %get-tuple-element.352.refs_0_.refs_9_, ...), custom_call_target="tpu_custom_call" | custom-call | flops 3623878656 | bytes 20000000 | tf_op jit(solution)/shard_map/expert_back/pallas_call | solution.py:47
  427.4 10.7 %expert_grad.2 = bf16[8,192,1536]{2,1,0:T(8,128)(2,1)S(1)} custom-call(s32[8]{0:T(128)S(1)} %stack.113.refs_0_, bf16[256,2304]{1,0:T(8,128)(2,1)S(1)} %copy-done.84, bf16[256,2304]{1,0:T(8,128)(2,1)S(1)} %copy-done.81, bf16[256,2304]{1,0:T(8,128)(2,1)} %collective-permute-done.54.refs_3_, bf16[256,2304]{1,0:T(8,128)(2,1)} %collective-permute-done.55.refs_4_, ...), custom_call_target="tpu_custom_call" | custom-call | flops 4831838208 | bytes 8000000 | tf_op jit(solution)/shard_map/expert_grad/pallas_call | solution.py:593
  439.9 7.7 %expert_grad.3 = bf16[8,96,1536]{2,1,0:T(8,128)(2,1)S(1)} custom-call(s32[8]{0:T(128)S(1)} %stack.113.refs_0_, bf16[256,2304]{1,0:T(8,128)(2,1)S(1)} %copy-done.85, bf16[256,2304]{1,0:T(8,128)(2,1)S(1)} %copy-done.82, bf16[256,2304]{1,0:T(8,128)(2,1)} %collective-permute-done.54.refs_3_, bf16[256,2304]{1,0:T(8,128)(2,1)} %collective-permute-done.55.refs_4_, ...), custom_call_target="tpu_custom_call" | custom-call | flops 2415919104 | bytes 8000000 | tf_op jit(solution)/shard_map/expert_grad/pallas_call | solution.py:593
  451.8 7.2 %attend_back.3 = (f32[128,1536]{1,0:T(8,128)S(1)}, bf16[128,1536]{1,0:T(8,128)(2,1)S(1)}, bf16[128,1536]{1,0:T(8,128)(2,1)S(1)}, bf16[512,512]{1,0:T(8,128)(2,1)...) custom-call(bf16[64,1664]{1,0:T(8,128)(2,1)S(1)} %copy-done.91, ...), custom_call_target="tpu_custom_call" | custom-call | flops 1610612736 | bytes 8000000 | tf_op jit(solution)/shard_map/attend_back/pallas_call | solution.py:47
  465.9 6.2 %collective-permute-done.33 = bf16[64,1536]{1,0:T(8,128)(2,1)S(1)} collective-permute-done((bf16[64,1536]{1,0:T(8,128)(2,1)S(1)}, bf16[64,1536]{1,0:T(8,128)(2,1)S(1)}, u32[]{:S(2)}, u32[]{:S(2)}) %collective-permute-start.33) | collective-permute-done | bytes 196640 | tf_op jit(solution)/shard_map/ppermute | solution.py:67
  494.7 6.3 %collective-permute-done.81 = bf16[2,2,192,768]{3,2,1,0:T(8,128)(2,1)S(1)} collective-permute-done((bf16[2,2,192,768]{3,2,1,0:T(8,128)(2,1)S(1)}, bf16[2,2,192,768]{3,2,1,0:T(8,128)(2,1)S(1)}, u32[]{:S(2)}, u32[]{:S(2)}) %collective-permute-start.81) | collective-permute-done | bytes 1179680 | tf_op jit(solution)/shard_map/ppermute | solution.py:88
  515.2 7.7 %collective-permute-done.96.refs_13_ = bf16[128,1536]{1,0:T(8,128)(2,1)S(1)} collective-permute-done((bf16[128,1536]{1,0:T(8,128)(2,1)S(1)}, bf16[128,1536]{1,0:T(8,128)(2,1)S(1)}, u32[]{:S(2)}, u32[]{:S(2)}) %collective-permute-start.96) | collective-permute-done | bytes 393248 | tf_op jit(solution)/shard_map/ppermute | solution.py:67
  524.2 7.2 %collective-permute-done.94.refs_11_ = bf16[128,1536]{1,0:T(8,128)(2,1)S(1)} collective-permute-done((bf16[128,1536]{1,0:T(8,128)(2,1)S(1)}, bf16[128,1536]{1,0:T(8,128)(2,1)S(1)}, u32[]{:S(2)}, u32[]{:S(2)}) %collective-permute-start.94) | collective-permute-done | bytes 393248 | tf_op jit(solution)/shard_map/ppermute | solution.py:67
  538.7 6.1 collective-permute-done.83.refs_3_
  549.1 5.5 collective-permute-done.90
  591.3 14.3 %all-to-all-done.1 = bf16[8,192,512]{2,1,0:T(8,128)(2,1)S(1)} async-done(((bf16[8,192,512]{2,1,0:T(8,128)(2,1)}), bf16[8,192,512]{2,1,0:T(8,128)(2,1)S(1)}, u32[]{:S(2)}, u32[]{:S(2)}) %all-to-all-start.1) | async-done | bytes 1572896 | tf_op jit(solution)/shard_map/all_to_all | solution.py:741
  (623 shorter events, 314.4 us)
Async XLA Ops:
  7.2 68.4 %all-gather.2.cloned.1.call-start = ((), (), s32[]{:S(2)}) async-start(), calls=%async_computation.2 | async-start | bytes 12828672 | tf_op jit(solution)/shard_map/all_gather | solution.py:619
  110.4 24.3 %collective-permute-start.18 = (bf16[64,1664]{1,0:T(8,128)(2,1)S(1)}, bf16[64,1664]{1,0:T(8,128)(2,1)S(1)}, u32[]{:S(2)}, u32[]{:S(2)}) collective-permute-start(bf16[64,1664]{1,0:T(8,128)(2,1)S(1)} %get-tuple-element.156.refs_0_), channel_id=1, source_target_pairs={{0,6},{1,7},{2,0},{3,1},{4,2},{5,3},{6,4},{7,5},{8,14},{9,15},{10,... | collective-permute-start | bytes 638984 | tf_op jit(solution)/shard_map/ppermute | solution.py:67
  113.2 22.4 %collective-permute-start.17 = (bf16[64,1664]{1,0:T(8,128)(2,1)S(1)}, bf16[64,1664]{1,0:T(8,128)(2,1)S(1)}, u32[]{:S(2)}, u32[]{:S(2)}) collective-permute-start(bf16[64,1664]{1,0:T(8,128)(2,1)S(1)} %get-tuple-element.156.refs_0_), channel_id=1, source_target_pairs={{0,4},{1,5},{2,6},{3,7},{4,0},{5,1},{6,2},{7,3},{8,12},{9,13},{10,... | collective-permute-start | bytes 638984 | tf_op jit(solution)/shard_map/ppermute | solution.py:67
  115.3 20.3 %collective-permute-start.16 = (bf16[64,1664]{1,0:T(8,128)(2,1)S(1)}, bf16[64,1664]{1,0:T(8,128)(2,1)S(1)}, u32[]{:S(2)}, u32[]{:S(2)}) collective-permute-start(bf16[64,1664]{1,0:T(8,128)(2,1)S(1)} %get-tuple-element.156.refs_0_), channel_id=1, source_target_pairs={{0,2},{1,3},{2,4},{3,5},{4,6},{5,7},{6,0},{7,1},{8,10},{9,11},{10,... | collective-permute-start | bytes 638984 | tf_op jit(solution)/shard_map/ppermute | solution.py:67
  194.6 55.1 %collective-permute-start.50 = (bf16[64,1536]{1,0:T(8,128)(2,1)S(1)}, bf16[64,1536]{1,0:T(8,128)(2,1)}, u32[]{:S(2)}, u32[]{:S(2)}) collective-permute-start(bf16[64,1536]{1,0:T(8,128)(2,1)S(1)} %get-tuple-element.354.refs_0_.refs_9_), channel_id=1, source_target_pairs={{0,6},{1,7},{2,0},{3,1},{4,2},{5,3},{6,4},{7,5},{8,14},{9,15},{10,... | collective-permute-start | bytes 589832 | tf_op jit(solution)/shard_map/ppermute | solution.py:67
  197.9 56.7 %collective-permute-start.49 = (bf16[64,1536]{1,0:T(8,128)(2,1)S(1)}, bf16[64,1536]{1,0:T(8,128)(2,1)}, u32[]{:S(2)}, u32[]{:S(2)}) collective-permute-start(bf16[64,1536]{1,0:T(8,128)(2,1)S(1)} %get-tuple-element.354.refs_0_.refs_9_), channel_id=1, source_target_pairs={{0,4},{1,5},{2,6},{3,7},{4,0},{5,1},{6,2},{7,3},{8,12},{9,13},{10,... | collective-permute-start | bytes 589832 | tf_op jit(solution)/shard_map/ppermute | solution.py:67
  199.2 102.0 %all-to-all-start = ((bf16[8,128,768]{2,1,0:T(8,128)(2,1)}), bf16[8,128,768]{2,1,0:T(8,128)(2,1)S(1)}, u32[]{:S(2)}, u32[]{:S(2)}) async-start(bf16[8,128,768]{2,1,0:T(8,128)(2,1)} %copy-done.49), calls=%async_computation | async-start | bytes 3145728 | tf_op jit(solution)/shard_map/all_to_all | solution.py:680
  202.8 32.1 %collective-permute-start.32 = (bf16[64,1664]{1,0:T(8,128)(2,1)S(1)}, bf16[64,1664]{1,0:T(8,128)(2,1)S(1)}, u32[]{:S(2)}, u32[]{:S(2)}) collective-permute-start(bf16[64,1664]{1,0:T(8,128)(2,1)S(1)} %get-tuple-element.165.refs_0_.refs_11_), channel_id=1, source_target_pairs={{0,6},{1,7},{2,0},{3,1},{4,2},{5,3},{6,4},{7,5},{8,14},{9,15},{10,... | collective-permute-start | bytes 638984 | tf_op jit(solution)/shard_map/ppermute | solution.py:67
  207.0 27.9 %collective-permute-start.31 = (bf16[64,1664]{1,0:T(8,128)(2,1)S(1)}, bf16[64,1664]{1,0:T(8,128)(2,1)S(1)}, u32[]{:S(2)}, u32[]{:S(2)}) collective-permute-start(bf16[64,1664]{1,0:T(8,128)(2,1)S(1)} %get-tuple-element.165.refs_0_.refs_11_), channel_id=1, source_target_pairs={{0,4},{1,5},{2,6},{3,7},{4,0},{5,1},{6,2},{7,3},{8,12},{9,13},{10,... | collective-permute-start | bytes 638984 | tf_op jit(solution)/shard_map/ppermute | solution.py:67
  207.9 29.1 %collective-permute-start.30 = (bf16[64,1664]{1,0:T(8,128)(2,1)S(1)}, bf16[64,1664]{1,0:T(8,128)(2,1)S(1)}, u32[]{:S(2)}, u32[]{:S(2)}) collective-permute-start(bf16[64,1664]{1,0:T(8,128)(2,1)S(1)} %get-tuple-element.165.refs_0_.refs_11_), channel_id=1, source_target_pairs={{0,2},{1,3},{2,4},{3,5},{4,6},{5,7},{6,0},{7,1},{8,10},{9,11},{10,... | collective-permute-start | bytes 638984 | tf_op jit(solution)/shard_map/ppermute | solution.py:67
  234.9 19.7 %collective-permute-start.48 = (bf16[64,1536]{1,0:T(8,128)(2,1)S(1)}, bf16[64,1536]{1,0:T(8,128)(2,1)S(1)}, u32[]{:S(2)}, u32[]{:S(2)}) collective-permute-start(bf16[64,1536]{1,0:T(8,128)(2,1)S(1)} %get-tuple-element.354.refs_0_.refs_9_), channel_id=1, source_target_pairs={{0,2},{1,3},{2,4},{3,5},{4,6},{5,7},{6,0},{7,1},{8,10},{9,11},{10,... | collective-permute-start | bytes 589832 | tf_op jit(solution)/shard_map/ppermute | solution.py:67
  235.0 66.2 %collective-permute-start.55 = (bf16[256,2304]{1,0:T(8,128)(2,1)}, bf16[256,2304]{1,0:T(8,128)(2,1)}, u32[]{:S(2)}, u32[]{:S(2)}) collective-permute-start(bf16[256,2304]{1,0:T(8,128)(2,1)} %get-tuple-element.193), channel_id=1, source_target_pairs={{0,1},{1,0},{2,3},{3,2},{4,5},{5,4},{6,7},{7,6},{8,9},{9,8},{10,11... | collective-permute-start | bytes 3538952 | tf_op jit(solution)/shard_map/ppermute | solution.py:63
  249.6 51.6 %collective-permute-start.54 = (bf16[256,2304]{1,0:T(8,128)(2,1)}, bf16[256,2304]{1,0:T(8,128)(2,1)}, u32[]{:S(2)}, u32[]{:S(2)}) collective-permute-start(bf16[256,2304]{1,0:T(8,128)(2,1)} %get-tuple-element.192), channel_id=1, source_target_pairs={{0,1},{1,0},{2,3},{3,2},{4,5},{5,4},{6,7},{7,6},{8,9},{9,8},{10,11... | collective-permute-start | bytes 3538952 | tf_op jit(solution)/shard_map/ppermute | solution.py:63
  369.3 28.7 %collective-permute-start.70 = (bf16[64,1536]{1,0:T(8,128)(2,1)S(1)}, bf16[64,1536]{1,0:T(8,128)(2,1)S(1)}, u32[]{:S(2)}, u32[]{:S(2)}) collective-permute-start(bf16[64,1536]{1,0:T(8,128)(2,1)S(1)} %get-tuple-element.352.refs_0_.refs_9_), channel_id=1, source_target_pairs={{0,6},{1,7},{2,0},{3,1},{4,2},{5,3},{6,4},{7,5},{8,14},{9,15},{10,... | collective-permute-start | bytes 589832 | tf_op jit(solution)/shard_map/ppermute | solution.py:67
  371.6 26.3 %collective-permute-start.69 = (bf16[64,1536]{1,0:T(8,128)(2,1)S(1)}, bf16[64,1536]{1,0:T(8,128)(2,1)S(1)}, u32[]{:S(2)}, u32[]{:S(2)}) collective-permute-start(bf16[64,1536]{1,0:T(8,128)(2,1)S(1)} %get-tuple-element.352.refs_0_.refs_9_), channel_id=1, source_target_pairs={{0,4},{1,5},{2,6},{3,7},{4,0},{5,1},{6,2},{7,3},{8,12},{9,13},{10,... | collective-permute-start | bytes 589832 | tf_op jit(solution)/shard_map/ppermute | solution.py:67
  377.1 21.6 %collective-permute-start.68 = (bf16[64,1536]{1,0:T(8,128)(2,1)S(1)}, bf16[64,1536]{1,0:T(8,128)(2,1)S(1)}, u32[]{:S(2)}, u32[]{:S(2)}) collective-permute-start(bf16[64,1536]{1,0:T(8,128)(2,1)S(1)} %get-tuple-element.352.refs_0_.refs_9_), channel_id=1, source_target_pairs={{0,2},{1,3},{2,4},{3,5},{4,6},{5,7},{6,0},{7,1},{8,10},{9,11},{10,... | collective-permute-start | bytes 589832 | tf_op jit(solution)/shard_map/ppermute | solution.py:67
  397.9 21.5 %collective-permute-start.74 = (bf16[256,3072]{1,0:T(8,128)(2,1)}, bf16[256,3072]{1,0:T(8,128)(2,1)}, u32[]{:S(2)}, u32[]{:S(2)}) collective-permute-start(bf16[256,3072]{1,0:T(8,128)(2,1)} %get-tuple-element.229), channel_id=1, source_target_pairs={{0,1},{1,0},{2,3},{3,2},{4,5},{5,4},{6,7},{7,6},{8,9},{9,8},{10,11... | collective-permute-start | bytes 4718600 | tf_op jit(solution)/shard_map/ppermute | solution.py:63
  415.7 22.4 %collective-permute-start.64 = (bf16[64,1664]{1,0:T(8,128)(2,1)}, bf16[64,1664]{1,0:T(8,128)(2,1)S(1)}, u32[]{:S(2)}, u32[]{:S(2)}) collective-permute-start(bf16[64,1664]{1,0:T(8,128)(2,1)} %copy-done.122), channel_id=1, source_target_pairs={{0,6},{1,7},{2,0},{3,1},{4,2},{5,3},{6,4},{7,5},{8,14},{9,15},{10,... | collective-permute-start | bytes 638984 | tf_op jit(solution)/shard_map/ppermute | solution.py:67
  416.5 31.1 %collective-permute-start.65 = (bf16[64,1664]{1,0:T(8,128)(2,1)}, bf16[64,1664]{1,0:T(8,128)(2,1)S(1)}, u32[]{:S(2)}, u32[]{:S(2)}) collective-permute-start(bf16[64,1664]{1,0:T(8,128)(2,1)} %copy-done.117), channel_id=1, source_target_pairs={{0,4},{1,5},{2,6},{3,7},{4,0},{5,1},{6,2},{7,3},{8,12},{9,13},{10,... | collective-permute-start | bytes 638984 | tf_op jit(solution)/shard_map/ppermute | solution.py:67
  418.1 31.5 %collective-permute-start.66 = (bf16[64,1664]{1,0:T(8,128)(2,1)}, bf16[64,1664]{1,0:T(8,128)(2,1)S(1)}, u32[]{:S(2)}, u32[]{:S(2)}) collective-permute-start(bf16[64,1664]{1,0:T(8,128)(2,1)} %copy-done.116), channel_id=1, source_target_pairs={{0,2},{1,3},{2,4},{3,5},{4,6},{5,7},{6,0},{7,1},{8,10},{9,11},{10,... | collective-permute-start | bytes 638984 | tf_op jit(solution)/shard_map/ppermute | solution.py:67
  419.4 31.8 %collective-permute-start.71 = (bf16[64,1664]{1,0:T(8,128)(2,1)}, bf16[64,1664]{1,0:T(8,128)(2,1)S(1)}, u32[]{:S(2)}, u32[]{:S(2)}) collective-permute-start(bf16[64,1664]{1,0:T(8,128)(2,1)} %copy-done.121), channel_id=1, source_target_pairs={{0,6},{1,7},{2,0},{3,1},{4,2},{5,3},{6,4},{7,5},{8,14},{9,15},{10,... | collective-permute-start | bytes 638984 | tf_op jit(solution)/shard_map/ppermute | solution.py:67
  421.3 30.3 %collective-permute-start.72 = (bf16[64,1664]{1,0:T(8,128)(2,1)}, bf16[64,1664]{1,0:T(8,128)(2,1)S(1)}, u32[]{:S(2)}, u32[]{:S(2)}) collective-permute-start(bf16[64,1664]{1,0:T(8,128)(2,1)} %copy-done.120), channel_id=1, source_target_pairs={{0,4},{1,5},{2,6},{3,7},{4,0},{5,1},{6,2},{7,3},{8,12},{9,13},{10,... | collective-permute-start | bytes 638984 | tf_op jit(solution)/shard_map/ppermute | solution.py:67
  459.3 33.4 %collective-permute-start.82 = (bf16[4,96,1536]{2,1,0:T(8,128)(2,1)S(1)}, bf16[4,96,1536]{2,1,0:T(8,128)(2,1)S(1)}, u32[]{:S(2)}, u32[]{:S(2)}) collective-permute-start(bf16[4,96,1536]{2,1,0:T(8,128)(2,1)S(1)} %slice_bitcast_fusion), channel_id=1, source_target_pairs={{0,8},{8,0},{16,24},{24,16},{32,40},{40,32},{48,56},{56,48},{1,9},... | collective-permute-start | bytes 3538952 | tf_op jit(solution)/shard_map/ppermute | solution.py:92
  464.3 28.8 %collective-permute-start.80 = (bf16[2,2,192,768]{3,2,1,0:T(8,128)(2,1)S(1)}, bf16[2,2,192,768]{3,2,1,0:T(8,128)(2,1)S(1)}, u32[]{:S(2)}, u32[]{:S(2)}) collective-permute-start(bf16[2,2,192,768]{3,2,1,0:T(8,128)(2,1)S(1)} %slice.226), channel_id=1, source_target_pairs={{0,16},{8,24},{16,0},{24,8},{32,48},{40,56},{48,32},{56,40},{1,17}... | collective-permute-start | bytes 3538952 | tf_op jit(solution)/shard_map/ppermute | solution.py:84
  472.4 28.6 %collective-permute-start.81 = (bf16[2,2,192,768]{3,2,1,0:T(8,128)(2,1)S(1)}, bf16[2,2,192,768]{3,2,1,0:T(8,128)(2,1)S(1)}, u32[]{:S(2)}, u32[]{:S(2)}) collective-permute-start(bf16[2,2,192,768]{3,2,1,0:T(8,128)(2,1)S(1)} %pad_maximum_fusion.3), channel_id=1, source_target_pairs={{0,48},{8,56},{16,32},{24,40},{32,16},{40,24},{48,0},{56,8},{1,49}... | collective-permute-start | bytes 3538952 | tf_op jit(solution)/shard_map/ppermute | solution.py:88
  485.6 20.2 %collective-permute-start.103 = (bf16[128,1536]{1,0:T(8,128)(2,1)S(1)}, bf16[128,1536]{1,0:T(8,128)(2,1)S(1)}, u32[]{:S(2)}, u32[]{:S(2)}) collective-permute-start(bf16[128,1536]{1,0:T(8,128)(2,1)S(1)} %get-tuple-element.268.refs_18_), channel_id=1, source_target_pairs={{0,6},{1,7},{2,0},{3,1},{4,2},{5,3},{6,4},{7,5},{8,14},{9,15},{10,... | collective-permute-start | bytes 1179656 | tf_op jit(solution)/shard_map/ppermute | solution.py:67
  493.0 21.7 %collective-permute-start.101 = (bf16[128,1536]{1,0:T(8,128)(2,1)S(1)}, bf16[128,1536]{1,0:T(8,128)(2,1)S(1)}, u32[]{:S(2)}, u32[]{:S(2)}) collective-permute-start(bf16[128,1536]{1,0:T(8,128)(2,1)S(1)} %get-tuple-element.268.refs_18_), channel_id=1, source_target_pairs={{0,2},{1,3},{2,4},{3,5},{4,6},{5,7},{6,0},{7,1},{8,10},{9,11},{10,... | collective-permute-start | bytes 1179656 | tf_op jit(solution)/shard_map/ppermute | solution.py:67
  501.3 21.6 %collective-permute-start.96 = (bf16[128,1536]{1,0:T(8,128)(2,1)S(1)}, bf16[128,1536]{1,0:T(8,128)(2,1)S(1)}, u32[]{:S(2)}, u32[]{:S(2)}) collective-permute-start(bf16[128,1536]{1,0:T(8,128)(2,1)S(1)} %get-tuple-element.247.refs_4_.refs_10_), channel_id=1, source_target_pairs={{0,6},{1,7},{2,0},{3,1},{4,2},{5,3},{6,4},{7,5},{8,14},{9,15},{10,... | collective-permute-start | bytes 1179656 | tf_op jit(solution)/shard_map/ppermute | solution.py:67
  506.6 24.8 %collective-permute-start.94 = (bf16[128,1536]{1,0:T(8,128)(2,1)S(1)}, bf16[128,1536]{1,0:T(8,128)(2,1)S(1)}, u32[]{:S(2)}, u32[]{:S(2)}) collective-permute-start(bf16[128,1536]{1,0:T(8,128)(2,1)S(1)} %get-tuple-element.247.refs_4_.refs_10_), channel_id=1, source_target_pairs={{0,2},{1,3},{2,4},{3,5},{4,6},{5,7},{6,0},{7,1},{8,10},{9,11},{10,... | collective-permute-start | bytes 1179656 | tf_op jit(solution)/shard_map/ppermute | solution.py:67
  534.8 19.9 %collective-permute-start.90 = (bf16[2,192,768]{2,1,0:T(8,128)(2,1)S(1)}, bf16[2,192,768]{2,1,0:T(8,128)(2,1)S(1)}, u32[]{:S(2)}, u32[]{:S(2)}) collective-permute-start(bf16[2,192,768]{2,1,0:T(8,128)(2,1)S(1)} %slice_bitcast_fusion.3), channel_id=1, source_target_pairs={{0,48},{8,56},{16,32},{24,40},{32,16},{40,24},{48,0},{56,8},{1,49}... | collective-permute-start | bytes 1769480 | tf_op jit(solution)/shard_map/ppermute | solution.py:88
  563.4 19.8 %collective-permute-start.110 = (bf16[96,768]{1,0:T(8,128)(2,1)}, bf16[96,768]{1,0:T(8,128)(2,1)}, u32[]{:S(2)}, u32[]{:S(2)}) collective-permute-start(bf16[96,768]{1,0:T(8,128)(2,1)} %slice_bitcast_fusion.11), channel_id=1, source_target_pairs={{0,48},{8,56},{16,32},{24,40},{32,16},{40,24},{48,0},{56,8},{1,49}... | collective-permute-start | bytes 442376 | tf_op jit(solution)/shard_map/ppermute | solution.py:88
  578.4 27.1 %all-to-all-start.1 = ((bf16[8,192,512]{2,1,0:T(8,128)(2,1)}), bf16[8,192,512]{2,1,0:T(8,128)(2,1)S(1)}, u32[]{:S(2)}, u32[]{:S(2)}) async-start(bf16[8,192,512]{2,1,0:T(8,128)(2,1)} %pad_maximum_fusion.2), calls=%async_computation.1 | async-start | bytes 3145728 | tf_op jit(solution)/shard_map/all_to_all | solution.py:741
  (239 other events, 2946.0 us)
Sparse Core Ops, SparseCore 0:
  10.7 64.8 all-gather.1

commit v3 on v1

v3 whole, which is shorter than its diff:
```python
import jax
import jax.numpy as jnp
from jax import lax
from jax.experimental import pallas as pl
from jax.experimental.pallas import tpu as pltpu
from jax.sharding import PartitionSpec as P

D = 1536
T = 64
R = 2 * T
C = 4 * T
HEADS = 12
KV_HEADS = 2
GROUP = HEADS // KV_HEADS
HS = 128
KW = KV_HEADS * HS
SLICE = D // 8
FF = 768
SEQ = 512
N_EXPERTS = 8
LANES = 128
EPS = 1e-06
ROPE_BASE = 1000000.0
SCALE = HS**-0.5
BF = jnp.bfloat16
VMEM = 24 * 2**20
F32 = jnp.float32

NN = (((1,), (0,)), ((), ()))
NT = (((1,), (1,)), ((), ()))
TN = (((0,), (0,)), ((), ()))


def mm(a, b, dims=NN):
    return lax.dot_general(a, b, dims, preferred_element_type=F32)


def sds(shape, dtype):
    return jax.ShapeDtypeStruct(shape, dtype)


def whole(shape):
    return pl.BlockSpec(shape, lambda *_: (0,) * len(shape))


def in_hbm(args):
    return [pltpu.with_memory_space_constraint(a, pltpu.HBM) for a in args]


HERE = pl.BlockSpec(memory_space=pltpu.VMEM)
AWAY = pl.BlockSpec(memory_space=pltpu.HBM)
SCALARS = pl.BlockSpec(memory_space=pltpu.SMEM)


def work(us):
    return pl.CostEstimate(flops=1, bytes_accessed=int(us * 3.7 * 10**6), transcendentals=0)


def call(kernel, name, here, away, outs, outs_away, scratch, us, vmem, scalars=None):
    scalars = [] if scalars is None else [scalars]
    return pl.pallas_call(
        kernel,
        name=name,
        in_specs=[SCALARS] * len(scalars) + [HERE] * len(here) + [AWAY] * len(away),
        out_specs=[HERE] * len(outs) + [AWAY] * len(outs_away),
        out_shape=outs + [pltpu.HBM(o.shape, o.dtype) for o in outs_away],
        scratch_shapes=scratch,
        compiler_params=pltpu.CompilerParams(vmem_limit_bytes=vmem * 2**20),
        cost_estimate=work(us),
    )(*scalars, *here, *in_hbm(away))


def fetch(src, dst, sem):
    copy = pltpu.make_async_copy(src, dst, sem)
    copy.start()
    return copy


def swap(x):
    return lax.ppermute(x, "shard", [(i, i ^ 1) for i in range(8)])


def along_y(x, k):
    return lax.ppermute(x, "shard", [(i, (i + 2 * k) % 8) for i in range(8)])


def from_chips(x):
    return [x, along_y(x, 1), along_y(x, 2), along_y(x, 3)]


def to_chips(blocks):
    return [blocks[0]] + [along_y(blocks[k], -k) for k in (1, 2, 3)]


def gather_blocks(x):
    same = from_chips(x)
    return same + [swap(b) for b in same]


def plus(a, b):
    return (a.astype(F32) + b.astype(F32)).astype(BF)


def rope(x, cos, sin):
    return x * cos + pltpu.roll(x, HS // 2, 1) * sin


def rope_back(x, cos, sin):
    return x * cos - pltpu.roll(x, HS // 2, 1) * sin


def qkv_kernel(x0_ref, x1_ref, gain_ref, cos_ref, sin_ref, w_ref, q_ref, kv_ref, h_ref, w_s, sems):
    copies = [fetch(w_ref.at[:, j * 512 : (j + 1) * 512], w_s.at[j], sems.at[j]) for j in range(4)]
    for m, x_ref in enumerate((x0_ref, x1_ref)):
        x = x_ref[...].astype(F32)
        r = lax.rsqrt(jnp.mean(x * x, axis=-1, keepdims=True) + EPS)
        h_ref[m * T : (m + 1) * T, :] = (x * r * gain_ref[0:1, :]).astype(BF)
    cos, sin = cos_ref[...], sin_ref[...]
    for j in range(4):
        copies[j].wait()
        y = mm(h_ref[...], w_s[j])
        for i in range(4 if j < 3 else 2):
            at = slice(i * HS, (i + 1) * HS)
            turned = rope(y[:, at], cos, sin).astype(BF)
            if j < 3:
                q_ref[:, j * 512 + i * HS : j * 512 + (i + 1) * HS] = turned
            else:
                kv_ref[:, at] = turned
        if j == 3:
            kv_ref[:, KW:] = y[:, KW:].astype(BF)


def qkv(x0, x1, gains, w, cos, sin):
    return call(
        qkv_kernel, "qkv", [x0, x1, gains, cos, sin], [w],
        [sds((R, D), BF), sds((R, 512), BF), sds((R, D), BF)], [],
        [pltpu.VMEM((4, D, 512), BF), pltpu.SemaphoreType.DMA((4,))],
        3.5, 10,
    )


def fetch_keys(kv_refs, kv_s, sems):
    return [
        fetch(kv_refs[i].at[m * T : (m + 1) * T, :], kv_s.at[m, i * T : (i + 1) * T, :], sems.at[m, i]) for i in range(1, 8) for m in range(2)
    ]


def own_keys(own, kv_s):
    for m in range(2):
        kv_s[m, 0:T, :] = own[m * T : (m + 1) * T, :]


def heads_of(ref, m, k):
    rows = slice(m * T, (m + 1) * T)
    return jnp.concatenate([ref[rows, h * HS : (h + 1) * HS] for h in range(k * GROUP, (k + 1) * GROUP)], axis=0)


def probs_of(q6, keys, allowed):
    s = mm(q6, keys, NT) * SCALE
    s = jnp.where(allowed[None] > 0, s.reshape(GROUP, T, SEQ), -1e30)
    e = jnp.exp(s - jnp.max(s, axis=-1, keepdims=True))
    p = e * (1.0 / jnp.sum(e, axis=-1, keepdims=True))
    return p.reshape(GROUP * T, SEQ)


def fetch_w_out(spots_ref, pieces, w_s, sems):
    copies = []
    for p, piece in enumerate(pieces):
        for k in range(4):
            i = p * 4 + k
            at = pl.ds(pl.multiple_of(spots_ref[i], 16), SLICE // 4)
            copies.append(fetch(piece.at[k], w_s.at[at, :], sems.at[i]))
    return copies


def attend_kernel(save, *refs):
    spots_ref, q_ref, own_ref, allowed_ref, x0_ref, x1_ref, gain_ref, chosen_ref, rest = *refs[:8], refs[8:]
    if save:
        h_ref, rest = rest[0], rest[1:]
    w_refs, wp_ref, kv_refs, rest = rest[:8], rest[8], (None,) + rest[9:16], rest[16:]
    if save:
        att_ref, mid_ref, hm0_ref, hm1_ref, left_ref, kv_s, w_s, wr_s, sems, kv_sems = rest
    else:
        att_ref, mid_ref, hm0_ref, hm1_ref, kv_s, w_s, wr_s, sems, kv_sems = rest
    key_copies = fetch_keys(kv_refs, kv_s, kv_sems)
    router_copy = fetch(wp_ref.at[:, 2048:], wr_s, sems.at[32])
    copies = fetch_w_out(spots_ref, w_refs, w_s, sems)
    own_keys(own_ref, kv_s)
    allowed = allowed_ref[...]
    for copy in key_copies:
        copy.wait()
    for m in range(2):
        for k in range(KV_HEADS):
            p = probs_of(heads_of(q_ref, m, k), kv_s[m, :, k * HS : (k + 1) * HS], allowed).astype(BF)
            o = mm(p, kv_s[m, :, KW + k * HS : KW + (k + 1) * HS])
            for g in range(GROUP):
                h = k * GROUP + g
                att_ref[m * T : (m + 1) * T, h * HS : (h + 1) * HS] = o[g * T : (g + 1) * T].astype(BF)
    square = [0.0, 0.0]
    for copy in copies:
        copy.wait()
    for j in range(3):
        at = slice(j * 512, (j + 1) * 512)
        y = mm(att_ref[...], w_s[:, at])
        for m, x_ref in enumerate((x0_ref, x1_ref)):
            rows = slice(m * T, (m + 1) * T)
            mid = x_ref[:, at].astype(F32) + y[rows]
            mid_ref[rows, at] = mid
            square[m] = square[m] + jnp.sum(mid * mid, axis=-1, keepdims=True)
    router_copy.wait()
    for m, hm_ref in enumerate((hm0_ref, hm1_ref)):
        rows = slice(m * T, (m + 1) * T)
        r = lax.rsqrt(square[m] * (1.0 / D) + EPS)
        hm_ref[:, :D] = (mid_ref[rows, :] * r * gain_ref[1:2, :]).astype(BF)
        logits = mm(hm_ref[:, :D], wr_s[...])
        chosen = chosen_ref[rows, :] > 0
        top = jnp.max(jnp.where(chosen, logits, -jnp.inf), axis=-1, keepdims=True)
        e = jnp.where(chosen, jnp.exp(jnp.minimum(logits - top, 0.0)), 0.0)
        gate = e / jnp.sum(e, axis=-1, keepdims=True)
        high = gate.astype(BF).astype(F32)
        hm_ref[:, D:] = (high + pltpu.roll(gate - high, N_EXPERTS, 1)).astype(BF)
        if save:
            for a in range(3):
                for i in range(8):
                    cut = slice(i * SLICE, (i + 1) * SLICE)
                    rows_of = hm_ref[:, cut] if a == 2 else (h_ref, att_ref)[a][rows, cut]
                    left_ref[i, rows, a * 256 : a * 256 + SLICE] = rows_of
                    left_ref[i, rows, a * 256 + SLICE : (a + 1) * 256] = jnp.zeros((T, 256 - SLICE), BF)


def attend(spots, q, kvs, allowed, x0, x1, w_o, w, gains, chosen, h_attn, save):
    more = [h_attn] if save else []
    return call(
        lambda *refs: attend_kernel(save, *refs), "attend", [q, kvs[0], allowed, x0, x1, gains, chosen, *more], [*w_o, w, *kvs[1:]],
        [sds((R, D), BF), sds((R, D), F32), sds((T, D + LANES), BF), sds((T, D + LANES), BF)] + [sds((8, R, 768), BF) for _ in more], [],
        [pltpu.VMEM((2, SEQ, 512), BF), pltpu.VMEM((D, D), BF), pltpu.VMEM((D, LANES), BF), pltpu.SemaphoreType.DMA((33,)),
         pltpu.SemaphoreType.DMA((2, 8))],
        7, 14, spots,
    )


FW = D + FF
GW = 2 * D
SLOTS = 3
WEIGHT_SLOTS = [pltpu.VMEM((SLOTS, D, 512), BF), pltpu.VMEM((SLOTS, 256, D), BF), pltpu.SemaphoreType.DMA((SLOTS, 3))]


def fetch_step(step, w_in, w_down, w_s, d_s, sems):
    e, f, slot = step // 3, step % 3, step % SLOTS
    return [
        fetch(w_in[e].at[:, f * 256 : (f + 1) * 256], w_s.at[slot, :, 0:256], sems.at[slot, 0]),
        fetch(w_in[e].at[:, FF + f * 256 : FF + (f + 1) * 256], w_s.at[slot, :, 256:512], sems.at[slot, 1]),
        fetch(w_down[e].at[f * 256 : (f + 1) * 256, :], d_s.at[slot], sems.at[slot, 2]),
    ]


def expert_kernel(save, *refs):
    own_ref, mine_ref, w_in, w_down, hm_refs, outs, rest = refs[0], refs[1], refs[2:4], refs[4:6], refs[6:9], refs[9:13], refs[13:]
    if save:
        g_ref, f_out, (gate_out, up_out, prod_out), rest = rest[0], rest[1:3], rest[3:6], rest[6:]
        (f_s, act_s, gate_s, up_s, prod_s, out_sems), rest = rest[:6], rest[6:]
        h_ref = f_s
    else:
        h_ref, g_ref, rest = rest[0], rest[1], rest[2:]
    lanes_s, hm_sems, acc, total, w_s, d_s, sems = rest
    arrive = []
    for i, b in enumerate(hm_refs, 1):
        at = slice(i * T, (i + 1) * T)
        arrive.append(fetch(b.at[:, :D], h_ref.at[at, :D], hm_sems.at[i, 0]))
        arrive.append(fetch(b.at[:, D:], lanes_s.at[at, :], hm_sems.at[i, 1]))
    copies = [fetch_step(step, w_in, w_down, w_s, d_s, sems) for step in range(SLOTS)]
    h_ref[0:T, :D] = own_ref[:, :D]
    lanes_s[0:T, :] = own_ref[:, D:]
    for copy in arrive:
        copy.wait()
    lanes = lanes_s[...].astype(F32)
    for e in range(2):
        g = jnp.sum(lanes * mine_ref[e : e + 1, :], axis=-1, keepdims=True)
        g_ref[e] = jnp.broadcast_to(g, (C, LANES))
    sent = []
    for step in range(6):
        e, f, slot = step // 3, step % 3, step % SLOTS
        for copy in copies[step]:
            copy.wait()
        both = mm(h_ref[:, :D], w_s[slot])
        gate, up = both[:, :256], both[:, 256:]
        act = (gate / (1.0 + jnp.exp(-gate)) * up).astype(BF)
        add = mm(act, d_s[slot])
        if save:
            cols = slice(f * 256, (f + 1) * 256)
            gate_s[e, :, cols] = gate
            up_s[e, :, cols] = up
            if e == 0:
                f_s[:, D + f * 256 : D + (f + 1) * 256] = act
            else:
                act_s[:, cols] = act
        if step + SLOTS < 6:
            copies.append(fetch_step(step + SLOTS, w_in, w_down, w_s, d_s, sems))
        if f == 0:
            acc[...] = add
        elif f == 1:
            acc[...] += add
        else:
            prod = (acc[...] + add).astype(BF)
            weighted = prod.astype(F32) * g_ref[e, :, 0:1]
            if save:
                prod_s[e] = prod
                sent.append(fetch(gate_s.at[e], gate_out.at[e], out_sems.at[e, 0]))
                sent.append(fetch(up_s.at[e], up_out.at[e], out_sems.at[e, 1]))
                sent.append(fetch(prod_s.at[e], prod_out.at[e], out_sems.at[e, 2]))
                if e == 0:
                    sent.append(fetch(f_s, f_out[0], out_sems.at[0, 3]))
                    sent.append(fetch(f_s.at[:, :D], f_out[1].at[:, :D], out_sems.at[0, 4]))
                else:
                    sent.append(fetch(act_s, f_out[1].at[:, D:], out_sems.at[1, 3]))
            if e == 0:
                total[...] = weighted
            else:
                part = (total[...] + weighted).astype(BF)
                for i, o in enumerate(outs):
                    o[...] = part[i * T : (i + 1) * T]
    for copy in sent:
        copy.wait()


def expert(hms, mine, w_in, w_down, save):
    outs, away = [sds((T, D), BF)] * 4, []
    scratch = [pltpu.VMEM((C, LANES), BF), pltpu.SemaphoreType.DMA((4, 2)), pltpu.VMEM((C, D), F32), pltpu.VMEM((C, D), F32)] + WEIGHT_SLOTS
    if save:
        outs = outs + [sds((2, C, LANES), F32)]
        away = [sds((C, FW), BF), sds((C, FW), BF), sds((2, C, FF), F32), sds((2, C, FF), F32), sds((2, C, D), BF)]
        scratch = [pltpu.VMEM((C, FF), BF) if i == 1 else pltpu.VMEM(o.shape, o.dtype) for i, o in enumerate(away)] + [pltpu.SemaphoreType.DMA((2, 5))] + scratch
    else:
        scratch = [pltpu.VMEM((C, D), BF), pltpu.VMEM((2, C, LANES), F32)] + scratch
    return call(
        lambda *refs: expert_kernel(save, *refs), "expert", [hms[0], mine], [*w_in, *w_down, *hms[1:]], outs, away, scratch,
        10 if save else 7.7, 24 if save else 16,
    )


def expert_back_kernel(save, *refs):
    own_ref, g_ref, put_ref, rest = refs[0], refs[1], refs[2], refs[3:]
    (gate_in, up_in, prod_in), w_in, w_down = rest[:3], rest[3:5], rest[5:7]
    g_in, outs, rest = rest[7:10], rest[10:14], rest[14:]
    if save:
        d_out, d_s, out_sems, rest = rest[:2], rest[2:4], rest[4], rest[5:]
    g_s, g_sems, lanes_s, dprod, gate_s, up_s, prod_s, in_sems, acc, total, w_s, d_w, sems = rest
    arrive = [fetch(b, g_s.at[i * T : (i + 1) * T, :], g_sems.at[i]) for i, b in enumerate(g_in, 1)]
    kept = [
        [fetch(src.at[e], dst.at[e], in_sems.at[e, i]) for i, (src, dst) in enumerate(((prod_in, prod_s), (gate_in, gate_s), (up_in, up_s)))]
        for e in range(2)
    ]
    copies = [fetch_step(step, w_in, w_down, w_s, d_w, sems) for step in range(SLOTS)]
    put = put_ref[...]
    g_s[0:T, :] = own_ref[...]
    for copy in arrive:
        copy.wait()
    sent = []
    for step in range(6):
        e, f, slot = step // 3, step % 3, step % SLOTS
        if f == 0:
            kept[e][0].wait()
            for i in range(4):
                at = slice(i * T, (i + 1) * T)
                g = g_s[at, :].astype(F32)
                d_prod = (g * g_ref[e, at, 0:1]).astype(BF)
                dprod[at, :] = d_prod
                if save:
                    d_s[e][at, D:] = d_prod
                d = jnp.sum(g * prod_s[e, at, :].astype(F32), axis=-1, keepdims=True)
                high = d.astype(BF).astype(F32)
                lanes = high * put[2 * e : 2 * e + 1, :] + (d - high) * put[2 * e + 1 : 2 * e + 2, :]
                lanes_s[at, :] = lanes if e == 0 else lanes_s[at, :] + lanes
            kept[e][1].wait()
            kept[e][2].wait()
        for copy in copies[step]:
            copy.wait()
        cols = slice(f * 256, (f + 1) * 256)
        d_act = mm(dprod[...], d_w[slot], NT)
        gate, up = gate_s[e, :, cols], up_s[e, :, cols]
        s = 1.0 / (1.0 + jnp.exp(-gate))
        dg = (d_act * up * (s * (1.0 + gate * (1.0 - s)))).astype(BF)
        du = (d_act * (gate * s)).astype(BF)
        if save:
            d_s[e][:, cols] = dg
            d_s[e][:, FF + f * 256 : FF + (f + 1) * 256] = du
        add = mm(jnp.concatenate([dg, du], axis=1), w_s[slot], NT)
        if step + SLOTS < 6:
            copies.append(fetch_step(step + SLOTS, w_in, w_down, w_s, d_w, sems))
        if f == 0:
            acc[...] = add
        elif f == 1:
            acc[...] += add
        else:
            rows_grad = (acc[...] + add).astype(BF).astype(F32)
            if save:
                sent.append(fetch(d_s[e], d_out[e], out_sems.at[e]))
            if e == 0:
                total[...] = rows_grad
            else:
                part = (total[...] + rows_grad).astype(BF)
                for i, o in enumerate(outs):
                    at = slice(i * T, (i + 1) * T)
                    o[:, :D] = part[at]
                    o[:, D:] = lanes_s[at, :].astype(BF)
    for copy in sent:
        copy.wait()


def expert_back(gs, kept, put, w_in, w_down, save):
    g_share, gate, up, produced = kept
    away, scratch = [], []
    if save:
        away = [sds((C, GW), BF)] * 2
        scratch = [pltpu.VMEM(o.shape, o.dtype) for o in away] + [pltpu.SemaphoreType.DMA((2,))]
    scratch = scratch + [
        pltpu.VMEM((C, D), BF), pltpu.SemaphoreType.DMA((4,)), pltpu.VMEM((C, LANES), F32), pltpu.VMEM((C, D), BF), pltpu.VMEM((2, C, FF), F32), pltpu.VMEM((2, C, FF), F32),
        pltpu.VMEM((2, C, D), BF), pltpu.SemaphoreType.DMA((2, 3)), pltpu.VMEM((C, D), F32), pltpu.VMEM((C, D), F32),
    ] + WEIGHT_SLOTS
    return call(
        lambda *refs: expert_back_kernel(save, *refs), "expert_back", [gs[0], g_share, put], [gate, up, produced, *w_in, *w_down, *gs[1:]],
        [sds((T, D + LANES), BF)] * 4, away, scratch, 12.5 if save else 11, 24,
    )


def norm_back(x, gain, grad):
    r = lax.rsqrt(jnp.mean(x * x, axis=-1, keepdims=True) + EPS)
    n = x * r
    scaled = grad * gain
    back = r * (scaled - n * jnp.mean(scaled * n, axis=-1, keepdims=True))
    return jnp.sum(grad * n, axis=0, keepdims=True), back


def mid_back_kernel(*refs):
    own_refs, g_refs, mid_ref, hm_refs, gain_ref, w_ref, far = refs[:2], refs[2:4], refs[4], refs[5:7], refs[7], refs[8], refs[9:15]
    dmid_ref, datt_ref, dl_ref, gain_out, wr_s, sem, far_s, sems = refs[15:]
    arrive = [fetch(b, far_s.at[i], sems.at[i]) for i, b in enumerate(far)]
    copy = fetch(w_ref.at[:, 2048:], wr_s, sem)
    grads = jnp.zeros((1, D), F32)
    for m in range(2):
        rows = slice(m * T, (m + 1) * T)
        total = own_refs[m][...].astype(F32)
        for i in range(3 * m, 3 * m + 3):
            arrive[i].wait()
            total = total + far_s[i].astype(F32)
        lanes = total[:, D:]
        d_gate = lanes + pltpu.roll(lanes, LANES - N_EXPERTS, 1)
        share = hm_refs[m][:, D:].astype(F32)
        gate = share + pltpu.roll(share, LANES - N_EXPERTS, 1)
        gate = jnp.where(lax.broadcasted_iota(jnp.int32, (T, LANES), 1) < N_EXPERTS, gate, 0.0)
        inner = jnp.sum(gate * d_gate, axis=-1, keepdims=True)
        d_logits = (gate * (d_gate - inner)).astype(BF)
        dl_ref[rows, :] = d_logits
        if m == 0:
            copy.wait()
        d_hm = total[:, :D] + mm(d_logits, wr_s[...], NT)
        grad_gain, back = norm_back(mid_ref[rows, :], gain_ref[1:2, :], d_hm)
        grads = grads + grad_gain
        d_mid = g_refs[m][...].astype(F32) + back
        dmid_ref[rows, :] = d_mid
        datt_ref[rows, :] = d_mid.astype(BF)
    gain_out[...] = jnp.broadcast_to(grads, (8, D))


def mid_back(rets, gs, mid, hms, gains, w):
    return call(
        mid_back_kernel, "mid_back", [rets[0], rets[4], *gs, mid, *hms, gains], [w, *rets[1:4], *rets[5:8]],
        [sds((R, D), F32), sds((R, D), BF), sds((R, LANES), BF), sds((8, D), F32)], [],
        [pltpu.VMEM((D, LANES), BF), pltpu.SemaphoreType.DMA, pltpu.VMEM((6, T, D + LANES), BF), pltpu.SemaphoreType.DMA((6,))],
        2.8, 8,
    )


def attn_back_kernel(*refs):
    spots_ref, datt_ref, q_ref, own_ref, allowed_ref, cos_ref, sin_ref = refs[:7]
    w_refs, kv_refs, rest = refs[7:15], (None,) + refs[15:22], refs[22:]
    dq_ref, same_ref, other_ref, da, kv_s, kv_acc, w_s, sems, kv_sems = rest
    copies = fetch_w_out(spots_ref, w_refs, w_s, sems)
    key_copies = fetch_keys(kv_refs, kv_s, kv_sems)
    own_keys(own_ref, kv_s)
    for copy in copies:
        copy.wait()
    for j in range(4):
        piece = mm(datt_ref[...], w_s[j * 384 : (j + 1) * 384, :], NT).astype(BF)
        for m in range(2):
            for i in range(3):
                da[m, j * 3 + i] = piece[m * T : (m + 1) * T, i * HS : (i + 1) * HS]
    for copy in key_copies:
        copy.wait()
    allowed = allowed_ref[...]
    cos, sin = cos_ref[:T, :], sin_ref[:T, :]
    for m in range(2):
        rows = slice(m * T, (m + 1) * T)
        for k in range(KV_HEADS):
            keys = kv_s[m, :, k * HS : (k + 1) * HS]
            values = kv_s[m, :, KW + k * HS : KW + (k + 1) * HS]
            q6 = heads_of(q_ref, m, k)
            d6 = da[m, k * GROUP : (k + 1) * GROUP].reshape(GROUP * T, HS)
            p = probs_of(q6, keys, allowed)
            dp = mm(d6, values, NT)
            ds = (p * (dp - jnp.sum(p * dp, axis=-1, keepdims=True)) * SCALE).astype(BF)
            dq = mm(ds, keys)
            for g in range(GROUP):
                h = k * GROUP + g
                dq_ref[rows, h * HS : (h + 1) * HS] = rope_back(dq[g * T : (g + 1) * T], cos, sin).astype(BF)
            kv_acc[:, k * HS : (k + 1) * HS] = mm(ds, q6, TN)
            kv_acc[:, KW + k * HS : KW + (k + 1) * HS] = mm(p.astype(BF), d6, TN)
        for i in range(4):
            at = slice(i * R + m * T, i * R + (m + 1) * T)
            same_ref[at, :] = kv_acc[i * T : (i + 1) * T].astype(BF)
            other_ref[at, :] = kv_acc[C + i * T : C + (i + 1) * T].astype(BF)


def attn_back(spots, d_att, w_o, q, kvs, allowed, cos, sin):
    return call(
        attn_back_kernel, "attn_back", [d_att, q, kvs[0], allowed, cos, sin], [*w_o, *kvs[1:]],
        [sds((R, D), BF), sds((4 * R, 512), BF), sds((4 * R, 512), BF)], [],
        [pltpu.VMEM((2, HEADS, T, HS), BF), pltpu.VMEM((2, SEQ, 512), BF), pltpu.VMEM((SEQ, 512), F32),
         pltpu.VMEM((D, D), BF), pltpu.SemaphoreType.DMA((32,)), pltpu.SemaphoreType.DMA((2, 8))],
        9, 16, spots,
    )


MSG = 512 + LANES


def qkv_back_kernel(*refs):
    own_ref, dq_ref, dl_ref, gm_ref, x0_ref, x1_ref, gain_ref, cos_ref, sin_ref, dmid_ref, w_ref = refs[:11]
    gin_ref, low0_ref, low1_ref, msg_ref, dh, w_s, sems, far_s, far_sems = refs[14:]
    arrive = [fetch(b, far_s.at[i], far_sems.at[i]) for i, b in enumerate(refs[11:14])]
    copies = [fetch(w_ref.at[j * 384 : (j + 1) * 384, 0:2048], w_s.at[j], sems.at[j]) for j in range(4)]
    d_kv = own_ref[...].astype(F32)
    for i in range(3):
        arrive[i].wait()
        d_kv = d_kv + far_s[i].astype(F32)
    cos, sin = cos_ref[...], sin_ref[...]
    for i in range(KV_HEADS):
        at = slice(i * HS, (i + 1) * HS)
        msg_ref[:R, at] = rope_back(d_kv[:, at], cos, sin).astype(BF)
    msg_ref[:R, KW:512] = d_kv[:, KW:].astype(BF)
    msg_ref[:R, 512:] = dl_ref[...]
    for j in range(4):
        copies[j].wait()
        dh[:, j * 384 : (j + 1) * 384] = mm(dq_ref[...], w_s[j, :, :D], NT) + mm(msg_ref[:R, :512], w_s[j, :, D:], NT)
    grads = jnp.zeros((1, D), F32)
    for m, (x_ref, low_ref) in enumerate(((x0_ref, low0_ref), (x1_ref, low1_ref))):
        rows = slice(m * T, (m + 1) * T)
        grad_gain, back = norm_back(x_ref[...].astype(F32), gain_ref[0:1, :], dh[rows])
        grads = grads + grad_gain
        g_in = dmid_ref[rows, :] + back
        gin_ref[rows, :] = g_in
        low_ref[...] = g_in.astype(BF)
    row = lax.broadcasted_iota(jnp.int32, (16, 512), 0)
    both = jnp.zeros((16, 512), F32)
    for c in range(3):
        at = slice(c * 512, (c + 1) * 512)
        both = jnp.where(row == c, jnp.broadcast_to(grads[:, at], (16, 512)), both)
        both = jnp.where(row == 3 + c, jnp.broadcast_to(gm_ref[0:1, at], (16, 512)), both)
    msg_ref[R:, :512] = both.astype(BF)
    msg_ref[R:, 512:] = jnp.zeros((16, LANES), BF)


def qkv_back(rets, dq, dl, gm, x0, x1, gains, w, cos, sin, d_mid):
    return call(
        qkv_back_kernel, "qkv_back", [rets[0], dq, dl, gm, x0, x1, gains, cos, sin, d_mid], [w, *rets[1:]],
        [sds((R, D), F32), sds((T, D), BF), sds((T, D), BF), sds((R + 16, MSG), BF)], [],
        [pltpu.VMEM((R, D), F32), pltpu.VMEM((4, 384, 2048), BF), pltpu.SemaphoreType.DMA((4,)),
         pltpu.VMEM((3, R, 512), BF), pltpu.SemaphoreType.DMA((3,))],
        6.2, 12,
    )


ROWS = SLICE + 16


def attn_grad_kernel(*refs):
    order_ref, left_ref, blocks, send_ref, (lh, rq, ro, rm, rg, sems) = refs[0], refs[1], refs[2:26], refs[26], refs[27:]
    left_copies, q_copies, o_copies, m_copies = [], [], [], []
    for i in range(8):
        at = slice(i * R, (i + 1) * R)
        left_copies.append(fetch(left_ref.at[order_ref[i]], lh.at[at, :], sems.at[0, i]))
        o_copies.append(fetch(blocks[16 + i], ro.at[at, :], sems.at[1, i]))
        q_copies.append(fetch(blocks[8 + i], rq.at[at, :], sems.at[2, i]))
        m_copies.append(fetch(blocks[i].at[:R, :], rm.at[at, :], sems.at[3, i]))
        m_copies.append(fetch(blocks[i].at[R:, :], rg.at[i], sems.at[4, i]))
    for copy in left_copies + o_copies:
        copy.wait()

    def spread(grads, width, lane):
        for r in range(8):
            send_ref[r, :SLICE, lane : lane + width] = grads[:SLICE, r * width : (r + 1) * width].astype(BF)

    spread(mm(lh[:, 256:512], ro[...], TN), SLICE, 320)
    for copy in q_copies:
        copy.wait()
    spread(mm(lh[:, :256], rq[...], TN), SLICE, 0)
    for copy in m_copies:
        copy.wait()
    spread(mm(lh[:, :256], rm[:, :512], TN), 64, SLICE)
    small = mm(lh[:, 512:], rm[:, 512:], TN)[:SLICE, :64].astype(BF)
    gains = sum(rg[i, :, :512].astype(F32) for i in range(8)).astype(BF)
    for r in range(8):
        send_ref[r, :SLICE, 256:320] = small
        send_ref[r, SLICE:, :] = gains


def attn_grad(order, left, msgs, dqs, datts):
    return pl.pallas_call(
        attn_grad_kernel,
        name="attn_grad",
        in_specs=[SCALARS] + [AWAY] * 25,
        out_specs=HERE,
        out_shape=sds((8, ROWS, 512), BF),
        scratch_shapes=[
            pltpu.VMEM((8 * R, 768), BF), pltpu.VMEM((8 * R, D), BF), pltpu.VMEM((8 * R, D), BF), pltpu.VMEM((8 * R, MSG), BF),
            pltpu.VMEM((8, 16, MSG), BF), pltpu.SemaphoreType.DMA((5, 8)),
        ],
        compiler_params=pltpu.CompilerParams(vmem_limit_bytes=20 * 2**20),
        cost_estimate=work(8.5),
    )(order, *in_hbm((left, *msgs, *dqs, *datts)))


def turn_kernel(*refs):
    lefts, (h_out, a_out, f_s, h_s, a_s, sems) = refs[:4], refs[4:]
    copies = [fetch(left, f_s.at[i], sems.at[i]) for i, left in enumerate(lefts)]
    for i in range(4):
        copies[i].wait()
        h_s[:, i * C : (i + 1) * C] = f_s[i, :, :D].T
        a_s[:, i * C : (i + 1) * C] = f_s[i, :, D:].T
    sent = [fetch(h_s, h_out, sems.at[4]), fetch(a_s, a_out, sems.at[5])]
    for copy in sent:
        copy.wait()


def turn(lefts):
    return call(
        turn_kernel, "turn", [], lefts, [], [sds((D, 4 * C), BF), sds((FF, 4 * C), BF)],
        [pltpu.VMEM((4, C, FW), BF), pltpu.VMEM((D, 4 * C), BF), pltpu.VMEM((FF, 4 * C), BF), pltpu.SemaphoreType.DMA((6,))],
        5, 14,
    )


def expert_grad_kernel(in_ref, down_ref, *refs):
    rights, out_ref, right = refs[:4], refs[4], refs[5]
    j = pl.program_id(0)
    for i in range(4):
        right[i * C : (i + 1) * C, :] = rights[i][...]

    def grads(left_ref, rows, first):
        for r in range(8):
            out_ref[r, first : first + rows, :] = mm(left_ref[r * rows : (r + 1) * rows, :], right[...]).astype(BF)

    @pl.when(j % 2 == 0)
    def _():
        grads(in_ref, SLICE, 0)

    @pl.when(j % 2 == 1)
    def _():
        grads(down_ref, SLICE // 2, SLICE)


def expert_grad(left_in, left_down, rights):
    return pl.pallas_call(
        expert_grad_kernel,
        name="expert_grad",
        grid=(12,),
        in_specs=[whole((D, 4 * C)), whole((FF, 4 * C))] + [pl.BlockSpec((C, 256), lambda j: (0, (j % 2) * 6 + j // 2))] * 4,
        out_specs=pl.BlockSpec((8, SLICE + SLICE // 2, 256), lambda j: (0, 0, j // 2)),
        out_shape=pltpu.HBM((8, SLICE + SLICE // 2, D), BF),
        scratch_shapes=[pltpu.VMEM((4 * C, 256), BF)],
        compiler_params=pltpu.CompilerParams(dimension_semantics=("arbitrary",), vmem_limit_bytes=VMEM),
        cost_estimate=work(20),
    )(*in_hbm((left_in, left_down, *rights)))


def body(tokens_in, cotangent, routes, gain_attn, w_query, w_keyval, w_out, gain_moe, w_router, w_in, w_down):
    is_first = lax.axis_index("section") == 0
    shard = lax.axis_index("shard")
    rep = lax.axis_index("rep")
    chip, core = shard // 2, shard % 2
    micros = range(2)

    extra = jnp.concatenate([w_router[0], gain_attn[0][:, None], gain_moe[0][:, None]], axis=1)
    extra = jnp.pad(extra, ((0, 0), (0, LANES - extra.shape[1])))
    packed = jnp.concatenate([w_query[0], w_keyval[0], extra], axis=1)
    w = lax.all_gather(packed, "shard", axis=0, tiled=True)
    pick = (jnp.arange(LANES)[None, :] == (jnp.arange(8)[:, None] + N_EXPERTS)) & (jnp.arange(8)[:, None] < 2)
    gains = mm(pick.astype(BF), w[:, 2048:], NT)
    z = rep // 2

    quarter = lax.dynamic_slice_in_dim(w_out[0], z * (SLICE // 4), SLICE // 4, 0)
    quarters = jnp.stack(from_chips(quarter))
    along_z = [quarters] + [lax.ppermute(quarters, "rep", [(i, ((i // 2 + k) % 4) * 2 + i % 2) for i in range(8)]) for k in (1, 2, 3)]
    w_o = along_z + [swap(piece) for piece in along_z]
    spots = [((chip - ky) % 4) * 2 * SLICE + c * SLICE + ((z - kz) % 4) * (SLICE // 4) for c in (core, 1 - core) for kz in range(4) for ky in range(4)]
    spots = jnp.stack(spots).astype(jnp.int32)

    inner = (w_in[0, 0], swap(w_in[0, 0]))
    outer = (w_down[0, 0], swap(w_down[0, 0]))
    w, gains, inner, outer = lax.optimization_barrier((w, gains, inner, outer))

    half = HS // 2
    frequency = ROPE_BASE ** (-jnp.arange(half, dtype=F32) * 2.0 / HS)
    place = shard * T + jnp.arange(T, dtype=jnp.int32)
    angles = place.astype(F32)[:, None] * frequency[None, :]
    angles = jnp.concatenate([angles, angles], axis=0)
    cos = jnp.concatenate([jnp.cos(angles)] * 2, axis=1)
    sin = jnp.concatenate([-jnp.sin(angles), jnp.sin(angles)], axis=1)
    order = jnp.stack([((chip - k) % 4) * 2 + c for c in (core, 1 - core) for k in range(4)]).astype(jnp.int32)
    key_place = (order[:, None] * T + jnp.arange(T, dtype=jnp.int32)[None, :]).reshape(1, SEQ)
    allowed = (key_place <= place[:, None]).astype(F32)
    lane = jnp.arange(LANES, dtype=jnp.int32)
    other = shard ^ 1
    mine = jnp.stack([(lane == e) | (lane == e + N_EXPERTS) for e in (shard, other)]).astype(F32)
    mine = jnp.pad(mine, ((0, 6), (0, 0)))
    put = jnp.stack([lane == shard, lane == shard + N_EXPERTS, lane == other, lane == other + N_EXPERTS]).astype(F32)
    put = jnp.pad(put, ((0, 4), (0, 0)))
    chosen = jnp.any(routes[0, :, 0].reshape(R, -1)[:, :, None] == lane[None, None, :], axis=1).astype(F32)

    hold = lax.optimization_barrier

    def layer(x, save):
        q, kv, h_attn = qkv(x[0], x[1], gains, w, cos, sin)
        kvs = gather_blocks(kv)
        att, mid, hm0, hm1, *left = attend(spots, q, kvs, allowed, x[0], x[1], w_o, w, gains, chosen, h_attn, save)
        hms = (hm0, hm1)
        first = from_chips(hm0)
        first, hm1 = hold((first, hm1))
        second = from_chips(hm1)
        out = expert(first, mine, inner, outer, save)
        second[0], _ = hold((second[0], out[0]))
        outs = [out, expert(second, mine, inner, outer, save)]
        return [out[:4] for out in outs], (x, q, kvs, mid, hms), [out[4:] for out in outs], left

    def finish(parts, mid):
        rets = [to_chips(part) for part in parts]
        return [(mid[m * T : (m + 1) * T] + sum(r.astype(F32) for r in rets[m])).astype(BF) for m in micros]

    def experts_back(blocks, more, save):
        rets, saved = [], []
        for m in micros:
            g_share, gate, up, produced = more[m][0], *more[m][3:]
            if m == 1:
                blocks[1][0], _ = hold((blocks[1][0], out[0]))
            out = expert_back(blocks[m], (g_share, gate, up, produced), put, inner, outer, save)
            rets += to_chips(out[:4])
            saved.append(out[4:])
        return rets, saved

    def keys_back(same, other):
        got = swap(other)
        return to_chips([plus(same[k * R : (k + 1) * R], got[k * R : (k + 1) * R]) for k in range(4)])

    tokens = [tokens_in[m, 0] for m in micros]
    given = [cotangent[m, 0] for m in micros]
    first, kept, *_ = layer(tokens, False)
    first = finish(first, kept[3])
    arrived = [lax.ppermute(first[m], "section", [(0, 1)]) for m in micros]
    arrived, given_first = hold((arrived, from_chips(given[0])))
    inputs = [jnp.where(is_first, tokens[m], arrived[m]) for m in micros]
    parts, kept, more, left = layer(inputs, True)
    (left,) = left
    f_own = [more[m][1] for m in micros]
    f_got = [swap(more[m][2]) for m in micros]

    x, q, kvs, mid, hms = kept
    left, _ = hold((left, parts[1]))
    left = lax.all_to_all(left, "shard", split_axis=0, concat_axis=0, tiled=True)
    rets, _ = experts_back([given_first, from_chips(given[1])], more, False)
    rets, f_got, left = hold((rets, f_got, left))
    d_mid, d_att, dl, gm = mid_back(rets, given, mid, hms, gains, w)
    dq, kv_same, kv_other = attn_back(spots, d_att, w_o, q, kvs, allowed, cos, sin)
    kv_rets, (h_turned, act_turned) = hold((keys_back(kv_same, kv_other), turn(f_own + f_got)))
    _, low0, low1, _ = qkv_back(kv_rets, dq, dl, gm, x[0], x[1], gains, w, cos, sin, d_mid)
    arrived = [lax.ppermute(low, "section", [(1, 0)]) for low in (low0, low1)]
    parts, _ = hold((parts, low0))
    acts = finish(parts, mid)
    arrived, acts = hold((arrived, acts))
    given = [jnp.where(is_first, arrived[m], given[m]) for m in micros]

    first = from_chips(given[0])
    first, second = hold((first, given[1]))
    rets, saved = experts_back([first, from_chips(second)], more, True)
    rights = [saved[m][0] for m in micros] + [swap(saved[m][1]) for m in micros]
    rets, send = hold((rets, expert_grad(h_turned, act_turned, rights)))
    expert_parts = lax.all_to_all(send, "rep", split_axis=0, concat_axis=0, tiled=True)
    d_mid, d_att, dl, gm = mid_back(rets, given, mid, hms, gains, w)
    datts = from_chips(d_att)
    dq, kv_same, kv_other = attn_back(spots, d_att, w_o, q, kvs, allowed, cos, sin)
    datts, kv_same, kv_other = hold((datts, kv_same, kv_other))
    kv_rets = keys_back(kv_same, kv_other)
    kv_rets, dq_sent = hold((kv_rets, dq))
    dqs = from_chips(dq_sent)
    g_in, _, _, msg = qkv_back(kv_rets, dq, dl, gm, x[0], x[1], gains, w, cos, sin, d_mid)

    msgs = from_chips(msg)
    dqs, msgs = hold((dqs, msgs))
    dqs, datts, msgs = (blocks + [swap(b) for b in blocks] for blocks in (dqs, datts, msgs))
    send = attn_grad(order, left, msgs, dqs, datts)
    expert_parts, send = hold((expert_parts, send))
    got = lax.all_to_all(send, "rep", split_axis=0, concat_axis=0, tiled=True)
    sums = jnp.sum(got.astype(F32), axis=0)
    g_q, g_kv, g_r, g_o = (sums[:SLICE, a:b] for a, b in ((0, 192), (192, 256), (256, 256 + N_EXPERTS), (320, 512)))
    g_gains = lax.dynamic_slice(sums[SLICE : SLICE + 6].reshape(2, D), (0, shard * SLICE), (2, SLICE))
    expert_sums = jnp.sum(expert_parts.astype(F32), axis=0)

    return (
        jnp.stack(acts)[None, :, None],
        g_in.reshape(1, 2, 1, T, D),
        g_gains[0:1],
        g_q[None],
        g_kv[None],
        g_o[None],
        g_gains[1:2],
        g_r[None],
        expert_sums[None, None, :SLICE],
        expert_sums[None, None, SLICE:],
    )


def solution(mesh):
    in_specs = (
        P(None, "rep", "shard", None),
        P(None, "rep", "shard", None),
        P("section", None, "rep", "shard", None),
        P("section", "shard"),
        P("section", "shard", None),
        P("section", "shard", None),
        P("section", "shard", None),
        P("section", "shard"),
        P("section", "shard", None),
        P("section", "shard", None, None),
        P("section", "shard", None, None),
    )
    out_specs = (
        P("section", None, "rep", "shard", None),
        P("section", None, "rep", "shard", None),
        P("section", "shard"),
        P("section", "shard", "rep"),
        P("section", "shard", "rep"),
        P("section", "shard", "rep"),
        P("section", "shard"),
        P("section", "shard", None),
        P("section", "shard", "rep", None),
        P("section", "shard", "rep", None),
    )
    return jax.shard_map(body, mesh=mesh, in_specs=in_specs, out_specs=out_specs, check_vma=False)
```

time: 722 us -> 557 us (0.77)
  local copies, waits for them, and re-layouts: 97.4 us -> 26.9 us
  waiting for transfers between devices: 243 us -> 189 us
  starting transfers between devices: 163 us -> 133 us
  Pallas kernels: 145 us -> 169 us
  other arithmetic: 31.5 us -> 13.1 us
  matrix products: 14.4 us -> 1.23 us
    all_gather x2 -> x1, waiting for transfers between devices: 54.6 us -> 0.01 us  [body(): w = lax.all_gather(packed, 'shard', axis=0, tiled=True)]
    all_to_all x2 -> x1, waiting for transfers between devices: 61.9 us -> 16.1 us  [body(): got = lax.all_to_all(send, 'rep', split_axis=0, concat_axis=0, tiled=True)]
    unnamed x491 -> x221, local copies, waits for them, and re-layouts: 66 us -> 21.1 us
    pallas_call x25 -> x21, Pallas kernels: 145 us -> 169 us  [the longest x19 143 us: call(): pl.pallas_call(kernel, name=name, in_specs=[SCALARS] * len(scalars) + [HE...]
    ppermute x84 -> x72, starting transfers between devices: 116 us -> 96.6 us  [along_y(): return lax.ppermute(x, 'shard', [(i, (i + 2 * k) % 8) for i in range(8)])]
    ppermute x2 -> x5, waiting for transfers between devices: 7.78 us -> 27 us  [the longest x3 24 us: body(): lax.ppermute(quarters, 'rep', [(i, (i // 2 + k) % 4 * 2 + i % 2) for i in...]
    ppermute x84 -> x72, waiting for transfers between devices: 114 us -> 132 us  [along_y(): return lax.ppermute(x, 'shard', [(i, (i + 2 * k) % 8) for i in range(8)])]
    reshape x16 -> x1, local copies, waits for them, and re-layouts: 17 us -> 0.01 us  [body(): sums[SLICE:SLICE + 6].reshape(2, D)]
  transfers between devices with their start and end apart: 169 -> 115, of which waited for: 47 -> 52; matrix products, arithmetic and copies ran while one was open for 9% -> 3% of each run, Pallas kernels for 20% -> 23%
where the time goes in v3:
time: 557 us; the launch traced here: 548 us
  waiting for transfers between devices  189 us (34%)
  Pallas kernels  169 us (30%)
  starting transfers between devices  133 us (24%)
  local copies, waits for them, and re-layouts  26.9 us (5%)
  between operations  16 us (3%)
  other arithmetic  13.1 us (2%)
    pallas_call x19, Pallas kernels, call(): pl.pallas_call(kernel, name=name, in_specs=[SCALARS] * len(scalars) + [HE...  143 us
    ppermute x72, waiting for transfers between devices, along_y(): return lax.ppermute(x, 'shard', [(i, (i + 2 * k) % 8) for i in range(8)])  132 us
    ppermute x72, starting transfers between devices, along_y(): return lax.ppermute(x, 'shard', [(i, (i + 2 * k) % 8) for i in range(8)])  96.6 us
    ppermute x3, waiting for transfers between devices, body(): lax.ppermute(quarters, 'rep', [(i, (i // 2 + k) % 4 * 2 + i % 2) for i in...  24 us
    unnamed x221, local copies, waits for them, and re-layouts  21.1 us
    pallas_call x1, Pallas kernels, expert_grad(): pl.pallas_call(expert_grad_kernel, name='expert_grad', grid=(12,), in_spe...  17.5 us
    all_to_all x1, waiting for transfers between devices, body(): got = lax.all_to_all(send, 'rep', split_axis=0, concat_axis=0, tiled=True)  16.1 us
  transfers between devices with their start and end apart: 115, of which 52 were waited for; matrix products, arithmetic and copies ran while one was open for 3% of the time, Pallas kernels for 23%

profile of v3, /device:TPU:0, one launch (start us, length us, event | category | flops | bytes accessed | tf_op | source)
XLA Modules:
  0.0 547.8 jit_solution(1203539544131979294)
XLA Ops:
  16.2 5.4 collective-permute-done.4
  34.7 10.2 %collective-permute-done.5.refs_9_.refs_10_.refs_8_ = bf16[4,48,1536]{2,1,0:T(8,128)(2,1)} collective-permute-done((bf16[4,48,1536]{2,1,0:T(8,128)(2,1)}, bf16[4,48,1536]{2,1,0:T(8,128)(2,1)}, u32[]{:S(2)}, u32[]{:S(2)}) %collective-permute-start.5) | collective-permute-done | bytes 589856 | tf_op jit(solution)/shard_map/ppermute | solution.py:693
  44.9 13.8 %collective-permute-done.6.refs_10_.refs_11_.refs_9_ = bf16[4,48,1536]{2,1,0:T(8,128)(2,1)} collective-permute-done((bf16[4,48,1536]{2,1,0:T(8,128)(2,1)}, bf16[4,48,1536]{2,1,0:T(8,128)(2,1)}, u32[]{:S(2)}, u32[]{:S(2)}) %collective-permute-start.6) | collective-permute-done | bytes 589856 | tf_op jit(solution)/shard_map/ppermute | solution.py:693
  68.5 6.4 %collective-permute-done.12.refs_17_ = bf16[128,512]{1,0:T(8,128)(2,1)S(1)} collective-permute-done((bf16[128,512]{1,0:T(8,128)(2,1)S(1)}, bf16[128,512]{1,0:T(8,128)(2,1)S(1)}, u32[]{:S(2)}, u32[]{:S(2)}) %collective-permute-start.12) | collective-permute-done | bytes 131104 | tf_op jit(solution)/shard_map/ppermute | solution.py:84
  77.6 6.9 %attend.2 = (bf16[128,1536]{1,0:T(8,128)(2,1)}, f32[128,1536]{1,0:T(8,128)S(1)}, bf16[64,1664]{1,0:T(8,128)(2,1)S(1)}, bf16[64,1664]{1,0:T(8,128)(2,1)S(1)}) custom-call(s32[32]{0:T(128)S(1)} %stack.192.refs_0_, bf16[128,1536]{1,0:T(8,128)(2,1)S(1)} %get-tuple-element.183.refs_1_, bf16[128,512]{1,0:T(8,128)(2,1)S(1)} %get-tuple-element.184.refs_2_, ...), custom_call_target="tpu_custom_call" | custom-call | flops 1 | bytes 25900000 | tf_op jit(solution)/shard_map/attend/pallas_call | solution.py:61
  93.3 5.2 collective-permute-done.20.refs_7_
  102.8 7.8 %expert.4 = (bf16[64,1536]{1,0:T(8,128)(2,1)S(1)}, bf16[64,1536]{1,0:T(8,128)(2,1)S(1)}, bf16[64,1536]{1,0:T(8,128)(2,1)S(1)}, bf16[64,1536]{1,0:T(8,128)(2,1)S(1)}) custom-call(bf16[64,1664]{1,0:T(8,128)(2,1)S(1)} %get-tuple-element.188.refs_0_, f32[8,128]{1,0:T(8,128)S(1)} %pad_convert_fusion.1.refs_1_, bf16[1536,1536]{1,0:T(8,128)(2,1)} %bitcast.92, ...), custom_call_target="tpu_custom_call" | custom-call | flops 1 | bytes 28490000 | tf_op jit(solution)/shard_map/expert/pallas_call | solution.py:61
  116.8 7.8 %expert.5 = (bf16[64,1536]{1,0:T(8,128)(2,1)S(1)}, bf16[64,1536]{1,0:T(8,128)(2,1)S(1)}, bf16[64,1536]{1,0:T(8,128)(2,1)S(1)}, bf16[64,1536]{1,0:T(8,128)(2,1)S(1)}) custom-call(bf16[64,1664]{1,0:T(8,128)(2,1)S(1)} %get-tuple-element.201.refs_0_, f32[8,128]{1,0:T(8,128)S(1)} %pad_convert_fusion.1.refs_1_, bf16[1536,1536]{1,0:T(8,128)(2,1)} %bitcast.93, ...), custom_call_target="tpu_custom_call" | custom-call | flops 1 | bytes 28490000 | tf_op jit(solution)/shard_map/expert/pallas_call | solution.py:61
  131.0 6.9 %collective-permute-done.31 = bf16[64,1536]{1,0:T(8,128)(2,1)S(1)} collective-permute-done((bf16[64,1536]{1,0:T(8,128)(2,1)S(1)}, bf16[64,1536]{1,0:T(8,128)(2,1)S(1)}, u32[]{:S(2)}, u32[]{:S(2)}) %collective-permute-start.31) | collective-permute-done | bytes 196640 | tf_op jit(solution)/shard_map/ppermute | solution.py:84
  166.4 6.9 %attend.3 = (bf16[128,1536]{1,0:T(8,128)(2,1)}, f32[128,1536]{1,0:T(8,128)S(1)}, bf16[64,1664]{1,0:T(8,128)(2,1)S(1)}, bf16[64,1664]{1,0:T(8,128)(2,1)S(1)}, bf16[8,128,768]{2,1,0:T(8,128)(2,1)S(1)}) custom-call(s32[32]{0:T(128)S(1)} %stack.192.refs_0_, bf16[128,1536]{1,0:T(8,128)(2,1)S(1)} %get-tuple-element.209.refs_1_.refs_2_, ...), custom_call_target="tpu_custom_call" | custom-call | flops 1 | bytes 25900000 | tf_op jit(solution)/shard_map/attend/pallas_call | solution.py:61
  178.9 8.8 %collective-permute-done.43.refs_6_ = bf16[64,1664]{1,0:T(8,128)(2,1)S(1)} collective-permute-done((bf16[64,1664]{1,0:T(8,128)(2,1)S(1)}, bf16[64,1664]{1,0:T(8,128)(2,1)S(1)}, u32[]{:S(2)}, u32[]{:S(2)}) %collective-permute-start.43) | collective-permute-done | bytes 213024 | tf_op jit(solution)/shard_map/ppermute | solution.py:84
  193.2 10.0 %expert.6 = (bf16[64,1536]{1,0:T(8,128)(2,1)S(1)}, bf16[64,1536]{1,0:T(8,128)(2,1)S(1)}, bf16[64,1536]{1,0:T(8,128)(2,1)S(1)}, bf16[64,1536]{1,0:T(8,128)(2,1)S(...) custom-call(bf16[64,1664]{1,0:T(8,128)(2,1)S(1)} %get-tuple-element., ...), custom_call_target="tpu_custom_call" | custom-call | flops 1 | bytes 37000000 | tf_op jit(solution)/shard_map/expert/pallas_call | solution.py:61
  206.7 10.0 %expert.7 = (bf16[64,1536]{1,0:T(8,128)(2,1)S(1)}, bf16[64,1536]{1,0:T(8,128)(2,1)S(1)}, bf16[64,1536]{1,0:T(8,128)(2,1)S(1)}, bf16[64,1536]{1,0:T(8,128)(2,1)S(...) custom-call(bf16[64,1664]{1,0:T(8,128)(2,1)S(1)} %get-tuple-element., ...), custom_call_target="tpu_custom_call" | custom-call | flops 1 | bytes 37000000 | tf_op jit(solution)/shard_map/expert/pallas_call | solution.py:61
  230.4 11.0 %expert_back.4 = (bf16[64,1664]{1,0:T(8,128)(2,1)S(1)}, bf16[64,1664]{1,0:T(8,128)(2,1)S(1)}, bf16[64,1664]{1,0:T(8,128)(2,1)S(1)}, bf16[64,1664]{1,0:T(8,128)(2,1)S(1)}) custom-call(bf16[64,1536]{1,0:T(8,128)(2,1)S(1)} %get-tuple-element.206.refs_0_.refs_2_, f32[2,256,128]{2,1,0:T(8,128)S(1)} %get-tuple-element.218.refs_1_, ...), custom_call_target="tpu_custom_call" | custom-call | flops 1 | bytes 40700000 | tf_op jit(solution)/shard_map/expert_back/pallas_call | solution.py:61
  241.5 7.7 %collective-permute-done.52.refs_10_ = bf16[64,1536]{1,0:T(8,128)(2,1)S(1)} collective-permute-done((bf16[64,1536]{1,0:T(8,128)(2,1)S(1)}, bf16[64,1536]{1,0:T(8,128)(2,1)S(1)}, u32[]{:S(2)}, u32[]{:S(2)}) %collective-permute-start.52) | collective-permute-done | bytes 196640 | tf_op jit(solution)/shard_map/ppermute | solution.py:84
  254.6 11.0 %expert_back.5 = (bf16[64,1664]{1,0:T(8,128)(2,1)S(1)}, bf16[64,1664]{1,0:T(8,128)(2,1)S(1)}, bf16[64,1664]{1,0:T(8,128)(2,1)S(1)}, bf16[64,1664]{1,0:T(8,128)(2,1)S(1)}) custom-call(bf16[64,1536]{1,0:T(8,128)(2,1)S(1)} %get-tuple-element.229.refs_0_.refs_3_, f32[2,256,128]{2,1,0:T(8,128)S(1)} %get-tuple-element.233.refs_1_, ...), custom_call_target="tpu_custom_call" | custom-call | flops 1 | bytes 40700000 | tf_op jit(solution)/shard_map/expert_back/pallas_call | solution.py:61
  271.2 6.3 %collective-permute-done.55.refs_12_ = bf16[64,1664]{1,0:T(8,128)(2,1)S(1)} collective-permute-done((bf16[64,1664]{1,0:T(8,128)(2,1)S(1)}, bf16[64,1664]{1,0:T(8,128)(2,1)S(1)}, u32[]{:S(2)}, u32[]{:S(2)}) %collective-permute-start.55) | collective-permute-done | bytes 213024 | tf_op jit(solution)/shard_map/ppermute | solution.py:84
  286.5 8.9 %attn_back.2 = (bf16[128,1536]{1,0:T(8,128)(2,1)S(1)}, bf16[512,512]{1,0:T(8,128)(2,1)S(1)}, bf16[512,512]{1,0:T(8,128)(2,1)S(1)}) custom-call(s32[32]{0:T(128)S(1)} %stack.192.refs_0_, bf16[128,1536]{1,0:T(8,128)(2,1)S(1)} %get-tuple-element.258.refs_1_, bf16[128,1536]{1,0:T(8,128)(2,1)S(1)} %get-tuple-element.209.refs_1_.refs_2_, ...), custom_call_target="tpu_custom_call" | custom-call | flops 1 | bytes 33300000 | tf_op jit(solution)/shard_map/attn_back/pallas_call | solution.py:61
  308.4 6.3 %qkv_back.2 = (f32[128,1536]{1,0:T(8,128)}, bf16[64,1536]{1,0:T(8,128)(2,1)S(1)}, bf16[64,1536]{1,0:T(8,128)(2,1)S(1)}, bf16[144,640]{1,0:T(8,128)(2,1)}) custom-call(bf16[128,512]{1,0:T(8,128)(2,1)S(1)} %get-tuple-element.267.refs_0_, bf16[128,1536]{1,0:T(8,128)(2,1)S(1)} %get-tuple-element.268.refs_1_, bf16[128,128]{1,0:T(8,128)(2,1)S(1)} %get-tuple-element.269.refs_2_, ...), custom_call_target="tpu_custom_call" | custom-call | flops 1 | bytes 22940000 | tf_op jit(solution)/shard_map/qkv_back/pallas_call | solution.py:61
  321.4 6.4 %collective-permute-done.71 = bf16[64,1536]{1,0:T(8,128)(2,1)S(1)} collective-permute-done((bf16[64,1536]{1,0:T(8,128)(2,1)S(1)}, bf16[64,1536]{1,0:T(8,128)(2,1)S(1)}, u32[]{:S(2)}, u32[]{:S(2)}) %collective-permute-start.71) | collective-permute-done | bytes 196640 | tf_op jit(solution)/shard_map/ppermute | solution.py:84
  355.3 11.9 %expert_back.6 = (bf16[64,1664]{1,0:T(8,128)(2,1)S(1)}, bf16[64,1664]{1,0:T(8,128)(2,1)S(1)}, bf16[64,1664]{1,0:T(8,128)(2,1)S(1)}, bf16[64,1664]{1,0:T(8,128)(2...) custom-call(bf16[64,1536]{1,0:T(8,128)(2,1)S(1)} %get-tuple-element.292.refs_0_.refs_2_, ...), custom_call_target="tpu_custom_call" | custom-call | flops 1 | bytes 46250000 | tf_op jit(solution)/shard_map/expert_back/pallas_call | solution.py:61
  369.0 11.9 %expert_back.7 = (bf16[64,1664]{1,0:T(8,128)(2,1)S(1)}, bf16[64,1664]{1,0:T(8,128)(2,1)S(1)}, bf16[64,1664]{1,0:T(8,128)(2,1)S(1)}, bf16[64,1664]{1,0:T(8,128)(2...) custom-call(bf16[64,1536]{1,0:T(8,128)(2,1)S(1)} %get-tuple-element.301.refs_0_.refs_3_, ...), custom_call_target="tpu_custom_call" | custom-call | flops 1 | bytes 46250000 | tf_op jit(solution)/shard_map/expert_back/pallas_call | solution.py:61
  394.3 17.5 %expert_grad.1 = bf16[8,288,1536]{2,1,0:T(8,128)(2,1)} custom-call(bf16[1536,1024]{1,0:T(8,128)(2,1)} %get-tuple-element.306.in_ref, bf16[768,1024]{1,0:T(8,128)(2,1)} %get-tuple-element.307.down_ref, bf16[256,3072]{1,0:T(8,128)(2,1)} %get-tuple-element.308.refs_0_, bf16[256,3072]{1,0:T(8,128)(2,1)} %get-tuple-element.309.refs_1_, ...), custom_call_target="tpu_custom_call" | custom-call | flops 1 | bytes 74000000 | tf_op jit(solution)/shard_map/expert_grad/pallas_call | solution.py:663
  413.4 5.0 all-to-all-start.1
  425.5 8.8 %attn_back.3 = (bf16[128,1536]{1,0:T(8,128)(2,1)S(1)}, bf16[512,512]{1,0:T(8,128)(2,1)S(1)}, bf16[512,512]{1,0:T(8,128)(2,1)S(1)}) custom-call(s32[32]{0:T(128)S(1)} %stack.192.refs_0_, bf16[128,1536]{1,0:T(8,128)(2,1)S(1)} %get-tuple-element.346.refs_1_.refs_18_, bf16[128,1536]{1,0:T(8,128)(2,1)S(1)} %get-tuple-element.209.refs_1_.refs_2_, ...), custom_call_target="tpu_custom_call" | custom-call | flops 1 | bytes 33300000 | tf_op jit(solution)/shard_map/attn_back/pallas_call | solution.py:61
  434.7 5.0 collective-permute-done.87.refs_20_
  456.7 6.2 %qkv_back.3 = (f32[128,1536]{1,0:T(8,128)}, bf16[64,1536]{1,0:T(8,128)(2,1)}, bf16[64,1536]{1,0:T(8,128)(2,1)}, bf16[144,640]{1,0:T(8,128)(2,1)S(1)}) custom-call(bf16[128,512]{1,0:T(8,128)(2,1)S(1)} %get-tuple-element.326.refs_0_, bf16[128,1536]{1,0:T(8,128)(2,1)S(1)} %get-tuple-element.342.refs_1_.refs_10_, ...), custom_call_target="tpu_custom_call" | custom-call | flops 1 | bytes 22940000 | tf_op jit(solution)/shard_map/qkv_back/pallas_call | solution.py:61
  467.8 15.6 %collective-permute-done.96.refs_3_ = bf16[144,640]{1,0:T(8,128)(2,1)S(1)} collective-permute-done((bf16[144,640]{1,0:T(8,128)(2,1)S(1)}, bf16[144,640]{1,0:T(8,128)(2,1)S(1)}, u32[]{:S(2)}, u32[]{:S(2)}) %collective-permute-start.96) | collective-permute-done | bytes 184352 | tf_op jit(solution)/shard_map/ppermute | solution.py:84
  484.6 9.2 %collective-permute-done.95.refs_13_ = bf16[128,1536]{1,0:T(8,128)(2,1)S(1)} collective-permute-done((bf16[128,1536]{1,0:T(8,128)(2,1)S(1)}, bf16[128,1536]{1,0:T(8,128)(2,1)S(1)}, u32[]{:S(2)}, u32[]{:S(2)}) %collective-permute-start.95) | collective-permute-done | bytes 393248 | tf_op jit(solution)/shard_map/ppermute | solution.py:84
  500.6 8.4 %attn_grad.1 = bf16[8,208,512]{2,1,0:T(8,128)(2,1)} custom-call(s32[8]{0:T(128)S(1)} %stack.201.refs_0_, bf16[8,128,768]{2,1,0:T(8,128)(2,1)} %all-to-all-done.refs_1_, bf16[144,640]{1,0:T(8,128)(2,1)} %copy-done.15, bf16[144,640]{1,0:T(8,128)(2,1)} %copy-done.90, bf16[144,640]{1,0:T(8,128)(2,1)} %copy-done.91, ...), custom_call_target="tpu_custom_call" | custom-call | flops 1 | bytes 31450000 | tf_op jit(solution)/shard_map/attn_grad/pallas_call | solution.py:608
  509.0 5.2 all-to-all-start.2
  521.2 16.1 %all-to-all-done.2 = bf16[8,208,512]{2,1,0:T(8,128)(2,1)S(1)} async-done(((bf16[8,208,512]{2,1,0:T(8,128)(2,1)}), bf16[8,208,512]{2,1,0:T(8,128)(2,1)S(1)}, u32[]{:S(2)}, u32[]{:S(2)}) %all-to-all-start.2) | async-done | bytes 1703968 | tf_op jit(solution)/shard_map/all_to_all | solution.py:801
  (491 shorter events, 247.2 us)
Async XLA Ops:
  7.2 52.8 %all-gather.2.cloned.1.call-start = ((), (), s32[]{:S(2)}) async-start(), calls=%async_computation.3 | async-start | bytes 7520256 | tf_op jit(solution)/shard_map/all_gather | solution.py:686
  10.4 50.8 %collective-permute-start = (bf16[1536,1536]{1,0:T(8,128)(2,1)}, bf16[1536,1536]{1,0:T(8,128)(2,1)}, u32[]{:S(2)}, u32[]{:S(2)}) collective-permute-start(bf16[1536,1536]{1,0:T(8,128)(2,1)} %bitcast.91), channel_id=1, source_target_pairs={{0,1},{1,0},{2,3},{3,2},{4,5},{5,4},{6,7},{7,6},{8,9},{9,8},{10,11... | collective-permute-start | bytes 14155784 | tf_op jit(solution)/shard_map/ppermute | solution.py:80
  15.9 43.9 %collective-permute-start.1 = (bf16[768,1536]{1,0:T(8,128)(2,1)S(1)}, bf16[768,1536]{1,0:T(8,128)(2,1)}, u32[]{:S(2)}, u32[]{:S(2)}) collective-permute-start(bf16[768,1536]{1,0:T(8,128)(2,1)S(1)} %bitcast.108), channel_id=1, source_target_pairs={{0,1},{1,0},{2,3},{3,2},{4,5},{5,4},{6,7},{7,6},{8,9},{9,8},{10,11... | collective-permute-start | bytes 7077896 | tf_op jit(solution)/shard_map/ppermute | solution.py:80
  27.0 17.9 %collective-permute-start.5 = (bf16[4,48,1536]{2,1,0:T(8,128)(2,1)}, bf16[4,48,1536]{2,1,0:T(8,128)(2,1)}, u32[]{:S(2)}, u32[]{:S(2)}) collective-permute-start(bf16[4,48,1536]{2,1,0:T(8,128)(2,1)} %pad_maximum_fusion.refs_8_.refs_9_.refs_7_), channel_id=1, source_target_pairs={{0,16},{8,24},{16,32},{24,40},{32,48},{40,56},{48,0},{56,8},{1,17}... | collective-permute-start | bytes 1769480 | tf_op jit(solution)/shard_map/ppermute | solution.py:693
  29.0 29.8 %collective-permute-start.6 = (bf16[4,48,1536]{2,1,0:T(8,128)(2,1)}, bf16[4,48,1536]{2,1,0:T(8,128)(2,1)}, u32[]{:S(2)}, u32[]{:S(2)}) collective-permute-start(bf16[4,48,1536]{2,1,0:T(8,128)(2,1)} %pad_maximum_fusion.refs_8_.refs_9_.refs_7_), channel_id=1, source_target_pairs={{0,32},{8,40},{16,48},{24,56},{32,0},{40,8},{48,16},{56,24},{1,33}... | collective-permute-start | bytes 1769480 | tf_op jit(solution)/shard_map/ppermute | solution.py:693
  32.6 26.4 %collective-permute-start.7 = (bf16[4,48,1536]{2,1,0:T(8,128)(2,1)}, bf16[4,48,1536]{2,1,0:T(8,128)(2,1)}, u32[]{:S(2)}, u32[]{:S(2)}) collective-permute-start(bf16[4,48,1536]{2,1,0:T(8,128)(2,1)} %pad_maximum_fusion.refs_8_.refs_9_.refs_7_), channel_id=1, source_target_pairs={{0,48},{8,56},{16,0},{24,8},{32,16},{40,24},{48,32},{56,40},{1,49}... | collective-permute-start | bytes 1769480 | tf_op jit(solution)/shard_map/ppermute | solution.py:693
  44.9 20.1 %collective-permute-start.8 = (bf16[4,48,1536]{2,1,0:T(8,128)(2,1)}, bf16[4,48,1536]{2,1,0:T(8,128)(2,1)}, u32[]{:S(2)}, u32[]{:S(2)}) collective-permute-start(bf16[4,48,1536]{2,1,0:T(8,128)(2,1)} %pad_maximum_fusion.refs_8_.refs_9_.refs_7_), channel_id=1, source_target_pairs={{0,1},{1,0},{2,3},{3,2},{4,5},{5,4},{6,7},{7,6},{8,9},{9,8},{10,11... | collective-permute-start | bytes 1769480 | tf_op jit(solution)/shard_map/ppermute | solution.py:80
  110.5 16.8 %collective-permute-start.24 = (bf16[64,1536]{1,0:T(8,128)(2,1)S(1)}, bf16[64,1536]{1,0:T(8,128)(2,1)S(1)}, u32[]{:S(2)}, u32[]{:S(2)}) collective-permute-start(bf16[64,1536]{1,0:T(8,128)(2,1)S(1)} %get-tuple-element.199), channel_id=1, source_target_pairs={{0,2},{1,3},{2,4},{3,5},{4,6},{5,7},{6,0},{7,1},{8,10},{9,11},{10,... | collective-permute-start | bytes 589832 | tf_op jit(solution)/shard_map/ppermute | solution.py:84
  128.7 17.5 %collective-permute-start.33 = (bf16[64,1536]{1,0:T(8,128)(2,1)S(1)}, bf16[64,1536]{1,0:T(8,128)(2,1)S(1)}, u32[]{:S(2)}, u32[]{:S(2)}) collective-permute-start(bf16[64,1536]{1,0:T(8,128)(2,1)S(1)} %get-tuple-element.206.refs_0_.refs_2_), channel_id=1, source_target_pairs={{0,2},{1,3},{2,4},{3,5},{4,6},{5,7},{6,0},{7,1},{8,10},{9,11},{10,... | collective-permute-start | bytes 589832 | tf_op jit(solution)/shard_map/ppermute | solution.py:84
  188.3 16.9 %collective-permute-start.49 = (bf16[64,1664]{1,0:T(8,128)(2,1)S(1)}, bf16[64,1664]{1,0:T(8,128)(2,1)S(1)}, u32[]{:S(2)}, u32[]{:S(2)}) collective-permute-start(bf16[64,1664]{1,0:T(8,128)(2,1)S(1)} %get-tuple-element.232.refs_0_.refs_6_), channel_id=1, source_target_pairs={{0,2},{1,3},{2,4},{3,5},{4,6},{5,7},{6,0},{7,1},{8,10},{9,11},{10,... | collective-permute-start | bytes 638984 | tf_op jit(solution)/shard_map/ppermute | solution.py:84
  219.4 62.6 %all-to-all-start = ((bf16[8,128,768]{2,1,0:T(8,128)(2,1)}), bf16[8,128,768]{2,1,0:T(8,128)(2,1)}, u32[]{:S(2)}, u32[]{:S(2)}) async-start(bf16[8,128,768]{2,1,0:T(8,128)(2,1)} %copy-done.4), calls=%async_computation | async-start | bytes 3145728 | tf_op jit(solution)/shard_map/all_to_all | solution.py:768
  223.7 57.6 %collective-permute-start.58 = (bf16[256,2304]{1,0:T(8,128)(2,1)}, bf16[256,2304]{1,0:T(8,128)(2,1)}, u32[]{:S(2)}, u32[]{:S(2)}) collective-permute-start(bf16[256,2304]{1,0:T(8,128)(2,1)} %get-tuple-element.241), channel_id=1, source_target_pairs={{0,1},{1,0},{2,3},{3,2},{4,5},{5,4},{6,7},{7,6},{8,9},{9,8},{10,11... | collective-permute-start | bytes 3538952 | tf_op jit(solution)/shard_map/ppermute | solution.py:80
  224.1 57.9 %collective-permute-start.59 = (bf16[256,2304]{1,0:T(8,128)(2,1)}, bf16[256,2304]{1,0:T(8,128)(2,1)}, u32[]{:S(2)}, u32[]{:S(2)}) collective-permute-start(bf16[256,2304]{1,0:T(8,128)(2,1)} %get-tuple-element.242), channel_id=1, source_target_pairs={{0,1},{1,0},{2,3},{3,2},{4,5},{5,4},{6,7},{7,6},{8,9},{9,8},{10,11... | collective-permute-start | bytes 3538952 | tf_op jit(solution)/shard_map/ppermute | solution.py:80
  224.3 25.0 %collective-permute-start.52 = (bf16[64,1536]{1,0:T(8,128)(2,1)S(1)}, bf16[64,1536]{1,0:T(8,128)(2,1)S(1)}, u32[]{:S(2)}, u32[]{:S(2)}) collective-permute-start(bf16[64,1536]{1,0:T(8,128)(2,1)S(1)} %get-tuple-element.229.refs_0_.refs_3_), channel_id=1, source_target_pairs={{0,2},{1,3},{2,4},{3,5},{4,6},{5,7},{6,0},{7,1},{8,10},{9,11},{10,... | collective-permute-start | bytes 589832 | tf_op jit(solution)/shard_map/ppermute | solution.py:84
  226.1 27.5 %collective-permute-start.53 = (bf16[64,1536]{1,0:T(8,128)(2,1)S(1)}, bf16[64,1536]{1,0:T(8,128)(2,1)S(1)}, u32[]{:S(2)}, u32[]{:S(2)}) collective-permute-start(bf16[64,1536]{1,0:T(8,128)(2,1)S(1)} %get-tuple-element.229.refs_0_.refs_3_), channel_id=1, source_target_pairs={{0,4},{1,5},{2,6},{3,7},{4,0},{5,1},{6,2},{7,3},{8,12},{9,13},{10,... | collective-permute-start | bytes 589832 | tf_op jit(solution)/shard_map/ppermute | solution.py:84
  228.8 25.2 %collective-permute-start.54 = (bf16[64,1536]{1,0:T(8,128)(2,1)S(1)}, bf16[64,1536]{1,0:T(8,128)(2,1)S(1)}, u32[]{:S(2)}, u32[]{:S(2)}) collective-permute-start(bf16[64,1536]{1,0:T(8,128)(2,1)S(1)} %get-tuple-element.229.refs_0_.refs_3_), channel_id=1, source_target_pairs={{0,6},{1,7},{2,0},{3,1},{4,2},{5,3},{6,4},{7,5},{8,14},{9,15},{10,... | collective-permute-start | bytes 589832 | tf_op jit(solution)/shard_map/ppermute | solution.py:84
  249.2 17.2 %collective-permute-start.46 = (bf16[64,1664]{1,0:T(8,128)(2,1)S(1)}, bf16[64,1664]{1,0:T(8,128)(2,1)S(1)}, u32[]{:S(2)}, u32[]{:S(2)}) collective-permute-start(bf16[64,1664]{1,0:T(8,128)(2,1)S(1)} %get-tuple-element.226), channel_id=1, source_target_pairs={{0,6},{1,7},{2,0},{3,1},{4,2},{5,3},{6,4},{7,5},{8,14},{9,15},{10,... | collective-permute-start | bytes 638984 | tf_op jit(solution)/shard_map/ppermute | solution.py:84
  254.0 17.0 %collective-permute-start.48 = (bf16[64,1664]{1,0:T(8,128)(2,1)S(1)}, bf16[64,1664]{1,0:T(8,128)(2,1)S(1)}, u32[]{:S(2)}, u32[]{:S(2)}) collective-permute-start(bf16[64,1664]{1,0:T(8,128)(2,1)S(1)} %get-tuple-element.228), channel_id=1, source_target_pairs={{0,2},{1,3},{2,4},{3,5},{4,6},{5,7},{6,0},{7,1},{8,10},{9,11},{10,... | collective-permute-start | bytes 638984 | tf_op jit(solution)/shard_map/ppermute | solution.py:84
  367.3 23.6 %collective-permute-start.84 = (bf16[256,3072]{1,0:T(8,128)(2,1)}, bf16[256,3072]{1,0:T(8,128)(2,1)S(1)}, u32[]{:S(2)}, u32[]{:S(2)}) collective-permute-start(bf16[256,3072]{1,0:T(8,128)(2,1)} %get-tuple-element.310), channel_id=1, source_target_pairs={{0,1},{1,0},{2,3},{3,2},{4,5},{5,4},{6,7},{7,6},{8,9},{9,8},{10,11... | collective-permute-start | bytes 4718600 | tf_op jit(solution)/shard_map/ppermute | solution.py:80
  382.2 29.6 %collective-permute-start.76 = (bf16[64,1664]{1,0:T(8,128)(2,1)S(1)}, bf16[64,1664]{1,0:T(8,128)(2,1)S(1)}, u32[]{:S(2)}, u32[]{:S(2)}) collective-permute-start(bf16[64,1664]{1,0:T(8,128)(2,1)S(1)} %get-tuple-element.298), channel_id=1, source_target_pairs={{0,4},{1,5},{2,6},{3,7},{4,0},{5,1},{6,2},{7,3},{8,12},{9,13},{10,... | collective-permute-start | bytes 638984 | tf_op jit(solution)/shard_map/ppermute | solution.py:84
  385.0 26.9 %collective-permute-start.77 = (bf16[64,1664]{1,0:T(8,128)(2,1)S(1)}, bf16[64,1664]{1,0:T(8,128)(2,1)S(1)}, u32[]{:S(2)}, u32[]{:S(2)}) collective-permute-start(bf16[64,1664]{1,0:T(8,128)(2,1)S(1)} %get-tuple-element.299), channel_id=1, source_target_pairs={{0,2},{1,3},{2,4},{3,5},{4,6},{5,7},{6,0},{7,1},{8,10},{9,11},{10,... | collective-permute-start | bytes 638984 | tf_op jit(solution)/shard_map/ppermute | solution.py:84
  389.5 22.4 %collective-permute-start.81 = (bf16[64,1664]{1,0:T(8,128)(2,1)S(1)}, bf16[64,1664]{1,0:T(8,128)(2,1)S(1)}, u32[]{:S(2)}, u32[]{:S(2)}) collective-permute-start(bf16[64,1664]{1,0:T(8,128)(2,1)S(1)} %get-tuple-element.303), channel_id=1, source_target_pairs={{0,6},{1,7},{2,0},{3,1},{4,2},{5,3},{6,4},{7,5},{8,14},{9,15},{10,... | collective-permute-start | bytes 638984 | tf_op jit(solution)/shard_map/ppermute | solution.py:84
  390.9 21.0 %collective-permute-start.82 = (bf16[64,1664]{1,0:T(8,128)(2,1)S(1)}, bf16[64,1664]{1,0:T(8,128)(2,1)S(1)}, u32[]{:S(2)}, u32[]{:S(2)}) collective-permute-start(bf16[64,1664]{1,0:T(8,128)(2,1)S(1)} %get-tuple-element.304), channel_id=1, source_target_pairs={{0,4},{1,5},{2,6},{3,7},{4,0},{5,1},{6,2},{7,3},{8,12},{9,13},{10,... | collective-permute-start | bytes 638984 | tf_op jit(solution)/shard_map/ppermute | solution.py:84
  393.1 18.8 %collective-permute-start.83 = (bf16[64,1664]{1,0:T(8,128)(2,1)S(1)}, bf16[64,1664]{1,0:T(8,128)(2,1)S(1)}, u32[]{:S(2)}, u32[]{:S(2)}) collective-permute-start(bf16[64,1664]{1,0:T(8,128)(2,1)S(1)} %get-tuple-element.305), channel_id=1, source_target_pairs={{0,2},{1,3},{2,4},{3,5},{4,6},{5,7},{6,0},{7,1},{8,10},{9,11},{10,... | collective-permute-start | bytes 638984 | tf_op jit(solution)/shard_map/ppermute | solution.py:84
  413.4 95.6 %all-to-all-start.1 = ((bf16[8,288,1536]{2,1,0:T(8,128)(2,1)}), bf16[8,288,1536]{2,1,0:T(8,128)(2,1)}, u32[]{:S(2)}, u32[]{:S(2)}) async-start(bf16[8,288,1536]{2,1,0:T(8,128)(2,1)} %expert_grad.1), calls=%async_computation.1 | async-start | bytes 14155776 | tf_op jit(solution)/shard_map/all_to_all | solution.py:786
  421.3 18.4 %collective-permute-start.87 = (bf16[128,1536]{1,0:T(8,128)(2,1)S(1)}, bf16[128,1536]{1,0:T(8,128)(2,1)S(1)}, u32[]{:S(2)}, u32[]{:S(2)}) collective-permute-start(bf16[128,1536]{1,0:T(8,128)(2,1)S(1)} %get-tuple-element.346.refs_1_.refs_18_), channel_id=1, source_target_pairs={{0,4},{1,5},{2,6},{3,7},{4,0},{5,1},{6,2},{7,3},{8,12},{9,13},{10,... | collective-permute-start | bytes 1179656 | tf_op jit(solution)/shard_map/ppermute | solution.py:84
  454.6 29.3 %collective-permute-start.93 = (bf16[128,1536]{1,0:T(8,128)(2,1)S(1)}, bf16[128,1536]{1,0:T(8,128)(2,1)S(1)}, u32[]{:S(2)}, u32[]{:S(2)}) collective-permute-start(bf16[128,1536]{1,0:T(8,128)(2,1)S(1)} %get-tuple-element.342.refs_1_.refs_10_), channel_id=1, source_target_pairs={{0,2},{1,3},{2,4},{3,5},{4,6},{5,7},{6,0},{7,1},{8,10},{9,11},{10,... | collective-permute-start | bytes 1179656 | tf_op jit(solution)/shard_map/ppermute | solution.py:84
  454.6 29.5 %collective-permute-start.94 = (bf16[128,1536]{1,0:T(8,128)(2,1)S(1)}, bf16[128,1536]{1,0:T(8,128)(2,1)}, u32[]{:S(2)}, u32[]{:S(2)}) collective-permute-start(bf16[128,1536]{1,0:T(8,128)(2,1)S(1)} %get-tuple-element.342.refs_1_.refs_10_), channel_id=1, source_target_pairs={{0,4},{1,5},{2,6},{3,7},{4,0},{5,1},{6,2},{7,3},{8,12},{9,13},{10,... | collective-permute-start | bytes 1179656 | tf_op jit(solution)/shard_map/ppermute | solution.py:84
  462.9 20.5 %collective-permute-start.96 = (bf16[144,640]{1,0:T(8,128)(2,1)S(1)}, bf16[144,640]{1,0:T(8,128)(2,1)S(1)}, u32[]{:S(2)}, u32[]{:S(2)}) collective-permute-start(bf16[144,640]{1,0:T(8,128)(2,1)S(1)} %get-tuple-element.338.refs_2_), channel_id=1, source_target_pairs={{0,2},{1,3},{2,4},{3,5},{4,6},{5,7},{6,0},{7,1},{8,10},{9,11},{10,... | collective-permute-start | bytes 552968 | tf_op jit(solution)/shard_map/ppermute | solution.py:84
  465.0 18.3 %collective-permute-start.97 = (bf16[144,640]{1,0:T(8,128)(2,1)S(1)}, bf16[144,640]{1,0:T(8,128)(2,1)S(1)}, u32[]{:S(2)}, u32[]{:S(2)}) collective-permute-start(bf16[144,640]{1,0:T(8,128)(2,1)S(1)} %get-tuple-element.338.refs_2_), channel_id=1, source_target_pairs={{0,4},{1,5},{2,6},{3,7},{4,0},{5,1},{6,2},{7,3},{8,12},{9,13},{10,... | collective-permute-start | bytes 552968 | tf_op jit(solution)/shard_map/ppermute | solution.py:84
  465.7 17.7 %collective-permute-start.98 = (bf16[144,640]{1,0:T(8,128)(2,1)S(1)}, bf16[144,640]{1,0:T(8,128)(2,1)}, u32[]{:S(2)}, u32[]{:S(2)}) collective-permute-start(bf16[144,640]{1,0:T(8,128)(2,1)S(1)} %get-tuple-element.338.refs_2_), channel_id=1, source_target_pairs={{0,6},{1,7},{2,0},{3,1},{4,2},{5,3},{6,4},{7,5},{8,14},{9,15},{10,... | collective-permute-start | bytes 552968 | tf_op jit(solution)/shard_map/ppermute | solution.py:84
  509.0 28.2 %all-to-all-start.2 = ((bf16[8,208,512]{2,1,0:T(8,128)(2,1)}), bf16[8,208,512]{2,1,0:T(8,128)(2,1)S(1)}, u32[]{:S(2)}, u32[]{:S(2)}) async-start(bf16[8,208,512]{2,1,0:T(8,128)(2,1)} %attn_grad.1), calls=%async_computation.2 | async-start | bytes 3407872 | tf_op jit(solution)/shard_map/all_to_all | solution.py:801
  (192 other events, 1685.2 us)
Sparse Core Ops, SparseCore 0:
  10.5 45.0 all-gather.1

commit v4 on v3

--- a/solution.py
+++ b/solution.py
@@ -9,6 +9,7 @@
 T = 64
 R = 2 * T
 C = 4 * T
+B = 4 * R
 HEADS = 12
 KV_HEADS = 2
 GROUP = HEADS // KV_HEADS
@@ -23,7 +24,7 @@
 ROPE_BASE = 1000000.0
 SCALE = HS**-0.5
 BF = jnp.bfloat16
-VMEM = 24 * 2**20
+VMEM = 18 * 2**20
 F32 = jnp.float32
 
 NN = (((1,), (0,)), ((), ()))
@@ -86,6 +87,12 @@
 
 def from_chips(x):
     return [x, along_y(x, 1), along_y(x, 2), along_y(x, 3)]
+
+
+def halves_from_chips(lo, hi):
+    near_lo, over_hi = along_y(lo, 1), along_y(hi, 3)
+    far_lo, far_hi = along_y(near_lo, 1), along_y(over_hi, 3)
+    return [lo, hi, near_lo, along_y(hi, 1), far_lo, far_hi, along_y(lo, 3), over_hi]
 
 
 def to_chips(blocks):
@@ -135,7 +142,7 @@
         qkv_kernel, "qkv", [x0, x1, gains, cos, sin], [w],
         [sds((R, D), BF), sds((R, 512), BF), sds((R, D), BF)], [],
         [pltpu.VMEM((4, D, 512), BF), pltpu.SemaphoreType.DMA((4,))],
-        3.5, 10,
+        3.5, 8,
     )
 
 
@@ -232,10 +239,10 @@
     more = [h_attn] if save else []
     return call(
         lambda *refs: attend_kernel(save, *refs), "attend", [q, kvs[0], allowed, x0, x1, gains, chosen, *more], [*w_o, w, *kvs[1:]],
-        [sds((R, D), BF), sds((R, D), F32), sds((T, D + LANES), BF), sds((T, D + LANES), BF)] + [sds((8, R, 768), BF) for _ in more], [],
+        [sds((R, D), BF), sds((R, D), F32)] + [sds((T, D + LANES), BF)] * 2 + [sds((8, R, 768), BF) for _ in more], [],
         [pltpu.VMEM((2, SEQ, 512), BF), pltpu.VMEM((D, D), BF), pltpu.VMEM((D, LANES), BF), pltpu.SemaphoreType.DMA((33,)),
          pltpu.SemaphoreType.DMA((2, 8))],
-        7, 14, spots,
+        7, 11, spots,
     )
 
 
@@ -254,8 +261,10 @@
     ]
 
 
-def expert_kernel(save, *refs):
-    own_ref, mine_ref, w_in, w_down, hm_refs, outs, rest = refs[0], refs[1], refs[2:4], refs[4:6], refs[6:9], refs[9:13], refs[13:]
+def expert_kernel(own, save, *refs):
+    own_refs, refs = refs[:own], refs[own:]
+    mine_ref, w_in, w_down, hm_refs, refs = refs[0], refs[1:3], refs[3:5], refs[5 : 5 + 3 * own], refs[5 + 3 * own :]
+    outs, rest = refs[:4], refs[4:]
     if save:
         g_ref, f_out, (gate_out, up_out, prod_out), rest = rest[0], rest[1:3], rest[3:6], rest[6:]
         (f_s, act_s, gate_s, up_s, prod_s, out_sems), rest = rest[:6], rest[6:]
@@ -263,20 +272,22 @@
     else:
         h_ref, g_ref, rest = rest[0], rest[1], rest[2:]
     lanes_s, hm_sems, acc, total, w_s, d_s, sems = rest
+    n = own_refs[0].shape[0]
     arrive = []
-    for i, b in enumerate(hm_refs, 1):
-        at = slice(i * T, (i + 1) * T)
+    for i, b in enumerate(hm_refs, own):
+        at = slice(i * n, (i + 1) * n)
         arrive.append(fetch(b.at[:, :D], h_ref.at[at, :D], hm_sems.at[i, 0]))
         arrive.append(fetch(b.at[:, D:], lanes_s.at[at, :], hm_sems.at[i, 1]))
     copies = [fetch_step(step, w_in, w_down, w_s, d_s, sems) for step in range(SLOTS)]
-    h_ref[0:T, :D] = own_ref[:, :D]
-    lanes_s[0:T, :] = own_ref[:, D:]
+    for i, b in enumerate(own_refs):
+        h_ref[i * n : (i + 1) * n, :D] = b[:, :D]
+        lanes_s[i * n : (i + 1) * n, :] = b[:, D:]
     for copy in arrive:
         copy.wait()
     lanes = lanes_s[...].astype(F32)
     for e in range(2):
         g = jnp.sum(lanes * mine_ref[e : e + 1, :], axis=-1, keepdims=True)
-        g_ref[e] = jnp.broadcast_to(g, (C, LANES))
+        g_ref[e] = jnp.broadcast_to(g, (4 * own * n, LANES))
     sent = []
     for step in range(6):
         e, f, slot = step // 3, step % 3, step % SLOTS
@@ -288,8 +299,8 @@
         add = mm(act, d_s[slot])
         if save:
             cols = slice(f * 256, (f + 1) * 256)
-            gate_s[e, :, cols] = gate
-            up_s[e, :, cols] = up
+            gate_s[e, :, cols] = gate.astype(BF)
+            up_s[e, :, cols] = up.astype(BF)
             if e == 0:
                 f_s[:, D + f * 256 : D + (f + 1) * 256] = act
             else:
@@ -318,41 +329,47 @@
             else:
                 part = (total[...] + weighted).astype(BF)
                 for i, o in enumerate(outs):
-                    o[...] = part[i * T : (i + 1) * T]
+                    o[...] = part[i * own * n : (i + 1) * own * n]
     for copy in sent:
         copy.wait()
 
 
 def expert(hms, mine, w_in, w_down, save):
-    outs, away = [sds((T, D), BF)] * 4, []
-    scratch = [pltpu.VMEM((C, LANES), BF), pltpu.SemaphoreType.DMA((4, 2)), pltpu.VMEM((C, D), F32), pltpu.VMEM((C, D), F32)] + WEIGHT_SLOTS
+    own, n = len(hms) // 4, hms[0].shape[0]
+    rows = len(hms) * n
+    outs, away = [sds((own * n, D), BF)] * 4, []
+    scratch = [pltpu.VMEM((rows, LANES), BF), pltpu.SemaphoreType.DMA((8, 2)), pltpu.VMEM((rows, D), F32), pltpu.VMEM((rows, D), F32)] + WEIGHT_SLOTS
     if save:
-        outs = outs + [sds((2, C, LANES), F32)]
-        away = [sds((C, FW), BF), sds((C, FW), BF), sds((2, C, FF), F32), sds((2, C, FF), F32), sds((2, C, D), BF)]
-        scratch = [pltpu.VMEM((C, FF), BF) if i == 1 else pltpu.VMEM(o.shape, o.dtype) for i, o in enumerate(away)] + [pltpu.SemaphoreType.DMA((2, 5))] + scratch
+        outs = outs + [sds((2, rows, LANES), F32)]
+        away = [sds((rows, FW), BF), sds((rows, FW), BF), sds((2, rows, FF), BF), sds((2, rows, FF), BF), sds((2, rows, D), BF)]
+        scratch = [pltpu.VMEM((rows, FF), BF) if i == 1 else pltpu.VMEM(o.shape, o.dtype) for i, o in enumerate(away)] + [pltpu.SemaphoreType.DMA((2, 5))] + scratch
     else:
-        scratch = [pltpu.VMEM((C, D), BF), pltpu.VMEM((2, C, LANES), F32)] + scratch
+        scratch = [pltpu.VMEM((rows, D), BF), pltpu.VMEM((2, rows, LANES), F32)] + scratch
     return call(
-        lambda *refs: expert_kernel(save, *refs), "expert", [hms[0], mine], [*w_in, *w_down, *hms[1:]], outs, away, scratch,
-        10 if save else 7.7, 24 if save else 16,
-    )
-
-
-def expert_back_kernel(save, *refs):
-    own_ref, g_ref, put_ref, rest = refs[0], refs[1], refs[2], refs[3:]
+        lambda *refs: expert_kernel(own, save, *refs), "expert", [*hms[:own], mine], [*w_in, *w_down, *hms[own:]], outs, away, scratch,
+        14 if save else 7.7, 34 if save else 12,
+    )
+
+
+def expert_back_kernel(own, save, *refs):
+    own_refs, refs = refs[:own], refs[own:]
+    g_ref, put_ref, rest = refs[0], refs[1], refs[2:]
     (gate_in, up_in, prod_in), w_in, w_down = rest[:3], rest[3:5], rest[5:7]
-    g_in, outs, rest = rest[7:10], rest[10:14], rest[14:]
+    g_in, rest = rest[7 : 7 + 3 * own], rest[7 + 3 * own :]
+    outs, rest = rest[:4], rest[4:]
     if save:
         d_out, d_s, out_sems, rest = rest[:2], rest[2:4], rest[4], rest[5:]
     g_s, g_sems, lanes_s, dprod, gate_s, up_s, prod_s, in_sems, acc, total, w_s, d_w, sems = rest
-    arrive = [fetch(b, g_s.at[i * T : (i + 1) * T, :], g_sems.at[i]) for i, b in enumerate(g_in, 1)]
+    n = own_refs[0].shape[0]
+    arrive = [fetch(b, g_s.at[i * n : (i + 1) * n, :], g_sems.at[i]) for i, b in enumerate(g_in, own)]
     kept = [
         [fetch(src.at[e], dst.at[e], in_sems.at[e, i]) for i, (src, dst) in enumerate(((prod_in, prod_s), (gate_in, gate_s), (up_in, up_s)))]
         for e in range(2)
     ]
     copies = [fetch_step(step, w_in, w_down, w_s, d_w, sems) for step in range(SLOTS)]
     put = put_ref[...]
-    g_s[0:T, :] = own_ref[...]
+    for i, b in enumerate(own_refs):
+        g_s[i * n : (i + 1) * n, :] = b[...]
     for copy in arrive:
         copy.wait()
     sent = []
@@ -360,7 +377,7 @@
         e, f, slot = step // 3, step % 3, step % SLOTS
         if f == 0:
             kept[e][0].wait()
-            for i in range(4):
+            for i in range(8):
                 at = slice(i * T, (i + 1) * T)
                 g = g_s[at, :].astype(F32)
                 d_prod = (g * g_ref[e, at, 0:1]).astype(BF)
@@ -377,7 +394,7 @@
             copy.wait()
         cols = slice(f * 256, (f + 1) * 256)
         d_act = mm(dprod[...], d_w[slot], NT)
-        gate, up = gate_s[e, :, cols], up_s[e, :, cols]
+        gate, up = gate_s[e, :, cols].astype(F32), up_s[e, :, cols].astype(F32)
         s = 1.0 / (1.0 + jnp.exp(-gate))
         dg = (d_act * up * (s * (1.0 + gate * (1.0 - s)))).astype(BF)
         du = (d_act * (gate * s)).astype(BF)
@@ -396,11 +413,11 @@
             if save:
                 sent.append(fetch(d_s[e], d_out[e], out_sems.at[e]))
             if e == 0:
-                total[...] = rows_grad
+                total[...] = rows_grad.astype(BF)
             else:
-                part = (total[...] + rows_grad).astype(BF)
+                part = (total[...].astype(F32) + rows_grad).astype(BF)
                 for i, o in enumerate(outs):
-                    at = slice(i * T, (i + 1) * T)
+                    at = slice(i * R, (i + 1) * R)
                     o[:, :D] = part[at]
                     o[:, D:] = lanes_s[at, :].astype(BF)
     for copy in sent:
@@ -409,17 +426,18 @@
 
 def expert_back(gs, kept, put, w_in, w_down, save):
     g_share, gate, up, produced = kept
+    own, rows = len(gs) // 4, B
     away, scratch = [], []
     if save:
-        away = [sds((C, GW), BF)] * 2
+        away = [sds((rows, GW), BF)] * 2
         scratch = [pltpu.VMEM(o.shape, o.dtype) for o in away] + [pltpu.SemaphoreType.DMA((2,))]
     scratch = scratch + [
-        pltpu.VMEM((C, D), BF), pltpu.SemaphoreType.DMA((4,)), pltpu.VMEM((C, LANES), F32), pltpu.VMEM((C, D), BF), pltpu.VMEM((2, C, FF), F32), pltpu.VMEM((2, C, FF), F32),
-        pltpu.VMEM((2, C, D), BF), pltpu.SemaphoreType.DMA((2, 3)), pltpu.VMEM((C, D), F32), pltpu.VMEM((C, D), F32),
+        pltpu.VMEM((rows, D), BF), pltpu.SemaphoreType.DMA((8,)), pltpu.VMEM((rows, LANES), F32), pltpu.VMEM((rows, D), BF), pltpu.VMEM((2, rows, FF), BF), pltpu.VMEM((2, rows, FF), BF),
+        pltpu.VMEM((2, rows, D), BF), pltpu.SemaphoreType.DMA((2, 3)), pltpu.VMEM((rows, D), F32), pltpu.VMEM((rows, D), BF),
     ] + WEIGHT_SLOTS
     return call(
-        lambda *refs: expert_back_kernel(save, *refs), "expert_back", [gs[0], g_share, put], [gate, up, produced, *w_in, *w_down, *gs[1:]],
-        [sds((T, D + LANES), BF)] * 4, away, scratch, 12.5 if save else 11, 24,
+        lambda *refs: expert_back_kernel(own, save, *refs), "expert_back", [*gs[:own], g_share, put], [gate, up, produced, *w_in, *w_down, *gs[own:]],
+        [sds((R, D + LANES), BF)] * 4, away, scratch, 17 if save else 15, 36 if save else 30,
     )
 
 
@@ -432,17 +450,18 @@
 
 
 def mid_back_kernel(*refs):
-    own_refs, g_refs, mid_ref, hm_refs, gain_ref, w_ref, far = refs[:2], refs[2:4], refs[4], refs[5:7], refs[7], refs[8], refs[9:15]
-    dmid_ref, datt_ref, dl_ref, gain_out, wr_s, sem, far_s, sems = refs[15:]
+    own_ref, g_ref, mid_ref, hm_refs, gain_ref, w_ref, far = *refs[:3], refs[3:5], refs[5], refs[6], refs[7:10]
+    dmid_ref, datt0_ref, datt1_ref, dl_ref, gain_out, wr_s, sem, far_s, sems = refs[10:]
     arrive = [fetch(b, far_s.at[i], sems.at[i]) for i, b in enumerate(far)]
     copy = fetch(w_ref.at[:, 2048:], wr_s, sem)
     grads = jnp.zeros((1, D), F32)
     for m in range(2):
         rows = slice(m * T, (m + 1) * T)
-        total = own_refs[m][...].astype(F32)
-        for i in range(3 * m, 3 * m + 3):
-            arrive[i].wait()
-            total = total + far_s[i].astype(F32)
+        total = own_ref[rows, :].astype(F32)
+        for i in range(3):
+            if m == 0:
+                arrive[i].wait()
+            total = total + far_s[i, rows, :].astype(F32)
         lanes = total[:, D:]
         d_gate = lanes + pltpu.roll(lanes, LANES - N_EXPERTS, 1)
         share = hm_refs[m][:, D:].astype(F32)
@@ -456,32 +475,33 @@
         d_hm = total[:, :D] + mm(d_logits, wr_s[...], NT)
         grad_gain, back = norm_back(mid_ref[rows, :], gain_ref[1:2, :], d_hm)
         grads = grads + grad_gain
-        d_mid = g_refs[m][...].astype(F32) + back
+        d_mid = g_ref[rows, :].astype(F32) + back
         dmid_ref[rows, :] = d_mid
-        datt_ref[rows, :] = d_mid.astype(BF)
+        (datt0_ref, datt1_ref)[m][...] = d_mid.astype(BF)
     gain_out[...] = jnp.broadcast_to(grads, (8, D))
 
 
-def mid_back(rets, gs, mid, hms, gains, w):
+def mid_back(rets, g, mid, hms, gains, w):
     return call(
-        mid_back_kernel, "mid_back", [rets[0], rets[4], *gs, mid, *hms, gains], [w, *rets[1:4], *rets[5:8]],
-        [sds((R, D), F32), sds((R, D), BF), sds((R, LANES), BF), sds((8, D), F32)], [],
-        [pltpu.VMEM((D, LANES), BF), pltpu.SemaphoreType.DMA, pltpu.VMEM((6, T, D + LANES), BF), pltpu.SemaphoreType.DMA((6,))],
-        2.8, 8,
+        mid_back_kernel, "mid_back", [rets[0], g, mid, *hms, gains], [w, *rets[1:]],
+        [sds((R, D), F32), sds((T, D), BF), sds((T, D), BF), sds((R, LANES), BF), sds((8, D), F32)], [],
+        [pltpu.VMEM((D, LANES), BF), pltpu.SemaphoreType.DMA, pltpu.VMEM((3, R, D + LANES), BF), pltpu.SemaphoreType.DMA((3,))],
+        2.8, 4,
     )
 
 
 def attn_back_kernel(*refs):
-    spots_ref, datt_ref, q_ref, own_ref, allowed_ref, cos_ref, sin_ref = refs[:7]
-    w_refs, kv_refs, rest = refs[7:15], (None,) + refs[15:22], refs[22:]
-    dq_ref, same_ref, other_ref, da, kv_s, kv_acc, w_s, sems, kv_sems = rest
+    spots_ref, datt0_ref, datt1_ref, q_ref, own_ref, allowed_ref, cos_ref, sin_ref = refs[:8]
+    w_refs, kv_refs, rest = refs[8:16], (None,) + refs[16:23], refs[23:]
+    dq0_ref, dq1_ref, same_ref, other_ref, da, kv_s, kv_acc, w_s, sems, kv_sems = rest
     copies = fetch_w_out(spots_ref, w_refs, w_s, sems)
     key_copies = fetch_keys(kv_refs, kv_s, kv_sems)
     own_keys(own_ref, kv_s)
+    d_att = jnp.concatenate([datt0_ref[...], datt1_ref[...]], axis=0)
     for copy in copies:
         copy.wait()
     for j in range(4):
-        piece = mm(datt_ref[...], w_s[j * 384 : (j + 1) * 384, :], NT).astype(BF)
+        piece = mm(d_att, w_s[j * 384 : (j + 1) * 384, :], NT).astype(BF)
         for m in range(2):
             for i in range(3):
                 da[m, j * 3 + i] = piece[m * T : (m + 1) * T, i * HS : (i + 1) * HS]
@@ -502,7 +522,7 @@
             dq = mm(ds, keys)
             for g in range(GROUP):
                 h = k * GROUP + g
-                dq_ref[rows, h * HS : (h + 1) * HS] = rope_back(dq[g * T : (g + 1) * T], cos, sin).astype(BF)
+                (dq0_ref, dq1_ref)[m][:, h * HS : (h + 1) * HS] = rope_back(dq[g * T : (g + 1) * T], cos, sin).astype(BF)
             kv_acc[:, k * HS : (k + 1) * HS] = mm(ds, q6, TN)
             kv_acc[:, KW + k * HS : KW + (k + 1) * HS] = mm(p.astype(BF), d6, TN)
         for i in range(4):
@@ -511,13 +531,13 @@
             other_ref[at, :] = kv_acc[C + i * T : C + (i + 1) * T].astype(BF)
 
 
-def attn_back(spots, d_att, w_o, q, kvs, allowed, cos, sin):
+def attn_back(spots, d_atts, w_o, q, kvs, allowed, cos, sin):
     return call(
-        attn_back_kernel, "attn_back", [d_att, q, kvs[0], allowed, cos, sin], [*w_o, *kvs[1:]],
-        [sds((R, D), BF), sds((4 * R, 512), BF), sds((4 * R, 512), BF)], [],
+        attn_back_kernel, "attn_back", [*d_atts, q, kvs[0], allowed, cos, sin], [*w_o, *kvs[1:]],
+        [sds((T, D), BF), sds((T, D), BF), sds((4 * R, 512), BF), sds((4 * R, 512), BF)], [],
         [pltpu.VMEM((2, HEADS, T, HS), BF), pltpu.VMEM((2, SEQ, 512), BF), pltpu.VMEM((SEQ, 512), F32),
          pltpu.VMEM((D, D), BF), pltpu.SemaphoreType.DMA((32,)), pltpu.SemaphoreType.DMA((2, 8))],
-        9, 16, spots,
+        9, 12, spots,
     )
 
 
@@ -525,9 +545,9 @@
 
 
 def qkv_back_kernel(*refs):
-    own_ref, dq_ref, dl_ref, gm_ref, x0_ref, x1_ref, gain_ref, cos_ref, sin_ref, dmid_ref, w_ref = refs[:11]
-    gin_ref, low0_ref, low1_ref, msg_ref, dh, w_s, sems, far_s, far_sems = refs[14:]
-    arrive = [fetch(b, far_s.at[i], far_sems.at[i]) for i, b in enumerate(refs[11:14])]
+    own_ref, dq0_ref, dq1_ref, dl_ref, gm_ref, x0_ref, x1_ref, gain_ref, cos_ref, sin_ref, dmid_ref, w_ref = refs[:12]
+    gin_ref, low_ref, msg_ref, dh, w_s, sems, far_s, far_sems = refs[15:]
+    arrive = [fetch(b, far_s.at[i], far_sems.at[i]) for i, b in enumerate(refs[12:15])]
     copies = [fetch(w_ref.at[j * 384 : (j + 1) * 384, 0:2048], w_s.at[j], sems.at[j]) for j in range(4)]
     d_kv = own_ref[...].astype(F32)
     for i in range(3):
@@ -539,17 +559,18 @@
         msg_ref[:R, at] = rope_back(d_kv[:, at], cos, sin).astype(BF)
     msg_ref[:R, KW:512] = d_kv[:, KW:].astype(BF)
     msg_ref[:R, 512:] = dl_ref[...]
+    dq = jnp.concatenate([dq0_ref[...], dq1_ref[...]], axis=0)
     for j in range(4):
         copies[j].wait()
-        dh[:, j * 384 : (j + 1) * 384] = mm(dq_ref[...], w_s[j, :, :D], NT) + mm(msg_ref[:R, :512], w_s[j, :, D:], NT)
+        dh[:, j * 384 : (j + 1) * 384] = mm(dq, w_s[j, :, :D], NT) + mm(msg_ref[:R, :512], w_s[j, :, D:], NT)
     grads = jnp.zeros((1, D), F32)
-    for m, (x_ref, low_ref) in enumerate(((x0_ref, low0_ref), (x1_ref, low1_ref))):
+    for m, x_ref in enumerate((x0_ref, x1_ref)):
         rows = slice(m * T, (m + 1) * T)
         grad_gain, back = norm_back(x_ref[...].astype(F32), gain_ref[0:1, :], dh[rows])
         grads = grads + grad_gain
         g_in = dmid_ref[rows, :] + back
         gin_ref[rows, :] = g_in
-        low_ref[...] = g_in.astype(BF)
+        low_ref[rows, :] = g_in.astype(BF)
     row = lax.broadcasted_iota(jnp.int32, (16, 512), 0)
     both = jnp.zeros((16, 512), F32)
     for c in range(3):
@@ -560,13 +581,13 @@
     msg_ref[R:, 512:] = jnp.zeros((16, LANES), BF)
 
 
-def qkv_back(rets, dq, dl, gm, x0, x1, gains, w, cos, sin, d_mid):
+def qkv_back(rets, dqs, dl, gm, x0, x1, gains, w, cos, sin, d_mid):
     return call(
-        qkv_back_kernel, "qkv_back", [rets[0], dq, dl, gm, x0, x1, gains, cos, sin, d_mid], [w, *rets[1:]],
-        [sds((R, D), F32), sds((T, D), BF), sds((T, D), BF), sds((R + 16, MSG), BF)], [],
+        qkv_back_kernel, "qkv_back", [rets[0], *dqs, dl, gm, x0, x1, gains, cos, sin, d_mid], [w, *rets[1:]],
+        [sds((R, D), F32), sds((R, D), BF), sds((R + 16, MSG), BF)], [],
         [pltpu.VMEM((R, D), F32), pltpu.VMEM((4, 384, 2048), BF), pltpu.SemaphoreType.DMA((4,)),
          pltpu.VMEM((3, R, 512), BF), pltpu.SemaphoreType.DMA((3,))],
-        6.2, 12,
+        6.2, 11,
     )
 
 
@@ -574,15 +595,17 @@
 
 
 def attn_grad_kernel(*refs):
-    order_ref, left_ref, blocks, send_ref, (lh, rq, ro, rm, rg, sems) = refs[0], refs[1], refs[2:26], refs[26], refs[27:]
+    order_ref, left_ref, msgs, dqs, datts, send_ref, (lh, rq, ro, rm, rg, sems) = refs[0], refs[1], refs[2:10], refs[10:26], refs[26:42], refs[42], refs[43:]
     left_copies, q_copies, o_copies, m_copies = [], [], [], []
     for i in range(8):
         at = slice(i * R, (i + 1) * R)
         left_copies.append(fetch(left_ref.at[order_ref[i]], lh.at[at, :], sems.at[0, i]))
-        o_copies.append(fetch(blocks[16 + i], ro.at[at, :], sems.at[1, i]))
-        q_copies.append(fetch(blocks[8 + i], rq.at[at, :], sems.at[2, i]))
-        m_copies.append(fetch(blocks[i].at[:R, :], rm.at[at, :], sems.at[3, i]))
-        m_copies.append(fetch(blocks[i].at[R:, :], rg.at[i], sems.at[4, i]))
+        for m in range(2):
+            half = slice(i * R + m * T, i * R + (m + 1) * T)
+            o_copies.append(fetch(datts[2 * i + m], ro.at[half, :], sems.at[1 + m, i]))
+            q_copies.append(fetch(dqs[2 * i + m], rq.at[half, :], sems.at[3 + m, i]))
+        m_copies.append(fetch(msgs[i].at[:R, :], rm.at[at, :], sems.at[5, i]))
+        m_copies.append(fetch(msgs[i].at[R:, :], rg.at[i], sems.at[6, i]))
     for copy in left_copies + o_copies:
         copy.wait()
 
@@ -608,12 +631,12 @@
     return pl.pallas_call(
         attn_grad_kernel,
         name="attn_grad",
-        in_specs=[SCALARS] + [AWAY] * 25,
+        in_specs=[SCALARS] + [AWAY] * 41,
         out_specs=HERE,
         out_shape=sds((8, ROWS, 512), BF),
         scratch_shapes=[
             pltpu.VMEM((8 * R, 768), BF), pltpu.VMEM((8 * R, D), BF), pltpu.VMEM((8 * R, D), BF), pltpu.VMEM((8 * R, MSG), BF),
-            pltpu.VMEM((8, 16, MSG), BF), pltpu.SemaphoreType.DMA((5, 8)),
+            pltpu.VMEM((8, 16, MSG), BF), pltpu.SemaphoreType.DMA((7, 8)),
         ],
         compiler_params=pltpu.CompilerParams(vmem_limit_bytes=20 * 2**20),
         cost_estimate=work(8.5),
@@ -621,13 +644,13 @@
 
 
 def turn_kernel(*refs):
-    lefts, (h_out, a_out, f_s, h_s, a_s, sems) = refs[:4], refs[4:]
+    lefts, (h_out, a_out, f_s, h_s, a_s, sems) = refs[:2], refs[2:]
     copies = [fetch(left, f_s.at[i], sems.at[i]) for i, left in enumerate(lefts)]
-    for i in range(4):
+    for i in range(2):
         copies[i].wait()
-        h_s[:, i * C : (i + 1) * C] = f_s[i, :, :D].T
-        a_s[:, i * C : (i + 1) * C] = f_s[i, :, D:].T
-    sent = [fetch(h_s, h_out, sems.at[4]), fetch(a_s, a_out, sems.at[5])]
+        h_s[:, i * B : (i + 1) * B] = f_s[i, :, :D].T
+        a_s[:, i * B : (i + 1) * B] = f_s[i, :, D:].T
+    sent = [fetch(h_s, h_out, sems.at[2]), fetch(a_s, a_out, sems.at[3])]
     for copy in sent:
         copy.wait()
 
@@ -635,20 +658,20 @@
 def turn(lefts):
     return call(
         turn_kernel, "turn", [], lefts, [], [sds((D, 4 * C), BF), sds((FF, 4 * C), BF)],
-        [pltpu.VMEM((4, C, FW), BF), pltpu.VMEM((D, 4 * C), BF), pltpu.VMEM((FF, 4 * C), BF), pltpu.SemaphoreType.DMA((6,))],
+        [pltpu.VMEM((2, B, FW), BF), pltpu.VMEM((D, 4 * C), BF), pltpu.VMEM((FF, 4 * C), BF), pltpu.SemaphoreType.DMA((6,))],
         5, 14,
     )
 
 
 def expert_grad_kernel(in_ref, down_ref, *refs):
-    rights, out_ref, right = refs[:4], refs[4], refs[5]
+    rights, out_ref, right = refs[:2], refs[2], refs[3]
     j = pl.program_id(0)
-    for i in range(4):
-        right[i * C : (i + 1) * C, :] = rights[i][...]
+    for i in range(2):
+        right[i * B : (i + 1) * B, :] = rights[i][...]
 
     def grads(left_ref, rows, first):
-        for r in range(8):
-            out_ref[r, first : first + rows, :] = mm(left_ref[r * rows : (r + 1) * rows, :], right[...]).astype(BF)
+        for r in range(0, 8, 2):
+            out_ref[r : r + 2, first : first + rows, :] = mm(left_ref[r * rows : (r + 2) * rows, :], right[...]).astype(BF).reshape(2, rows, 512)
 
     @pl.when(j % 2 == 0)
     def _():
@@ -663,12 +686,12 @@
     return pl.pallas_call(
         expert_grad_kernel,
         name="expert_grad",
-        grid=(12,),
-        in_specs=[whole((D, 4 * C)), whole((FF, 4 * C))] + [pl.BlockSpec((C, 256), lambda j: (0, (j % 2) * 6 + j // 2))] * 4,
-        out_specs=pl.BlockSpec((8, SLICE + SLICE // 2, 256), lambda j: (0, 0, j // 2)),
+        grid=(6,),
+        in_specs=[whole((D, 4 * C)), whole((FF, 4 * C))] + [pl.BlockSpec((B, 512), lambda j: (0, (j % 2) * 3 + j // 2))] * 2,
+        out_specs=pl.BlockSpec((8, SLICE + SLICE // 2, 512), lambda j: (0, 0, j // 2)),
         out_shape=pltpu.HBM((8, SLICE + SLICE // 2, D), BF),
-        scratch_shapes=[pltpu.VMEM((4 * C, 256), BF)],
-        compiler_params=pltpu.CompilerParams(dimension_semantics=("arbitrary",), vmem_limit_bytes=VMEM),
+        scratch_shapes=[pltpu.VMEM((4 * C, 512), BF)],
+        compiler_params=pltpu.CompilerParams(dimension_semantics=("arbitrary",), vmem_limit_bytes=26 * 2**20),
         cost_estimate=work(20),
     )(*in_hbm((left_in, left_down, *rights)))
 
@@ -719,79 +742,59 @@
 
     hold = lax.optimization_barrier
 
-    def layer(x, save):
+    def attention(x, save):
         q, kv, h_attn = qkv(x[0], x[1], gains, w, cos, sin)
         kvs = gather_blocks(kv)
-        att, mid, hm0, hm1, *left = attend(spots, q, kvs, allowed, x[0], x[1], w_o, w, gains, chosen, h_attn, save)
-        hms = (hm0, hm1)
-        first = from_chips(hm0)
-        first, hm1 = hold((first, hm1))
-        second = from_chips(hm1)
-        out = expert(first, mine, inner, outer, save)
-        second[0], _ = hold((second[0], out[0]))
-        outs = [out, expert(second, mine, inner, outer, save)]
-        return [out[:4] for out in outs], (x, q, kvs, mid, hms), [out[4:] for out in outs], left
-
-    def finish(parts, mid):
-        rets = [to_chips(part) for part in parts]
-        return [(mid[m * T : (m + 1) * T] + sum(r.astype(F32) for r in rets[m])).astype(BF) for m in micros]
-
-    def experts_back(blocks, more, save):
-        rets, saved = [], []
-        for m in micros:
-            g_share, gate, up, produced = more[m][0], *more[m][3:]
-            if m == 1:
-                blocks[1][0], _ = hold((blocks[1][0], out[0]))
-            out = expert_back(blocks[m], (g_share, gate, up, produced), put, inner, outer, save)
-            rets += to_chips(out[:4])
-            saved.append(out[4:])
-        return rets, saved
+        att, mid, *hm = attend(spots, q, kvs, allowed, x[0], x[1], w_o, w, gains, chosen, h_attn, save)
+        return q, kvs, mid, hm
 
     def keys_back(same, other):
         got = swap(other)
         return to_chips([plus(same[k * R : (k + 1) * R], got[k * R : (k + 1) * R]) for k in range(4)])
 
     tokens = [tokens_in[m, 0] for m in micros]
-    given = [cotangent[m, 0] for m in micros]
-    first, kept, *_ = layer(tokens, False)
-    first = finish(first, kept[3])
+    given = cotangent.reshape(R, D)
+    _, _, mid, hms = attention(tokens, False)
+    blocks = [from_chips(hm) for hm in hms]
+    out = expert(blocks[0], mine, inner, outer, False)
+    blocks[1][0], _ = hold((blocks[1][0], out[0]))
+    outs = [out, expert(blocks[1], mine, inner, outer, False)]
+    first = [(mid[m * T : (m + 1) * T] + sum(r.astype(F32) for r in to_chips(outs[m]))).astype(BF) for m in micros]
     arrived = [lax.ppermute(first[m], "section", [(0, 1)]) for m in micros]
-    arrived, given_first = hold((arrived, from_chips(given[0])))
-    inputs = [jnp.where(is_first, tokens[m], arrived[m]) for m in micros]
-    parts, kept, more, left = layer(inputs, True)
-    (left,) = left
-    f_own = [more[m][1] for m in micros]
-    f_got = [swap(more[m][2]) for m in micros]
-
-    x, q, kvs, mid, hms = kept
-    left, _ = hold((left, parts[1]))
+    arrived, given_blocks = hold((arrived, from_chips(given)))
+
+    x = [jnp.where(is_first, tokens[m], arrived[m]) for m in micros]
+    q, kvs, mid, (*hms, left) = attention(x, True)
+    out = expert(halves_from_chips(*hms), mine, inner, outer, True)
+    parts, (g_share, f_own, f_other), kept = out[:4], out[4:7], out[7:]
+    f_got = swap(f_other)
+
+    acts = (mid + sum(r.astype(F32) for r in to_chips(parts))).astype(BF)
+    out = expert_back(given_blocks, (g_share, *kept), put, inner, outer, False)
+    out, acts = hold((out, acts))
+    rets = to_chips(out)
+    rets, f_got, left = hold((rets, f_got, left))
     left = lax.all_to_all(left, "shard", split_axis=0, concat_axis=0, tiled=True)
-    rets, _ = experts_back([given_first, from_chips(given[1])], more, False)
-    rets, f_got, left = hold((rets, f_got, left))
-    d_mid, d_att, dl, gm = mid_back(rets, given, mid, hms, gains, w)
-    dq, kv_same, kv_other = attn_back(spots, d_att, w_o, q, kvs, allowed, cos, sin)
-    kv_rets, (h_turned, act_turned) = hold((keys_back(kv_same, kv_other), turn(f_own + f_got)))
-    _, low0, low1, _ = qkv_back(kv_rets, dq, dl, gm, x[0], x[1], gains, w, cos, sin, d_mid)
-    arrived = [lax.ppermute(low, "section", [(1, 0)]) for low in (low0, low1)]
-    parts, _ = hold((parts, low0))
-    acts = finish(parts, mid)
-    arrived, acts = hold((arrived, acts))
-    given = [jnp.where(is_first, arrived[m], given[m]) for m in micros]
-
-    first = from_chips(given[0])
-    first, second = hold((first, given[1]))
-    rets, saved = experts_back([first, from_chips(second)], more, True)
-    rights = [saved[m][0] for m in micros] + [swap(saved[m][1]) for m in micros]
+    d_mid, datt0, datt1, dl, gm = mid_back(rets, given, mid, hms, gains, w)
+    dq0, dq1, kv_same, kv_other = attn_back(spots, (datt0, datt1), w_o, q, kvs, allowed, cos, sin)
+    kv_rets, (h_turned, act_turned), left = hold((keys_back(kv_same, kv_other), turn([f_own, f_got]), left))
+    _, low, _ = qkv_back(kv_rets, (dq0, dq1), dl, gm, x[0], x[1], gains, w, cos, sin, d_mid)
+    arrived = lax.ppermute(low, "section", [(1, 0)])
+    halves = [jnp.where(is_first, arrived[m * T : (m + 1) * T], given[m * T : (m + 1) * T]) for m in micros]
+    given = jnp.where(is_first, arrived, given)
+
+    out = expert_back(halves_from_chips(*halves), (g_share, *kept), put, inner, outer, True)
+    rets, rights = to_chips(out[:4]), [out[4], swap(out[5])]
     rets, send = hold((rets, expert_grad(h_turned, act_turned, rights)))
     expert_parts = lax.all_to_all(send, "rep", split_axis=0, concat_axis=0, tiled=True)
-    d_mid, d_att, dl, gm = mid_back(rets, given, mid, hms, gains, w)
-    datts = from_chips(d_att)
-    dq, kv_same, kv_other = attn_back(spots, d_att, w_o, q, kvs, allowed, cos, sin)
+    d_mid, datt0, datt1, dl, gm = mid_back(rets, given, mid, hms, gains, w)
+    datts = halves_from_chips(datt0, datt1)
+    dq0, dq1, kv_same, kv_other = attn_back(spots, (datt0, datt1), w_o, q, kvs, allowed, cos, sin)
     datts, kv_same, kv_other = hold((datts, kv_same, kv_other))
     kv_rets = keys_back(kv_same, kv_other)
-    kv_rets, dq_sent = hold((kv_rets, dq))
-    dqs = from_chips(dq_sent)
-    g_in, _, _, msg = qkv_back(kv_rets, dq, dl, gm, x[0], x[1], gains, w, cos, sin, d_mid)
+    kv_rets, dq0_sent, dq1_sent = hold((kv_rets, dq0, dq1))
+    dqs = halves_from_chips(dq0_sent, dq1_sent)
+    g_in, _, msg = qkv_back(kv_rets, (dq0, dq1), dl, gm, x[0], x[1], gains, w, cos, sin, d_mid)
 
     msgs = from_chips(msg)
     dqs, msgs = hold((dqs, msgs))
@@ -805,7 +808,7 @@
     expert_sums = jnp.sum(expert_parts.astype(F32), axis=0)
 
     return (
-        jnp.stack(acts)[None, :, None],
+        acts.reshape(1, 2, 1, T, D),
         g_in.reshape(1, 2, 1, T, D),
         g_gains[0:1],
         g_q[None],

time: 557 us -> 515 us (0.925)
  Pallas kernels: 169 us -> 150 us
  starting transfers between devices: 133 us -> 121 us
  waiting for transfers between devices: 189 us -> 179 us
    ppermute x72 -> x66, waiting for transfers between devices: 132 us -> 108 us  [along_y(): return lax.ppermute(x, 'shard', [(i, (i + 2 * k) % 8) for i in range(8)])]
    pallas_call x19 -> x16, Pallas kernels: 143 us -> 128 us  [call(): pl.pallas_call(kernel, name=name, in_specs=[SCALARS] * len(scalars) + [HE...]
    ppermute x72 -> x66, starting transfers between devices: 96.6 us -> 85.6 us  [along_y(): return lax.ppermute(x, 'shard', [(i, (i + 2 * k) % 8) for i in range(8)])]
    ppermute x2 -> x1, waiting for transfers between devices: 3 us -> 12.6 us  [body(): arrived = lax.ppermute(low, 'section', [(1, 0)])]
    ppermute x32 -> x38, waiting for transfers between devices: 9.63 us -> 11.5 us  [swap(): return lax.ppermute(x, 'shard', [(i, i ^ 1) for i in range(8)])]
    unnamed x221 -> x217, local copies, waits for them, and re-layouts: 21.1 us -> 21.6 us
  transfers between devices with their start and end apart: 115 -> 114, of which waited for: 52 -> 51; matrix products, arithmetic and copies ran while one was open for 3% -> 3% of each run, Pallas kernels for 23% -> 18%
where the time goes in v4:
time: 515 us; the launch traced here: 506 us
  waiting for transfers between devices  179 us (35%)
  Pallas kernels  150 us (29%)
  starting transfers between devices  121 us (23%)
  local copies, waits for them, and re-layouts  26.3 us (5%)
  between operations  16.1 us (3%)
  other arithmetic  12.5 us (2%)
    pallas_call x16, Pallas kernels, call(): pl.pallas_call(kernel, name=name, in_specs=[SCALARS] * len(scalars) + [HE...  128 us
    ppermute x66, waiting for transfers between devices, along_y(): return lax.ppermute(x, 'shard', [(i, (i + 2 * k) % 8) for i in range(8)])  108 us
    ppermute x66, starting transfers between devices, along_y(): return lax.ppermute(x, 'shard', [(i, (i + 2 * k) % 8) for i in range(8)])  85.6 us
    ppermute x3, waiting for transfers between devices, body(): lax.ppermute(quarters, 'rep', [(i, (i // 2 + k) % 4 * 2 + i % 2) for i in...  27.1 us
    unnamed x217, local copies, waits for them, and re-layouts  21.6 us
    all_to_all x1, waiting for transfers between devices, body(): got = lax.all_to_all(send, 'rep', split_axis=0, concat_axis=0, tiled=True)  17 us
    pallas_call x1, Pallas kernels, expert_grad(): pl.pallas_call(expert_grad_kernel, name='expert_grad', grid=(6,), in_spec...  13.5 us
    ppermute x1, waiting for transfers between devices, body(): arrived = lax.ppermute(low, 'section', [(1, 0)])  12.6 us
  transfers between devices with their start and end apart: 114, of which 51 were waited for; matrix products, arithmetic and copies ran while one was open for 3% of the time, Pallas kernels for 18%

profile of v4, /device:TPU:0, one launch (start us, length us, event | category | flops | bytes accessed | tf_op | source)
XLA Modules:
  0.0 505.9 jit_solution(15893826671811324454)
XLA Ops:
  16.1 5.4 %collective-permute-done.4 = bf16[48,1536]{1,0:T(8,128)(2,1)} collective-permute-done((bf16[48,1536]{1,0:T(8,128)(2,1)}, bf16[48,1536]{1,0:T(8,128)(2,1)}, u32[]{:S(2)}, u32[]{:S(2)}) %collective-permute-start.4) | collective-permute-done | bytes 147488 | tf_op jit(solution)/shard_map/ppermute | solution.py:85
  27.2 4.0 collective-permute-start.7
  32.6 24.4 %collective-permute-done.7.refs_11_.refs_12_ = bf16[4,48,1536]{2,1,0:T(8,128)(2,1)} collective-permute-done((bf16[4,48,1536]{2,1,0:T(8,128)(2,1)}, bf16[4,48,1536]{2,1,0:T(8,128)(2,1)}, u32[]{:S(2)}, u32[]{:S(2)}) %collective-permute-start.7) | collective-permute-done | bytes 589856 | tf_op jit(solution)/shard_map/ppermute | solution.py:716
  68.8 3.9 collective-permute-done.14.refs_19_
  78.2 6.9 %attend.2 = (bf16[128,1536]{1,0:T(8,128)(2,1)}, f32[128,1536]{1,0:T(8,128)S(1)}, bf16[64,1664]{1,0:T(8,128)(2,1)S(1)}, bf16[64,1664]{1,0:T(8,128)(2,1)S(1)}) custom-call(s32[32]{0:T(128)S(1)} %stack.183.refs_0_, bf16[128,1536]{1,0:T(8,128)(2,1)S(1)} %get-tuple-element.141.refs_1_, bf16[128,512]{1,0:T(8,128)(2,1)S(1)} %get-tuple-element.142.refs_2_, ...), custom_call_target="tpu_custom_call" | custom-call | flops 1 | bytes 25900000 | tf_op jit(solution)/shard_map/attend/pallas_call | solution.py:62
  96.3 4.6 collective-permute-done.19.refs_6_
  101.6 7.9 %expert.3 = (bf16[64,1536]{1,0:T(8,128)(2,1)S(1)}, bf16[64,1536]{1,0:T(8,128)(2,1)S(1)}, bf16[64,1536]{1,0:T(8,128)(2,1)S(1)}, bf16[64,1536]{1,0:T(8,128)(2,1)S(1)}) custom-call(bf16[64,1664]{1,0:T(8,128)(2,1)S(1)} %get-tuple-element.144.refs_0_, f32[8,128]{1,0:T(8,128)S(1)} %pad_convert_fusion.1.refs_1_.refs_2_, bf16[1536,1536]{1,0:T(8,128)(2,1)} %bitcast.92, ...), custom_call_target="tpu_custom_call" | custom-call | flops 1 | bytes 28490000 | tf_op jit(solution)/shard_map/expert/pallas_call | solution.py:62
  113.6 7.9 %expert.4 = (bf16[64,1536]{1,0:T(8,128)(2,1)S(1)}, bf16[64,1536]{1,0:T(8,128)(2,1)S(1)}, bf16[64,1536]{1,0:T(8,128)(2,1)S(1)}, bf16[64,1536]{1,0:T(8,128)(2,1)S(1)}) custom-call(bf16[64,1664]{1,0:T(8,128)(2,1)S(1)} %get-tuple-element.154.refs_0_, f32[8,128]{1,0:T(8,128)S(1)} %pad_convert_fusion.1.refs_1_.refs_2_, bf16[1536,1536]{1,0:T(8,128)(2,1)} %bitcast.93, ...), custom_call_target="tpu_custom_call" | custom-call | flops 1 | bytes 28490000 | tf_op jit(solution)/shard_map/expert/pallas_call | solution.py:62
  133.1 9.6 %collective-permute-done.31 = bf16[64,1536]{1,0:T(8,128)(2,1)S(1)} collective-permute-done((bf16[64,1536]{1,0:T(8,128)(2,1)S(1)}, bf16[64,1536]{1,0:T(8,128)(2,1)S(1)}, u32[]{:S(2)}, u32[]{:S(2)}) %collective-permute-start.31) | collective-permute-done | bytes 196640 | tf_op jit(solution)/shard_map/ppermute | solution.py:85
  142.9 4.9 collective-permute-start.32
  166.7 7.0 %attend.3 = (bf16[128,1536]{1,0:T(8,128)(2,1)}, f32[128,1536]{1,0:T(8,128)S(1)}, bf16[64,1664]{1,0:T(8,128)(2,1)S(1)}, bf16[64,1664]{1,0:T(8,128)(2,1)S(1)}, bf16[8,128,768]{2,1,0:T(8,128)(2,1)S(1)}) custom-call(s32[32]{0:T(128)S(1)} %stack.183.refs_0_, bf16[128,1536]{1,0:T(8,128)(2,1)S(1)} %get-tuple-element.162.refs_1_.refs_3_, ...), custom_call_target="tpu_custom_call" | custom-call | flops 1 | bytes 25900000 | tf_op jit(solution)/shard_map/attend/pallas_call | solution.py:62
  180.1 4.0 collective-permute-done.43.refs_7_
  193.8 14.0 %expert.5 = (bf16[128,1536]{1,0:T(8,128)(2,1)S(1)}, bf16[128,1536]{1,0:T(8,128)(2,1)S(1)}, bf16[128,1536]{1,0:T(8,128)(2,1)S(1)}, bf16[128,1536]{1,0:T(8,128)(2,...) custom-call(bf16[64,1664]{1,0:T(8,128)(2,1)S(1)} %get-tuple-element., ...), custom_call_target="tpu_custom_call" | custom-call | flops 1 | bytes 51800000 | tf_op jit(solution)/shard_map/expert/pallas_call | solution.py:62
  211.4 17.6 %expert_back.2 = (bf16[128,1664]{1,0:T(8,128)(2,1)S(1)}, bf16[128,1664]{1,0:T(8,128)(2,1)S(1)}, bf16[128,1664]{1,0:T(8,128)(2,1)S(1)}, bf16[128,1664]{1,0:T(8,128)(2,1)S(1)}) custom-call(bf16[128,1536]{1,0:T(8,128)(2,1)S(1)} %bitcast.89, f32[2,512,128]{2,1,0:T(8,128)S(1)} %get-tuple-element.167.refs_1_.refs_2_, ...), custom_call_target="tpu_custom_call" | custom-call | flops 1 | bytes 55500000 | tf_op jit(solution)/shard_map/expert_back/pallas_call | solution.py:62
  235.5 9.5 %collective-permute-done.52.refs_7_ = bf16[128,1664]{1,0:T(8,128)(2,1)S(1)} collective-permute-done((bf16[128,1664]{1,0:T(8,128)(2,1)S(1)}, bf16[128,1664]{1,0:T(8,128)(2,1)S(1)}, u32[]{:S(2)}, u32[]{:S(2)}) %collective-permute-start.52) | collective-permute-done | bytes 426016 | tf_op jit(solution)/shard_map/ppermute | solution.py:85
  247.4 7.7 %collective-permute-done.54.refs_9_ = bf16[128,1664]{1,0:T(8,128)(2,1)S(1)} collective-permute-done((bf16[128,1664]{1,0:T(8,128)(2,1)S(1)}, bf16[128,1664]{1,0:T(8,128)(2,1)S(1)}, u32[]{:S(2)}, u32[]{:S(2)}) %collective-permute-start.54) | collective-permute-done | bytes 426016 | tf_op jit(solution)/shard_map/ppermute | solution.py:85
  255.9 4.5 all-to-all-start
  264.6 8.9 %attn_back.2 = (bf16[64,1536]{1,0:T(8,128)(2,1)S(1)}, bf16[64,1536]{1,0:T(8,128)(2,1)S(1)}, bf16[512,512]{1,0:T(8,128)(2,1)S(1)}, bf16[512,512]{1,0:T(8,128)(2,1)S(1)}) custom-call(s32[32]{0:T(128)S(1)} %stack.183.refs_0_, bf16[64,1536]{1,0:T(8,128)(2,1)S(1)} %get-tuple-element.194.refs_1_, bf16[64,1536]{1,0:T(8,128)(2,1)S(1)} %get-tuple-element.195.refs_2_, ...), custom_call_target="tpu_custom_call" | custom-call | flops 1 | bytes 33300000 | tf_op jit(solution)/shard_map/attn_back/pallas_call | solution.py:62
  283.6 5.1 %turn.1 = (bf16[1536,1024]{1,0:T(8,128)(2,1)}, bf16[768,1024]{1,0:T(8,128)(2,1)}) custom-call(bf16[512,2304]{1,0:T(8,128)(2,1)} %get-tuple-element.198.refs_0_, bf16[512,2304]{1,0:T(8,128)(2,1)} %collective-permute-done.55.refs_1_), custom_call_target="tpu_custom_call" | custom-call | flops 1 | bytes 18500000 | tf_op jit(solution)/shard_map/turn/pallas_call | solution.py:62
  292.6 6.2 %qkv_back.2 = (f32[128,1536]{1,0:T(8,128)}, bf16[128,1536]{1,0:T(8,128)(2,1)S(1)}, bf16[144,640]{1,0:T(8,128)(2,1)}) custom-call(bf16[128,512]{1,0:T(8,128)(2,1)S(1)} %copy-done.10, bf16[64,1536]{1,0:T(8,128)(2,1)S(1)} %copy-done.16, bf16[64,1536]{1,0:T(8,128)(2,1)S(1)} %copy-done.18, bf16[128,128]{1,0:T(8,128)(2,1)S(1)} %get-tuple-element.206.refs_3_, ...), custom_call_target="tpu_custom_call" | custom-call | flops 1 | bytes 22940000 | tf_op jit(solution)/shard_map/qkv_back/pallas_call | solution.py:62
  300.2 12.6 %collective-permute-done.60 = bf16[128,1536]{1,0:T(8,128)(2,1)S(1)} collective-permute-done((bf16[128,1536]{1,0:T(8,128)(2,1)S(1)}, bf16[128,1536]{1,0:T(8,128)(2,1)S(1)}, u32[]{:S(2)}, u32[]{:S(2)}) %collective-permute-start.60) | collective-permute-done | bytes 393248 | tf_op jit(solution)/shard_map/ppermute | solution.py:782
  331.5 19.9 %expert_back.3 = (bf16[128,1664]{1,0:T(8,128)(2,1)S(1)}, bf16[128,1664]{1,0:T(8,128)(2,1)S(1)}, bf16[128,1664]{1,0:T(8,128)(2,1)S(1)}, bf16[128,1664]{1,0:T(8,12...) custom-call(bf16[64,1536]{1,0:T(8,128)(2,1)S(1)} %get-tuple-element.317.refs_0_, ...), custom_call_target="tpu_custom_call" | custom-call | flops 1 | bytes 62900000 | tf_op jit(solution)/shard_map/expert_back/pallas_call | solution.py:62
  359.1 13.5 %expert_grad.1 = bf16[8,288,1536]{2,1,0:T(8,128)(2,1)} custom-call(bf16[1536,1024]{1,0:T(8,128)(2,1)} %get-tuple-element.217.in_ref, bf16[768,1024]{1,0:T(8,128)(2,1)} %get-tuple-element.218.down_ref, bf16[512,3072]{1,0:T(8,128)(2,1)} %get-tuple-element.219.refs_0_, bf16[512,3072]{1,0:T(8,128)(2,1)} %copy-done.22), custom_call_target="tpu_custom_call" | custom-call | flops 1 | bytes 74000000 | tf_op jit(solution)/shard_map/expert_grad/pallas_call | solution.py:686
  375.6 4.9 all-to-all-start.1
  396.2 8.9 %attn_back.3 = (bf16[64,1536]{1,0:T(8,128)(2,1)S(1)}, bf16[64,1536]{1,0:T(8,128)(2,1)S(1)}, bf16[512,512]{1,0:T(8,128)(2,1)S(1)}, bf16[512,512]{1,0:T(8,128)(2,1)S(1)}) custom-call(s32[32]{0:T(128)S(1)} %stack.183.refs_0_, bf16[64,1536]{1,0:T(8,128)(2,1)S(1)} %get-tuple-element.258.refs_1_.refs_26_, ...), custom_call_target="tpu_custom_call" | custom-call | flops 1 | bytes 33300000 | tf_op jit(solution)/shard_map/attn_back/pallas_call | solution.py:62
  411.4 5.6 %collective-permute-done.80.refs_14_ = bf16[128,512]{1,0:T(8,128)(2,1)S(1)} collective-permute-done((bf16[128,512]{1,0:T(8,128)(2,1)S(1)}, bf16[128,512]{1,0:T(8,128)(2,1)S(1)}, u32[]{:S(2)}, u32[]{:S(2)}) %collective-permute-start.80) | collective-permute-done | bytes 131104 | tf_op jit(solution)/shard_map/ppermute | solution.py:85
  418.3 6.3 %qkv_back.3 = (f32[128,1536]{1,0:T(8,128)}, bf16[128,1536]{1,0:T(8,128)(2,1)}, bf16[144,640]{1,0:T(8,128)(2,1)S(1)}) custom-call(bf16[128,512]{1,0:T(8,128)(2,1)S(1)} %get-tuple-element.233.refs_0_, bf16[64,1536]{1,0:T(8,128)(2,1)S(1)} %get-tuple-element.250.refs_1_.refs_10_, bf16[64,1536]{1,0:T(8,128)(2,1)S(1)} %get-tuple-element.251.refs_2_.refs_11_, ...), custom_call_target="tpu_custom_call" | custom-call | flops 1 | bytes 22940000 | tf_op jit(solution)/shard_map/qkv_back/pallas_call | solution.py:62
  432.4 6.5 %collective-permute-done.88.refs_4_ = bf16[144,640]{1,0:T(8,128)(2,1)S(1)} collective-permute-done((bf16[144,640]{1,0:T(8,128)(2,1)S(1)}, bf16[144,640]{1,0:T(8,128)(2,1)S(1)}, u32[]{:S(2)}, u32[]{:S(2)}) %collective-permute-start.88) | collective-permute-done | bytes 184352 | tf_op jit(solution)/shard_map/ppermute | solution.py:85
  458.0 8.7 %attn_grad.1 = bf16[8,208,512]{2,1,0:T(8,128)(2,1)} custom-call(s32[8]{0:T(128)S(1)} %stack.192.refs_0_, bf16[8,128,768]{2,1,0:T(8,128)(2,1)} %all-to-all-done.refs_1_, bf16[144,640]{1,0:T(8,128)(2,1)} %copy-done.19, bf16[144,640]{1,0:T(8,128)(2,1)} %copy-done.91, bf16[144,640]{1,0:T(8,128)(2,1)} %copy-done.90, bf16[144,640]{1,0:T(8,128)(2,1)} %copy-done.89, ...), custom_call_target="tpu_custom_call" | custom-call | flops 1 | bytes 31450000 | tf_op jit(solution)/shard_map/attn_grad/pallas_call | solution.py:631
  466.7 5.5 %all-to-all-start.2 = ((bf16[8,208,512]{2,1,0:T(8,128)(2,1)}), bf16[8,208,512]{2,1,0:T(8,128)(2,1)S(1)}, u32[]{:S(2)}, u32[]{:S(2)}) async-start(bf16[8,208,512]{2,1,0:T(8,128)(2,1)} %attn_grad.1), calls=%async_computation.2 | async-start | bytes 3407872 | tf_op jit(solution)/shard_map/all_to_all | solution.py:804
  472.3 4.2 convert_reduce_fusion
  478.4 17.0 %all-to-all-done.2 = bf16[8,208,512]{2,1,0:T(8,128)(2,1)S(1)} async-done(((bf16[8,208,512]{2,1,0:T(8,128)(2,1)}), bf16[8,208,512]{2,1,0:T(8,128)(2,1)S(1)}, u32[]{:S(2)}, u32[]{:S(2)}) %all-to-all-start.2) | async-done | bytes 1703968 | tf_op jit(solution)/shard_map/all_to_all | solution.py:804
  (481 shorter events, 212.2 us)
Async XLA Ops:
  7.2 54.1 %all-gather.2.cloned.1.call-start = ((), (), s32[]{:S(2)}) async-start(), calls=%async_computation.3 | async-start | bytes 7520256 | tf_op jit(solution)/shard_map/all_gather | solution.py:709
  10.4 52.1 %collective-permute-start = (bf16[1536,1536]{1,0:T(8,128)(2,1)}, bf16[1536,1536]{1,0:T(8,128)(2,1)}, u32[]{:S(2)}, u32[]{:S(2)}) collective-permute-start(bf16[1536,1536]{1,0:T(8,128)(2,1)} %bitcast.91), channel_id=1, source_target_pairs={{0,1},{1,0},{2,3},{3,2},{4,5},{5,4},{6,7},{7,6},{8,9},{9,8},{10,11... | collective-permute-start | bytes 14155784 | tf_op jit(solution)/shard_map/ppermute | solution.py:81
  15.9 44.8 %collective-permute-start.1 = (bf16[768,1536]{1,0:T(8,128)(2,1)S(1)}, bf16[768,1536]{1,0:T(8,128)(2,1)}, u32[]{:S(2)}, u32[]{:S(2)}) collective-permute-start(bf16[768,1536]{1,0:T(8,128)(2,1)S(1)} %bitcast.102), channel_id=1, source_target_pairs={{0,1},{1,0},{2,3},{3,2},{4,5},{5,4},{6,7},{7,6},{8,9},{9,8},{10,11... | collective-permute-start | bytes 7077896 | tf_op jit(solution)/shard_map/ppermute | solution.py:81
  27.2 29.8 %collective-permute-start.7 = (bf16[4,48,1536]{2,1,0:T(8,128)(2,1)}, bf16[4,48,1536]{2,1,0:T(8,128)(2,1)}, u32[]{:S(2)}, u32[]{:S(2)}) collective-permute-start(bf16[4,48,1536]{2,1,0:T(8,128)(2,1)} %pad_maximum_fusion.refs_8_.refs_9_), channel_id=1, source_target_pairs={{0,48},{8,56},{16,0},{24,8},{32,16},{40,24},{48,32},{56,40},{1,49}... | collective-permute-start | bytes 1769480 | tf_op jit(solution)/shard_map/ppermute | solution.py:716
  31.2 25.7 %collective-permute-start.6 = (bf16[4,48,1536]{2,1,0:T(8,128)(2,1)}, bf16[4,48,1536]{2,1,0:T(8,128)(2,1)}, u32[]{:S(2)}, u32[]{:S(2)}) collective-permute-start(bf16[4,48,1536]{2,1,0:T(8,128)(2,1)} %pad_maximum_fusion.refs_8_.refs_9_), channel_id=1, source_target_pairs={{0,32},{8,40},{16,48},{24,56},{32,0},{40,8},{48,16},{56,24},{1,33}... | collective-permute-start | bytes 1769480 | tf_op jit(solution)/shard_map/ppermute | solution.py:716
  31.3 29.1 %collective-permute-start.5 = (bf16[4,48,1536]{2,1,0:T(8,128)(2,1)}, bf16[4,48,1536]{2,1,0:T(8,128)(2,1)}, u32[]{:S(2)}, u32[]{:S(2)}) collective-permute-start(bf16[4,48,1536]{2,1,0:T(8,128)(2,1)} %pad_maximum_fusion.refs_8_.refs_9_), channel_id=1, source_target_pairs={{0,16},{8,24},{16,32},{24,40},{32,48},{40,56},{48,0},{56,8},{1,17}... | collective-permute-start | bytes 1769480 | tf_op jit(solution)/shard_map/ppermute | solution.py:716
  60.7 15.9 %collective-permute-start.9 = (bf16[4,48,1536]{2,1,0:T(8,128)(2,1)}, bf16[4,48,1536]{2,1,0:T(8,128)(2,1)S(1)}, u32[]{:S(2)}, u32[]{:S(2)}) collective-permute-start(bf16[4,48,1536]{2,1,0:T(8,128)(2,1)} %collective-permute-done.5.refs_9_.refs_10_), channel_id=1, source_target_pairs={{0,1},{1,0},{2,3},{3,2},{4,5},{5,4},{6,7},{7,6},{8,9},{9,8},{10,11... | collective-permute-start | bytes 1769480 | tf_op jit(solution)/shard_map/ppermute | solution.py:81
  87.6 23.3 %collective-permute-start.28 = (bf16[64,1664]{1,0:T(8,128)(2,1)S(1)}, bf16[64,1664]{1,0:T(8,128)(2,1)S(1)}, u32[]{:S(2)}, u32[]{:S(2)}) collective-permute-start(bf16[64,1664]{1,0:T(8,128)(2,1)S(1)} %get-tuple-element.154.refs_0_), channel_id=1, source_target_pairs={{0,6},{1,7},{2,0},{3,1},{4,2},{5,3},{6,4},{7,5},{8,14},{9,15},{10,... | collective-permute-start | bytes 638984 | tf_op jit(solution)/shard_map/ppermute | solution.py:85
  90.2 22.1 %collective-permute-start.27 = (bf16[64,1664]{1,0:T(8,128)(2,1)S(1)}, bf16[64,1664]{1,0:T(8,128)(2,1)S(1)}, u32[]{:S(2)}, u32[]{:S(2)}) collective-permute-start(bf16[64,1664]{1,0:T(8,128)(2,1)S(1)} %get-tuple-element.154.refs_0_), channel_id=1, source_target_pairs={{0,4},{1,5},{2,6},{3,7},{4,0},{5,1},{6,2},{7,3},{8,12},{9,13},{10,... | collective-permute-start | bytes 638984 | tf_op jit(solution)/shard_map/ppermute | solution.py:85
  95.8 16.4 %collective-permute-start.26 = (bf16[64,1664]{1,0:T(8,128)(2,1)S(1)}, bf16[64,1664]{1,0:T(8,128)(2,1)S(1)}, u32[]{:S(2)}, u32[]{:S(2)}) collective-permute-start(bf16[64,1664]{1,0:T(8,128)(2,1)S(1)} %get-tuple-element.154.refs_0_), channel_id=1, source_target_pairs={{0,2},{1,3},{2,4},{3,5},{4,6},{5,7},{6,0},{7,1},{8,10},{9,11},{10,... | collective-permute-start | bytes 638984 | tf_op jit(solution)/shard_map/ppermute | solution.py:85
  109.5 15.7 %collective-permute-start.22 = (bf16[64,1536]{1,0:T(8,128)(2,1)S(1)}, bf16[64,1536]{1,0:T(8,128)(2,1)S(1)}, u32[]{:S(2)}, u32[]{:S(2)}) collective-permute-start(bf16[64,1536]{1,0:T(8,128)(2,1)S(1)} %get-tuple-element.150), channel_id=1, source_target_pairs={{0,6},{1,7},{2,0},{3,1},{4,2},{5,3},{6,4},{7,5},{8,14},{9,15},{10,... | collective-permute-start | bytes 589832 | tf_op jit(solution)/shard_map/ppermute | solution.py:85
  110.1 16.4 %collective-permute-start.23 = (bf16[64,1536]{1,0:T(8,128)(2,1)S(1)}, bf16[64,1536]{1,0:T(8,128)(2,1)S(1)}, u32[]{:S(2)}, u32[]{:S(2)}) collective-permute-start(bf16[64,1536]{1,0:T(8,128)(2,1)S(1)} %get-tuple-element.151), channel_id=1, source_target_pairs={{0,4},{1,5},{2,6},{3,7},{4,0},{5,1},{6,2},{7,3},{8,12},{9,13},{10,... | collective-permute-start | bytes 589832 | tf_op jit(solution)/shard_map/ppermute | solution.py:85
  110.9 17.5 %collective-permute-start.24 = (bf16[64,1536]{1,0:T(8,128)(2,1)S(1)}, bf16[64,1536]{1,0:T(8,128)(2,1)S(1)}, u32[]{:S(2)}, u32[]{:S(2)}) collective-permute-start(bf16[64,1536]{1,0:T(8,128)(2,1)S(1)} %get-tuple-element.152), channel_id=1, source_target_pairs={{0,2},{1,3},{2,4},{3,5},{4,6},{5,7},{6,0},{7,1},{8,10},{9,11},{10,... | collective-permute-start | bytes 589832 | tf_op jit(solution)/shard_map/ppermute | solution.py:85
  125.2 17.5 %collective-permute-start.31 = (bf16[64,1536]{1,0:T(8,128)(2,1)S(1)}, bf16[64,1536]{1,0:T(8,128)(2,1)S(1)}, u32[]{:S(2)}, u32[]{:S(2)}) collective-permute-start(bf16[64,1536]{1,0:T(8,128)(2,1)S(1)} %get-tuple-element.158), channel_id=1, source_target_pairs={{0,2},{1,3},{2,4},{3,5},{4,6},{5,7},{6,0},{7,1},{8,10},{9,11},{10,... | collective-permute-start | bytes 589832 | tf_op jit(solution)/shard_map/ppermute | solution.py:85
  126.5 22.9 %collective-permute-start.35 = (bf16[128,1536]{1,0:T(8,128)(2,1)S(1)}, bf16[128,1536]{1,0:T(8,128)(2,1)S(1)}, u32[]{:S(2)}, u32[]{:S(2)}) collective-permute-start(bf16[128,1536]{1,0:T(8,128)(2,1)S(1)} %bitcast.86), channel_id=1, source_target_pairs={{0,6},{1,7},{2,0},{3,1},{4,2},{5,3},{6,4},{7,5},{8,14},{9,15},{10,... | collective-permute-start | bytes 1179656 | tf_op jit(solution)/shard_map/ppermute | solution.py:85
  128.4 21.0 %collective-permute-start.34 = (bf16[128,1536]{1,0:T(8,128)(2,1)S(1)}, bf16[128,1536]{1,0:T(8,128)(2,1)S(1)}, u32[]{:S(2)}, u32[]{:S(2)}) collective-permute-start(bf16[128,1536]{1,0:T(8,128)(2,1)S(1)} %bitcast.87), channel_id=1, source_target_pairs={{0,4},{1,5},{2,6},{3,7},{4,0},{5,1},{6,2},{7,3},{8,12},{9,13},{10,... | collective-permute-start | bytes 1179656 | tf_op jit(solution)/shard_map/ppermute | solution.py:85
  131.1 20.0 %collective-permute-start.33 = (bf16[128,1536]{1,0:T(8,128)(2,1)S(1)}, bf16[128,1536]{1,0:T(8,128)(2,1)S(1)}, u32[]{:S(2)}, u32[]{:S(2)}) collective-permute-start(bf16[128,1536]{1,0:T(8,128)(2,1)S(1)} %bitcast.88), channel_id=1, source_target_pairs={{0,2},{1,3},{2,4},{3,5},{4,6},{5,7},{6,0},{7,1},{8,10},{9,11},{10,... | collective-permute-start | bytes 1179656 | tf_op jit(solution)/shard_map/ppermute | solution.py:85
  207.8 47.3 %collective-permute-start.55 = (bf16[512,2304]{1,0:T(8,128)(2,1)}, bf16[512,2304]{1,0:T(8,128)(2,1)}, u32[]{:S(2)}, u32[]{:S(2)}) collective-permute-start(bf16[512,2304]{1,0:T(8,128)(2,1)} %get-tuple-element.188), channel_id=1, source_target_pairs={{0,1},{1,0},{2,3},{3,2},{4,5},{5,4},{6,7},{7,6},{8,9},{9,8},{10,11... | collective-permute-start | bytes 7077896 | tf_op jit(solution)/shard_map/ppermute | solution.py:81
  207.9 21.9 %collective-permute-start.49 = (bf16[128,1536]{1,0:T(8,128)(2,1)S(1)}, bf16[128,1536]{1,0:T(8,128)(2,1)S(1)}, u32[]{:S(2)}, u32[]{:S(2)}) collective-permute-start(bf16[128,1536]{1,0:T(8,128)(2,1)S(1)} %get-tuple-element.180), channel_id=1, source_target_pairs={{0,6},{1,7},{2,0},{3,1},{4,2},{5,3},{6,4},{7,5},{8,14},{9,15},{10,... | collective-permute-start | bytes 1179656 | tf_op jit(solution)/shard_map/ppermute | solution.py:85
  210.3 19.6 %collective-permute-start.50 = (bf16[128,1536]{1,0:T(8,128)(2,1)S(1)}, bf16[128,1536]{1,0:T(8,128)(2,1)S(1)}, u32[]{:S(2)}, u32[]{:S(2)}) collective-permute-start(bf16[128,1536]{1,0:T(8,128)(2,1)S(1)} %get-tuple-element.181), channel_id=1, source_target_pairs={{0,4},{1,5},{2,6},{3,7},{4,0},{5,1},{6,2},{7,3},{8,12},{9,13},{10,... | collective-permute-start | bytes 1179656 | tf_op jit(solution)/shard_map/ppermute | solution.py:85
  210.3 21.0 %collective-permute-start.51 = (bf16[128,1536]{1,0:T(8,128)(2,1)S(1)}, bf16[128,1536]{1,0:T(8,128)(2,1)S(1)}, u32[]{:S(2)}, u32[]{:S(2)}) collective-permute-start(bf16[128,1536]{1,0:T(8,128)(2,1)S(1)} %get-tuple-element.182), channel_id=1, source_target_pairs={{0,2},{1,3},{2,4},{3,5},{4,6},{5,7},{6,0},{7,1},{8,10},{9,11},{10,... | collective-permute-start | bytes 1179656 | tf_op jit(solution)/shard_map/ppermute | solution.py:85
  235.5 19.6 %collective-permute-start.54 = (bf16[128,1664]{1,0:T(8,128)(2,1)S(1)}, bf16[128,1664]{1,0:T(8,128)(2,1)S(1)}, u32[]{:S(2)}, u32[]{:S(2)}) collective-permute-start(bf16[128,1664]{1,0:T(8,128)(2,1)S(1)} %get-tuple-element.187), channel_id=1, source_target_pairs={{0,2},{1,3},{2,4},{3,5},{4,6},{5,7},{6,0},{7,1},{8,10},{9,11},{10,... | collective-permute-start | bytes 1277960 | tf_op jit(solution)/shard_map/ppermute | solution.py:85
  255.9 32.8 %all-to-all-start = ((bf16[8,128,768]{2,1,0:T(8,128)(2,1)}), bf16[8,128,768]{2,1,0:T(8,128)(2,1)}, u32[]{:S(2)}, u32[]{:S(2)}) async-start(bf16[8,128,768]{2,1,0:T(8,128)(2,1)} %copy-done.3), calls=%async_computation | async-start | bytes 3145728 | tf_op jit(solution)/shard_map/all_to_all | solution.py:777
  351.5 21.1 %collective-permute-start.67 = (bf16[128,1664]{1,0:T(8,128)(2,1)S(1)}, bf16[128,1664]{1,0:T(8,128)(2,1)S(1)}, u32[]{:S(2)}, u32[]{:S(2)}) collective-permute-start(bf16[128,1664]{1,0:T(8,128)(2,1)S(1)} %get-tuple-element.214), channel_id=1, source_target_pairs={{0,6},{1,7},{2,0},{3,1},{4,2},{5,3},{6,4},{7,5},{8,14},{9,15},{10,... | collective-permute-start | bytes 1277960 | tf_op jit(solution)/shard_map/ppermute | solution.py:85
  352.2 20.4 %collective-permute-start.68 = (bf16[128,1664]{1,0:T(8,128)(2,1)S(1)}, bf16[128,1664]{1,0:T(8,128)(2,1)S(1)}, u32[]{:S(2)}, u32[]{:S(2)}) collective-permute-start(bf16[128,1664]{1,0:T(8,128)(2,1)S(1)} %get-tuple-element.215), channel_id=1, source_target_pairs={{0,4},{1,5},{2,6},{3,7},{4,0},{5,1},{6,2},{7,3},{8,12},{9,13},{10,... | collective-permute-start | bytes 1277960 | tf_op jit(solution)/shard_map/ppermute | solution.py:85
  352.5 22.3 %collective-permute-start.69 = (bf16[128,1664]{1,0:T(8,128)(2,1)S(1)}, bf16[128,1664]{1,0:T(8,128)(2,1)S(1)}, u32[]{:S(2)}, u32[]{:S(2)}) collective-permute-start(bf16[128,1664]{1,0:T(8,128)(2,1)S(1)} %get-tuple-element.216), channel_id=1, source_target_pairs={{0,2},{1,3},{2,4},{3,5},{4,6},{5,7},{6,0},{7,1},{8,10},{9,11},{10,... | collective-permute-start | bytes 1277960 | tf_op jit(solution)/shard_map/ppermute | solution.py:85
  375.6 91.1 %all-to-all-start.1 = ((bf16[8,288,1536]{2,1,0:T(8,128)(2,1)}), bf16[8,288,1536]{2,1,0:T(8,128)(2,1)}, u32[]{:S(2)}, u32[]{:S(2)}) async-start(bf16[8,288,1536]{2,1,0:T(8,128)(2,1)} %expert_grad.1), calls=%async_computation.1 | async-start | bytes 14155776 | tf_op jit(solution)/shard_map/all_to_all | solution.py:789
  387.2 17.9 %collective-permute-start.76 = (bf16[64,1536]{1,0:T(8,128)(2,1)S(1)}, bf16[64,1536]{1,0:T(8,128)(2,1)S(1)}, u32[]{:S(2)}, u32[]{:S(2)}) collective-permute-start(bf16[64,1536]{1,0:T(8,128)(2,1)S(1)} %get-tuple-element.258.refs_1_.refs_26_), channel_id=1, source_target_pairs={{0,6},{1,7},{2,0},{3,1},{4,2},{5,3},{6,4},{7,5},{8,14},{9,15},{10,... | collective-permute-start | bytes 589832 | tf_op jit(solution)/shard_map/ppermute | solution.py:85
  387.6 17.5 %collective-permute-start.72 = (bf16[64,1536]{1,0:T(8,128)(2,1)S(1)}, bf16[64,1536]{1,0:T(8,128)(2,1)S(1)}, u32[]{:S(2)}, u32[]{:S(2)}) collective-permute-start(bf16[64,1536]{1,0:T(8,128)(2,1)S(1)} %get-tuple-element.259.refs_2_.refs_27_), channel_id=1, source_target_pairs={{0,2},{1,3},{2,4},{3,5},{4,6},{5,7},{6,0},{7,1},{8,10},{9,11},{10,... | collective-permute-start | bytes 589832 | tf_op jit(solution)/shard_map/ppermute | solution.py:85
  410.7 16.3 %collective-permute-start.102 = (bf16[64,1536]{1,0:T(8,128)(2,1)S(1)}, bf16[64,1536]{1,0:T(8,128)(2,1)S(1)}, u32[]{:S(2)}, u32[]{:S(2)}) collective-permute-start(bf16[64,1536]{1,0:T(8,128)(2,1)S(1)} %get-tuple-element.258.refs_1_.refs_26_), channel_id=1, source_target_pairs={{0,1},{1,0},{2,3},{3,2},{4,5},{5,4},{6,7},{7,6},{8,9},{9,8},{10,11... | collective-permute-start | bytes 589832 | tf_op jit(solution)/shard_map/ppermute | solution.py:81
  410.7 19.5 %collective-permute-start.103 = (bf16[64,1536]{1,0:T(8,128)(2,1)S(1)}, bf16[64,1536]{1,0:T(8,128)(2,1)S(1)}, u32[]{:S(2)}, u32[]{:S(2)}) collective-permute-start(bf16[64,1536]{1,0:T(8,128)(2,1)S(1)} %get-tuple-element.259.refs_2_.refs_27_), channel_id=1, source_target_pairs={{0,1},{1,0},{2,3},{3,2},{4,5},{5,4},{6,7},{7,6},{8,9},{9,8},{10,11... | collective-permute-start | bytes 589832 | tf_op jit(solution)/shard_map/ppermute | solution.py:81
  466.7 28.7 %all-to-all-start.2 = ((bf16[8,208,512]{2,1,0:T(8,128)(2,1)}), bf16[8,208,512]{2,1,0:T(8,128)(2,1)S(1)}, u32[]{:S(2)}, u32[]{:S(2)}) async-start(bf16[8,208,512]{2,1,0:T(8,128)(2,1)} %attn_grad.1), calls=%async_computation.2 | async-start | bytes 3407872 | tf_op jit(solution)/shard_map/all_to_all | solution.py:804
  (189 other events, 1635.9 us)
Sparse Core Ops, SparseCore 0:
  10.5 45.0 all-gather.1

commit v5 on v4

--- a/solution.py
+++ b/solution.py
@@ -347,7 +347,7 @@
         scratch = [pltpu.VMEM((rows, D), BF), pltpu.VMEM((2, rows, LANES), F32)] + scratch
     return call(
         lambda *refs: expert_kernel(own, save, *refs), "expert", [*hms[:own], mine], [*w_in, *w_down, *hms[own:]], outs, away, scratch,
-        14 if save else 7.7, 34 if save else 12,
+        14 if save else 7.7, 30 if save else 12,
     )
 
 
@@ -437,7 +437,7 @@
     ] + WEIGHT_SLOTS
     return call(
         lambda *refs: expert_back_kernel(own, save, *refs), "expert_back", [*gs[:own], g_share, put], [gate, up, produced, *w_in, *w_down, *gs[own:]],
-        [sds((R, D + LANES), BF)] * 4, away, scratch, 17 if save else 15, 36 if save else 30,
+        [sds((R, D + LANES), BF)] * 4, away, scratch, 19 if save else 17, 32 if save else 26,
     )
 
 
@@ -761,7 +761,7 @@
     outs = [out, expert(blocks[1], mine, inner, outer, False)]
     first = [(mid[m * T : (m + 1) * T] + sum(r.astype(F32) for r in to_chips(outs[m]))).astype(BF) for m in micros]
     arrived = [lax.ppermute(first[m], "section", [(0, 1)]) for m in micros]
-    arrived, given_blocks = hold((arrived, from_chips(given)))
+    arrived, given_blocks = hold((arrived, halves_from_chips(cotangent[0, 0], cotangent[1, 0])))
 
     x = [jnp.where(is_first, tokens[m], arrived[m]) for m in micros]
     q, kvs, mid, (*hms, left) = attention(x, True)

time: 515 us -> 510 us (level)
  waiting for transfers between devices: 179 us -> 162 us
  starting transfers between devices: 121 us -> 135 us
    ppermute x66 -> x69, waiting for transfers between devices: 108 us -> 90.6 us  [along_y(): return lax.ppermute(x, 'shard', [(i, (i + 2 * k) % 8) for i in range(8)])]
    ppermute x66 -> x69, starting transfers between devices: 85.6 us -> 96.9 us  [along_y(): return lax.ppermute(x, 'shard', [(i, (i + 2 * k) % 8) for i in range(8)])]
    unnamed x217 -> x233, local copies, waits for them, and re-layouts: 21.6 us -> 21.8 us
  transfers between devices with their start and end apart: 114 -> 117, of which waited for: 51 -> 49; matrix products, arithmetic and copies ran while one was open for 3% -> 2% of each run, Pallas kernels for 18% -> 19%
where the time goes in v5:
time: 510 us; the launch traced here: 501 us
  waiting for transfers between devices  162 us (32%)
  Pallas kernels  151 us (30%)
  starting transfers between devices  135 us (26%)
  local copies, waits for them, and re-layouts  25.9 us (5%)
  between operations  16.3 us (3%)
  other arithmetic  10.6 us (2%)
    pallas_call x16, Pallas kernels, call(): pl.pallas_call(kernel, name=name, in_specs=[SCALARS] * len(scalars) + [HE...  128 us
    ppermute x69, starting transfers between devices, along_y(): return lax.ppermute(x, 'shard', [(i, (i + 2 * k) % 8) for i in range(8)])  96.9 us
    ppermute x69, waiting for transfers between devices, along_y(): return lax.ppermute(x, 'shard', [(i, (i + 2 * k) % 8) for i in range(8)])  90.6 us
    ppermute x3, waiting for transfers between devices, body(): lax.ppermute(quarters, 'rep', [(i, (i // 2 + k) % 4 * 2 + i % 2) for i in...  26.7 us
    unnamed x233, local copies, waits for them, and re-layouts  21.8 us
    all_to_all x1, waiting for transfers between devices, body(): got = lax.all_to_all(send, 'rep', split_axis=0, concat_axis=0, tiled=True)  17 us
    pallas_call x1, Pallas kernels, expert_grad(): pl.pallas_call(expert_grad_kernel, name='expert_grad', grid=(6,), in_spec...  13.5 us
    ppermute x1, waiting for transfers between devices, body(): arrived = lax.ppermute(low, 'section', [(1, 0)])  12.5 us
  transfers between devices with their start and end apart: 117, of which 49 were waited for; matrix products, arithmetic and copies ran while one was open for 2% of the time, Pallas kernels for 19%

profile of v5, /device:TPU:0, one launch (start us, length us, event | category | flops | bytes accessed | tf_op | source)
XLA Modules:
  0.0 500.6 jit_solution(3287526966614480208)
XLA Ops:
  15.5 5.0 %collective-permute-done.4 = bf16[48,1536]{1,0:T(8,128)(2,1)S(1)} collective-permute-done((bf16[48,1536]{1,0:T(8,128)(2,1)S(1)}, bf16[48,1536]{1,0:T(8,128)(2,1)S(1)}, u32[]{:S(2)}, u32[]{:S(2)}) %collective-permute-start.4) | collective-permute-done | bytes 147488 | tf_op jit(solution)/shard_map/ppermute | solution.py:85
  24.4 4.1 collective-permute-start.7
  29.9 24.0 %collective-permute-done.7.refs_11_.refs_12_ = bf16[4,48,1536]{2,1,0:T(8,128)(2,1)S(1)} collective-permute-done((bf16[4,48,1536]{2,1,0:T(8,128)(2,1)S(1)}, bf16[4,48,1536]{2,1,0:T(8,128)(2,1)S(1)}, u32[]{:S(2)}, u32[]{:S(2)}) %collective-permute-start.7) | collective-permute-done | bytes 589856 | tf_op jit(solution)/shard_map/ppermute | solution.py:716
  66.4 4.1 collective-permute-done.14.refs_19_
  76.0 6.9 %attend.2 = (bf16[128,1536]{1,0:T(8,128)(2,1)}, f32[128,1536]{1,0:T(8,128)S(1)}, bf16[64,1664]{1,0:T(8,128)(2,1)S(1)}, bf16[64,1664]{1,0:T(8,128)(2,1)S(1)}) custom-call(s32[32]{0:T(128)S(1)} %stack.183.refs_0_, bf16[128,1536]{1,0:T(8,128)(2,1)S(1)} %get-tuple-element.145.refs_1_, bf16[128,512]{1,0:T(8,128)(2,1)S(1)} %get-tuple-element.146.refs_2_, ...), custom_call_target="tpu_custom_call" | custom-call | flops 1 | bytes 25900000 | tf_op jit(solution)/shard_map/attend/pallas_call | solution.py:62
  94.1 4.2 collective-permute-start.36
  99.4 7.8 %expert.3 = (bf16[64,1536]{1,0:T(8,128)(2,1)S(1)}, bf16[64,1536]{1,0:T(8,128)(2,1)S(1)}, bf16[64,1536]{1,0:T(8,128)(2,1)S(1)}, bf16[64,1536]{1,0:T(8,128)(2,1)S(1)}) custom-call(bf16[64,1664]{1,0:T(8,128)(2,1)S(1)} %get-tuple-element.148.refs_0_, f32[8,128]{1,0:T(8,128)S(1)} %pad_convert_fusion.1.refs_1_.refs_2_, bf16[1536,1536]{1,0:T(8,128)(2,1)} %bitcast.92, ...), custom_call_target="tpu_custom_call" | custom-call | flops 1 | bytes 28490000 | tf_op jit(solution)/shard_map/expert/pallas_call | solution.py:62
  110.9 7.8 %expert.4 = (bf16[64,1536]{1,0:T(8,128)(2,1)S(1)}, bf16[64,1536]{1,0:T(8,128)(2,1)S(1)}, bf16[64,1536]{1,0:T(8,128)(2,1)S(1)}, bf16[64,1536]{1,0:T(8,128)(2,1)S(1)}) custom-call(bf16[64,1664]{1,0:T(8,128)(2,1)S(1)} %get-tuple-element.158.refs_0_, f32[8,128]{1,0:T(8,128)S(1)} %pad_convert_fusion.1.refs_1_.refs_2_, bf16[1536,1536]{1,0:T(8,128)(2,1)} %bitcast.93, ...), custom_call_target="tpu_custom_call" | custom-call | flops 1 | bytes 28490000 | tf_op jit(solution)/shard_map/expert/pallas_call | solution.py:62
  127.7 4.2 collective-permute-start.37
  134.0 4.9 collective-permute-start.32
  161.0 7.0 %attend.3 = (bf16[128,1536]{1,0:T(8,128)(2,1)}, f32[128,1536]{1,0:T(8,128)S(1)}, bf16[64,1664]{1,0:T(8,128)(2,1)S(1)}, bf16[64,1664]{1,0:T(8,128)(2,1)S(1)}, bf16[8,128,768]{2,1,0:T(8,128)(2,1)S(1)}) custom-call(s32[32]{0:T(128)S(1)} %stack.183.refs_0_, bf16[128,1536]{1,0:T(8,128)(2,1)S(1)} %get-tuple-element.167.refs_1_.refs_3_, ...), custom_call_target="tpu_custom_call" | custom-call | flops 1 | bytes 25900000 | tf_op jit(solution)/shard_map/attend/pallas_call | solution.py:62
  174.4 4.0 collective-permute-done.46.refs_7_
  188.1 14.0 %expert.5 = (bf16[128,1536]{1,0:T(8,128)(2,1)S(1)}, bf16[128,1536]{1,0:T(8,128)(2,1)S(1)}, bf16[128,1536]{1,0:T(8,128)(2,1)S(1)}, bf16[128,1536]{1,0:T(8,128)(2,...) custom-call(bf16[64,1664]{1,0:T(8,128)(2,1)S(1)} %get-tuple-element., ...), custom_call_target="tpu_custom_call" | custom-call | flops 1 | bytes 51800000 | tf_op jit(solution)/shard_map/expert/pallas_call | solution.py:62
  205.8 17.9 %expert_back.2 = (bf16[128,1664]{1,0:T(8,128)(2,1)S(1)}, bf16[128,1664]{1,0:T(8,128)(2,1)S(1)}, bf16[128,1664]{1,0:T(8,128)(2,1)S(1)}, bf16[128,1664]{1,0:T(8,128)(2,1)S(1)}) custom-call(bf16[64,1536]{1,0:T(8,128)(2,1)S(1)} %copy-done.7, bf16[64,1536]{1,0:T(8,128)(2,1)S(1)} %copy-done.5, f32[2,512,128]{2,1,0:T(8,128)S(1)} %get-tuple-element.172.refs_2_, ...), custom_call_target="tpu_custom_call" | custom-call | flops 1 | bytes 62900000 | tf_op jit(solution)/shard_map/expert_back/pallas_call | solution.py:62
  230.1 9.2 %collective-permute-done.55.refs_7_ = bf16[128,1664]{1,0:T(8,128)(2,1)S(1)} collective-permute-done((bf16[128,1664]{1,0:T(8,128)(2,1)S(1)}, bf16[128,1664]{1,0:T(8,128)(2,1)S(1)}, u32[]{:S(2)}, u32[]{:S(2)}) %collective-permute-start.55) | collective-permute-done | bytes 426016 | tf_op jit(solution)/shard_map/ppermute | solution.py:85
  242.1 7.7 %collective-permute-done.57.refs_9_ = bf16[128,1664]{1,0:T(8,128)(2,1)S(1)} collective-permute-done((bf16[128,1664]{1,0:T(8,128)(2,1)S(1)}, bf16[128,1664]{1,0:T(8,128)(2,1)S(1)}, u32[]{:S(2)}, u32[]{:S(2)}) %collective-permute-start.57) | collective-permute-done | bytes 426016 | tf_op jit(solution)/shard_map/ppermute | solution.py:85
  250.5 4.5 all-to-all-start
  259.2 8.9 %attn_back.2 = (bf16[64,1536]{1,0:T(8,128)(2,1)S(1)}, bf16[64,1536]{1,0:T(8,128)(2,1)S(1)}, bf16[512,512]{1,0:T(8,128)(2,1)S(1)}, bf16[512,512]{1,0:T(8,128)(2,1)S(1)}) custom-call(s32[32]{0:T(128)S(1)} %stack.183.refs_0_, bf16[64,1536]{1,0:T(8,128)(2,1)S(1)} %get-tuple-element.202.refs_1_, bf16[64,1536]{1,0:T(8,128)(2,1)S(1)} %get-tuple-element.203.refs_2_, ...), custom_call_target="tpu_custom_call" | custom-call | flops 1 | bytes 33300000 | tf_op jit(solution)/shard_map/attn_back/pallas_call | solution.py:62
  278.2 5.1 %turn.1 = (bf16[1536,1024]{1,0:T(8,128)(2,1)}, bf16[768,1024]{1,0:T(8,128)(2,1)}) custom-call(bf16[512,2304]{1,0:T(8,128)(2,1)} %get-tuple-element.206.refs_0_, bf16[512,2304]{1,0:T(8,128)(2,1)} %collective-permute-done.58.refs_1_), custom_call_target="tpu_custom_call" | custom-call | flops 1 | bytes 18500000 | tf_op jit(solution)/shard_map/turn/pallas_call | solution.py:62
  287.3 6.2 %qkv_back.2 = (f32[128,1536]{1,0:T(8,128)}, bf16[128,1536]{1,0:T(8,128)(2,1)S(1)}, bf16[144,640]{1,0:T(8,128)(2,1)}) custom-call(bf16[128,512]{1,0:T(8,128)(2,1)S(1)} %copy-done.14, bf16[64,1536]{1,0:T(8,128)(2,1)S(1)} %copy-done.20, bf16[64,1536]{1,0:T(8,128)(2,1)S(1)} %copy-done.22, bf16[128,128]{1,0:T(8,128)(2,1)S(1)} %get-tuple-element.214.refs_3_, ...), custom_call_target="tpu_custom_call" | custom-call | flops 1 | bytes 22940000 | tf_op jit(solution)/shard_map/qkv_back/pallas_call | solution.py:62
  294.8 12.5 %collective-permute-done.63 = bf16[128,1536]{1,0:T(8,128)(2,1)S(1)} collective-permute-done((bf16[128,1536]{1,0:T(8,128)(2,1)S(1)}, bf16[128,1536]{1,0:T(8,128)(2,1)S(1)}, u32[]{:S(2)}, u32[]{:S(2)}) %collective-permute-start.63) | collective-permute-done | bytes 393248 | tf_op jit(solution)/shard_map/ppermute | solution.py:782
  326.1 19.9 %expert_back.3 = (bf16[128,1664]{1,0:T(8,128)(2,1)S(1)}, bf16[128,1664]{1,0:T(8,128)(2,1)S(1)}, bf16[128,1664]{1,0:T(8,128)(2,1)S(1)}, bf16[128,1664]{1,0:T(8,12...) custom-call(bf16[64,1536]{1,0:T(8,128)(2,1)S(1)} %get-tuple-element.325.refs_0_, ...), custom_call_target="tpu_custom_call" | custom-call | flops 1 | bytes 70300000 | tf_op jit(solution)/shard_map/expert_back/pallas_call | solution.py:62
  353.8 13.5 %expert_grad.1 = bf16[8,288,1536]{2,1,0:T(8,128)(2,1)} custom-call(bf16[1536,1024]{1,0:T(8,128)(2,1)} %get-tuple-element.225.in_ref, bf16[768,1024]{1,0:T(8,128)(2,1)} %get-tuple-element.226.down_ref, bf16[512,3072]{1,0:T(8,128)(2,1)} %get-tuple-element.227.refs_0_, bf16[512,3072]{1,0:T(8,128)(2,1)} %copy-done.27), custom_call_target="tpu_custom_call" | custom-call | flops 1 | bytes 74000000 | tf_op jit(solution)/shard_map/expert_grad/pallas_call | solution.py:686
  370.2 4.9 all-to-all-start.1
  390.9 8.9 %attn_back.3 = (bf16[64,1536]{1,0:T(8,128)(2,1)S(1)}, bf16[64,1536]{1,0:T(8,128)(2,1)S(1)}, bf16[512,512]{1,0:T(8,128)(2,1)S(1)}, bf16[512,512]{1,0:T(8,128)(2,1)S(1)}) custom-call(s32[32]{0:T(128)S(1)} %stack.183.refs_0_, bf16[64,1536]{1,0:T(8,128)(2,1)S(1)} %get-tuple-element.266.refs_1_.refs_26_, ...), custom_call_target="tpu_custom_call" | custom-call | flops 1 | bytes 33300000 | tf_op jit(solution)/shard_map/attn_back/pallas_call | solution.py:62
  406.0 5.6 %collective-permute-done.83.refs_14_ = bf16[128,512]{1,0:T(8,128)(2,1)S(1)} collective-permute-done((bf16[128,512]{1,0:T(8,128)(2,1)S(1)}, bf16[128,512]{1,0:T(8,128)(2,1)S(1)}, u32[]{:S(2)}, u32[]{:S(2)}) %collective-permute-start.83) | collective-permute-done | bytes 131104 | tf_op jit(solution)/shard_map/ppermute | solution.py:85
  412.9 6.3 %qkv_back.3 = (f32[128,1536]{1,0:T(8,128)}, bf16[128,1536]{1,0:T(8,128)(2,1)}, bf16[144,640]{1,0:T(8,128)(2,1)S(1)}) custom-call(bf16[128,512]{1,0:T(8,128)(2,1)S(1)} %get-tuple-element.241.refs_0_, bf16[64,1536]{1,0:T(8,128)(2,1)S(1)} %get-tuple-element.258.refs_1_.refs_10_, bf16[64,1536]{1,0:T(8,128)(2,1)S(1)} %get-tuple-element.259.refs_2_.refs_11_, ...), custom_call_target="tpu_custom_call" | custom-call | flops 1 | bytes 22940000 | tf_op jit(solution)/shard_map/qkv_back/pallas_call | solution.py:62
  427.0 6.5 %collective-permute-done.91.refs_4_ = bf16[144,640]{1,0:T(8,128)(2,1)S(1)} collective-permute-done((bf16[144,640]{1,0:T(8,128)(2,1)S(1)}, bf16[144,640]{1,0:T(8,128)(2,1)S(1)}, u32[]{:S(2)}, u32[]{:S(2)}) %collective-permute-start.91) | collective-permute-done | bytes 184352 | tf_op jit(solution)/shard_map/ppermute | solution.py:85
  452.6 8.7 %attn_grad.1 = bf16[8,208,512]{2,1,0:T(8,128)(2,1)} custom-call(s32[8]{0:T(128)S(1)} %stack.192.refs_0_, bf16[8,128,768]{2,1,0:T(8,128)(2,1)} %all-to-all-done.refs_1_, bf16[144,640]{1,0:T(8,128)(2,1)} %copy-done.23, bf16[144,640]{1,0:T(8,128)(2,1)} %copy-done.99, bf16[144,640]{1,0:T(8,128)(2,1)} %copy-done.98, bf16[144,640]{1,0:T(8,128)(2,1)} %copy-done.97, ...), custom_call_target="tpu_custom_call" | custom-call | flops 1 | bytes 31450000 | tf_op jit(solution)/shard_map/attn_grad/pallas_call | solution.py:631
  461.3 5.6 %all-to-all-start.2 = ((bf16[8,208,512]{2,1,0:T(8,128)(2,1)}), bf16[8,208,512]{2,1,0:T(8,128)(2,1)S(1)}, u32[]{:S(2)}, u32[]{:S(2)}) async-start(bf16[8,208,512]{2,1,0:T(8,128)(2,1)} %attn_grad.1), calls=%async_computation.2 | async-start | bytes 3407872 | tf_op jit(solution)/shard_map/all_to_all | solution.py:804
  466.9 4.2 convert_reduce_fusion
  473.1 17.0 %all-to-all-done.2 = bf16[8,208,512]{2,1,0:T(8,128)(2,1)S(1)} async-done(((bf16[8,208,512]{2,1,0:T(8,128)(2,1)}), bf16[8,208,512]{2,1,0:T(8,128)(2,1)S(1)}, u32[]{:S(2)}, u32[]{:S(2)}) %all-to-all-start.2) | async-done | bytes 1703968 | tf_op jit(solution)/shard_map/all_to_all | solution.py:804
  (504 shorter events, 213.1 us)
Async XLA Ops:
  7.2 51.9 %all-gather.2.cloned.1.call-start = ((), (), s32[]{:S(2)}) async-start(), calls=%async_computation.3 | async-start | bytes 7520256 | tf_op jit(solution)/shard_map/all_gather | solution.py:709
  10.3 50.0 %collective-permute-start = (bf16[1536,1536]{1,0:T(8,128)(2,1)}, bf16[1536,1536]{1,0:T(8,128)(2,1)}, u32[]{:S(2)}, u32[]{:S(2)}) collective-permute-start(bf16[1536,1536]{1,0:T(8,128)(2,1)} %bitcast.91), channel_id=1, source_target_pairs={{0,1},{1,0},{2,3},{3,2},{4,5},{5,4},{6,7},{7,6},{8,9},{9,8},{10,11... | collective-permute-start | bytes 14155784 | tf_op jit(solution)/shard_map/ppermute | solution.py:81
  15.3 43.2 %collective-permute-start.1 = (bf16[768,1536]{1,0:T(8,128)(2,1)}, bf16[768,1536]{1,0:T(8,128)(2,1)}, u32[]{:S(2)}, u32[]{:S(2)}) collective-permute-start(bf16[768,1536]{1,0:T(8,128)(2,1)} %bitcast.40.refs_4_.refs_5_.refs_9_), channel_id=1, source_target_pairs={{0,1},{1,0},{2,3},{3,2},{4,5},{5,4},{6,7},{7,6},{8,9},{9,8},{10,11... | collective-permute-start | bytes 7077896 | tf_op jit(solution)/shard_map/ppermute | solution.py:81
  24.4 29.5 %collective-permute-start.7 = (bf16[4,48,1536]{2,1,0:T(8,128)(2,1)S(1)}, bf16[4,48,1536]{2,1,0:T(8,128)(2,1)S(1)}, u32[]{:S(2)}, u32[]{:S(2)}) collective-permute-start(bf16[4,48,1536]{2,1,0:T(8,128)(2,1)S(1)} %pad_maximum_fusion.refs_8_.refs_9_), channel_id=1, source_target_pairs={{0,48},{8,56},{16,0},{24,8},{32,16},{40,24},{48,32},{56,40},{1,49}... | collective-permute-start | bytes 1769480 | tf_op jit(solution)/shard_map/ppermute | solution.py:716
  28.5 25.4 %collective-permute-start.6 = (bf16[4,48,1536]{2,1,0:T(8,128)(2,1)S(1)}, bf16[4,48,1536]{2,1,0:T(8,128)(2,1)}, u32[]{:S(2)}, u32[]{:S(2)}) collective-permute-start(bf16[4,48,1536]{2,1,0:T(8,128)(2,1)S(1)} %pad_maximum_fusion.refs_8_.refs_9_), channel_id=1, source_target_pairs={{0,32},{8,40},{16,48},{24,56},{32,0},{40,8},{48,16},{56,24},{1,33}... | collective-permute-start | bytes 1769480 | tf_op jit(solution)/shard_map/ppermute | solution.py:716
  28.5 28.8 %collective-permute-start.5 = (bf16[4,48,1536]{2,1,0:T(8,128)(2,1)S(1)}, bf16[4,48,1536]{2,1,0:T(8,128)(2,1)S(1)}, u32[]{:S(2)}, u32[]{:S(2)}) collective-permute-start(bf16[4,48,1536]{2,1,0:T(8,128)(2,1)S(1)} %pad_maximum_fusion.refs_8_.refs_9_), channel_id=1, source_target_pairs={{0,16},{8,24},{16,32},{24,40},{32,48},{40,56},{48,0},{56,8},{1,17}... | collective-permute-start | bytes 1769480 | tf_op jit(solution)/shard_map/ppermute | solution.py:716
  58.5 15.9 %collective-permute-start.9 = (bf16[4,48,1536]{2,1,0:T(8,128)(2,1)}, bf16[4,48,1536]{2,1,0:T(8,128)(2,1)}, u32[]{:S(2)}, u32[]{:S(2)}) collective-permute-start(bf16[4,48,1536]{2,1,0:T(8,128)(2,1)} %copy-done.26), channel_id=1, source_target_pairs={{0,1},{1,0},{2,3},{3,2},{4,5},{5,4},{6,7},{7,6},{8,9},{9,8},{10,11... | collective-permute-start | bytes 1769480 | tf_op jit(solution)/shard_map/ppermute | solution.py:81
  85.4 21.9 %collective-permute-start.28 = (bf16[64,1664]{1,0:T(8,128)(2,1)S(1)}, bf16[64,1664]{1,0:T(8,128)(2,1)S(1)}, u32[]{:S(2)}, u32[]{:S(2)}) collective-permute-start(bf16[64,1664]{1,0:T(8,128)(2,1)S(1)} %get-tuple-element.158.refs_0_), channel_id=1, source_target_pairs={{0,6},{1,7},{2,0},{3,1},{4,2},{5,3},{6,4},{7,5},{8,14},{9,15},{10,... | collective-permute-start | bytes 638984 | tf_op jit(solution)/shard_map/ppermute | solution.py:85
  87.9 22.0 %collective-permute-start.27 = (bf16[64,1664]{1,0:T(8,128)(2,1)S(1)}, bf16[64,1664]{1,0:T(8,128)(2,1)S(1)}, u32[]{:S(2)}, u32[]{:S(2)}) collective-permute-start(bf16[64,1664]{1,0:T(8,128)(2,1)S(1)} %get-tuple-element.158.refs_0_), channel_id=1, source_target_pairs={{0,4},{1,5},{2,6},{3,7},{4,0},{5,1},{6,2},{7,3},{8,12},{9,13},{10,... | collective-permute-start | bytes 638984 | tf_op jit(solution)/shard_map/ppermute | solution.py:85
  93.6 16.3 %collective-permute-start.26 = (bf16[64,1664]{1,0:T(8,128)(2,1)S(1)}, bf16[64,1664]{1,0:T(8,128)(2,1)S(1)}, u32[]{:S(2)}, u32[]{:S(2)}) collective-permute-start(bf16[64,1664]{1,0:T(8,128)(2,1)S(1)} %get-tuple-element.158.refs_0_), channel_id=1, source_target_pairs={{0,2},{1,3},{2,4},{3,5},{4,6},{5,7},{6,0},{7,1},{8,10},{9,11},{10,... | collective-permute-start | bytes 638984 | tf_op jit(solution)/shard_map/ppermute | solution.py:85
  94.1 24.6 %collective-permute-start.36 = (bf16[64,1536]{1,0:T(8,128)(2,1)S(1)}, bf16[64,1536]{1,0:T(8,128)(2,1)S(1)}, u32[]{:S(2)}, u32[]{:S(2)}) collective-permute-start(bf16[64,1536]{1,0:T(8,128)(2,1)S(1)} %get-tuple-element.164.refs_1_), channel_id=1, source_target_pairs={{0,6},{1,7},{2,0},{3,1},{4,2},{5,3},{6,4},{7,5},{8,14},{9,15},{10,... | collective-permute-start | bytes 589832 | tf_op jit(solution)/shard_map/ppermute | solution.py:85
  98.8 22.5 %collective-permute-start.33 = (bf16[64,1536]{1,0:T(8,128)(2,1)S(1)}, bf16[64,1536]{1,0:T(8,128)(2,1)S(1)}, u32[]{:S(2)}, u32[]{:S(2)}) collective-permute-start(bf16[64,1536]{1,0:T(8,128)(2,1)S(1)} %get-tuple-element.163.refs_0_), channel_id=1, source_target_pairs={{0,2},{1,3},{2,4},{3,5},{4,6},{5,7},{6,0},{7,1},{8,10},{9,11},{10,... | collective-permute-start | bytes 589832 | tf_op jit(solution)/shard_map/ppermute | solution.py:85
  107.3 16.2 %collective-permute-start.22 = (bf16[64,1536]{1,0:T(8,128)(2,1)S(1)}, bf16[64,1536]{1,0:T(8,128)(2,1)S(1)}, u32[]{:S(2)}, u32[]{:S(2)}) collective-permute-start(bf16[64,1536]{1,0:T(8,128)(2,1)S(1)} %get-tuple-element.154), channel_id=1, source_target_pairs={{0,6},{1,7},{2,0},{3,1},{4,2},{5,3},{6,4},{7,5},{8,14},{9,15},{10,... | collective-permute-start | bytes 589832 | tf_op jit(solution)/shard_map/ppermute | solution.py:85
  110.0 14.8 %collective-permute-start.24 = (bf16[64,1536]{1,0:T(8,128)(2,1)S(1)}, bf16[64,1536]{1,0:T(8,128)(2,1)S(1)}, u32[]{:S(2)}, u32[]{:S(2)}) collective-permute-start(bf16[64,1536]{1,0:T(8,128)(2,1)S(1)} %get-tuple-element.156), channel_id=1, source_target_pairs={{0,2},{1,3},{2,4},{3,5},{4,6},{5,7},{6,0},{7,1},{8,10},{9,11},{10,... | collective-permute-start | bytes 589832 | tf_op jit(solution)/shard_map/ppermute | solution.py:85
  123.5 15.4 %collective-permute-start.34 = (bf16[64,1536]{1,0:T(8,128)(2,1)S(1)}, bf16[64,1536]{1,0:T(8,128)(2,1)S(1)}, u32[]{:S(2)}, u32[]{:S(2)}) collective-permute-start(bf16[64,1536]{1,0:T(8,128)(2,1)S(1)} %get-tuple-element.164.refs_1_), channel_id=1, source_target_pairs={{0,2},{1,3},{2,4},{3,5},{4,6},{5,7},{6,0},{7,1},{8,10},{9,11},{10,... | collective-permute-start | bytes 589832 | tf_op jit(solution)/shard_map/ppermute | solution.py:85
  124.7 18.7 %collective-permute-start.38 = (bf16[64,1536]{1,0:T(8,128)(2,1)S(1)}, bf16[64,1536]{1,0:T(8,128)(2,1)S(1)}, u32[]{:S(2)}, u32[]{:S(2)}) collective-permute-start(bf16[64,1536]{1,0:T(8,128)(2,1)S(1)} %get-tuple-element.163.refs_0_), channel_id=1, source_target_pairs={{0,6},{1,7},{2,0},{3,1},{4,2},{5,3},{6,4},{7,5},{8,14},{9,15},{10,... | collective-permute-start | bytes 589832 | tf_op jit(solution)/shard_map/ppermute | solution.py:85
  127.7 15.8 %collective-permute-start.37 = (bf16[64,1536]{1,0:T(8,128)(2,1)S(1)}, bf16[64,1536]{1,0:T(8,128)(2,1)S(1)}, u32[]{:S(2)}, u32[]{:S(2)}) collective-permute-start(bf16[64,1536]{1,0:T(8,128)(2,1)S(1)} %collective-permute-done.36.refs_16_), channel_id=1, source_target_pairs={{0,6},{1,7},{2,0},{3,1},{4,2},{5,3},{6,4},{7,5},{8,14},{9,15},{10,... | collective-permute-start | bytes 589832 | tf_op jit(solution)/shard_map/ppermute | solution.py:85
  202.2 47.6 %collective-permute-start.58 = (bf16[512,2304]{1,0:T(8,128)(2,1)}, bf16[512,2304]{1,0:T(8,128)(2,1)}, u32[]{:S(2)}, u32[]{:S(2)}) collective-permute-start(bf16[512,2304]{1,0:T(8,128)(2,1)} %get-tuple-element.196), channel_id=1, source_target_pairs={{0,1},{1,0},{2,3},{3,2},{4,5},{5,4},{6,7},{7,6},{8,9},{9,8},{10,11... | collective-permute-start | bytes 7077896 | tf_op jit(solution)/shard_map/ppermute | solution.py:81
  202.3 22.2 %collective-permute-start.52 = (bf16[128,1536]{1,0:T(8,128)(2,1)S(1)}, bf16[128,1536]{1,0:T(8,128)(2,1)S(1)}, u32[]{:S(2)}, u32[]{:S(2)}) collective-permute-start(bf16[128,1536]{1,0:T(8,128)(2,1)S(1)} %get-tuple-element.188), channel_id=1, source_target_pairs={{0,6},{1,7},{2,0},{3,1},{4,2},{5,3},{6,4},{7,5},{8,14},{9,15},{10,... | collective-permute-start | bytes 1179656 | tf_op jit(solution)/shard_map/ppermute | solution.py:85
  204.6 19.8 %collective-permute-start.53 = (bf16[128,1536]{1,0:T(8,128)(2,1)S(1)}, bf16[128,1536]{1,0:T(8,128)(2,1)S(1)}, u32[]{:S(2)}, u32[]{:S(2)}) collective-permute-start(bf16[128,1536]{1,0:T(8,128)(2,1)S(1)} %get-tuple-element.189), channel_id=1, source_target_pairs={{0,4},{1,5},{2,6},{3,7},{4,0},{5,1},{6,2},{7,3},{8,12},{9,13},{10,... | collective-permute-start | bytes 1179656 | tf_op jit(solution)/shard_map/ppermute | solution.py:85
  204.6 21.0 %collective-permute-start.54 = (bf16[128,1536]{1,0:T(8,128)(2,1)S(1)}, bf16[128,1536]{1,0:T(8,128)(2,1)S(1)}, u32[]{:S(2)}, u32[]{:S(2)}) collective-permute-start(bf16[128,1536]{1,0:T(8,128)(2,1)S(1)} %get-tuple-element.190), channel_id=1, source_target_pairs={{0,2},{1,3},{2,4},{3,5},{4,6},{5,7},{6,0},{7,1},{8,10},{9,11},{10,... | collective-permute-start | bytes 1179656 | tf_op jit(solution)/shard_map/ppermute | solution.py:85
  230.1 19.6 %collective-permute-start.57 = (bf16[128,1664]{1,0:T(8,128)(2,1)S(1)}, bf16[128,1664]{1,0:T(8,128)(2,1)S(1)}, u32[]{:S(2)}, u32[]{:S(2)}) collective-permute-start(bf16[128,1664]{1,0:T(8,128)(2,1)S(1)} %get-tuple-element.195), channel_id=1, source_target_pairs={{0,2},{1,3},{2,4},{3,5},{4,6},{5,7},{6,0},{7,1},{8,10},{9,11},{10,... | collective-permute-start | bytes 1277960 | tf_op jit(solution)/shard_map/ppermute | solution.py:85
  250.5 32.9 %all-to-all-start = ((bf16[8,128,768]{2,1,0:T(8,128)(2,1)}), bf16[8,128,768]{2,1,0:T(8,128)(2,1)}, u32[]{:S(2)}, u32[]{:S(2)}) async-start(bf16[8,128,768]{2,1,0:T(8,128)(2,1)} %copy-done.3), calls=%async_computation | async-start | bytes 3145728 | tf_op jit(solution)/shard_map/all_to_all | solution.py:777
  346.2 21.1 %collective-permute-start.70 = (bf16[128,1664]{1,0:T(8,128)(2,1)S(1)}, bf16[128,1664]{1,0:T(8,128)(2,1)S(1)}, u32[]{:S(2)}, u32[]{:S(2)}) collective-permute-start(bf16[128,1664]{1,0:T(8,128)(2,1)S(1)} %get-tuple-element.222), channel_id=1, source_target_pairs={{0,6},{1,7},{2,0},{3,1},{4,2},{5,3},{6,4},{7,5},{8,14},{9,15},{10,... | collective-permute-start | bytes 1277960 | tf_op jit(solution)/shard_map/ppermute | solution.py:85
  346.9 20.4 %collective-permute-start.71 = (bf16[128,1664]{1,0:T(8,128)(2,1)S(1)}, bf16[128,1664]{1,0:T(8,128)(2,1)S(1)}, u32[]{:S(2)}, u32[]{:S(2)}) collective-permute-start(bf16[128,1664]{1,0:T(8,128)(2,1)S(1)} %get-tuple-element.223), channel_id=1, source_target_pairs={{0,4},{1,5},{2,6},{3,7},{4,0},{5,1},{6,2},{7,3},{8,12},{9,13},{10,... | collective-permute-start | bytes 1277960 | tf_op jit(solution)/shard_map/ppermute | solution.py:85
  347.1 22.3 %collective-permute-start.72 = (bf16[128,1664]{1,0:T(8,128)(2,1)S(1)}, bf16[128,1664]{1,0:T(8,128)(2,1)S(1)}, u32[]{:S(2)}, u32[]{:S(2)}) collective-permute-start(bf16[128,1664]{1,0:T(8,128)(2,1)S(1)} %get-tuple-element.224), channel_id=1, source_target_pairs={{0,2},{1,3},{2,4},{3,5},{4,6},{5,7},{6,0},{7,1},{8,10},{9,11},{10,... | collective-permute-start | bytes 1277960 | tf_op jit(solution)/shard_map/ppermute | solution.py:85
  370.2 91.1 %all-to-all-start.1 = ((bf16[8,288,1536]{2,1,0:T(8,128)(2,1)}), bf16[8,288,1536]{2,1,0:T(8,128)(2,1)}, u32[]{:S(2)}, u32[]{:S(2)}) async-start(bf16[8,288,1536]{2,1,0:T(8,128)(2,1)} %expert_grad.1), calls=%async_computation.1 | async-start | bytes 14155776 | tf_op jit(solution)/shard_map/all_to_all | solution.py:789
  381.8 17.9 %collective-permute-start.79 = (bf16[64,1536]{1,0:T(8,128)(2,1)S(1)}, bf16[64,1536]{1,0:T(8,128)(2,1)S(1)}, u32[]{:S(2)}, u32[]{:S(2)}) collective-permute-start(bf16[64,1536]{1,0:T(8,128)(2,1)S(1)} %get-tuple-element.266.refs_1_.refs_26_), channel_id=1, source_target_pairs={{0,6},{1,7},{2,0},{3,1},{4,2},{5,3},{6,4},{7,5},{8,14},{9,15},{10,... | collective-permute-start | bytes 589832 | tf_op jit(solution)/shard_map/ppermute | solution.py:85
  382.2 17.5 %collective-permute-start.75 = (bf16[64,1536]{1,0:T(8,128)(2,1)S(1)}, bf16[64,1536]{1,0:T(8,128)(2,1)S(1)}, u32[]{:S(2)}, u32[]{:S(2)}) collective-permute-start(bf16[64,1536]{1,0:T(8,128)(2,1)S(1)} %get-tuple-element.267.refs_2_.refs_27_), channel_id=1, source_target_pairs={{0,2},{1,3},{2,4},{3,5},{4,6},{5,7},{6,0},{7,1},{8,10},{9,11},{10,... | collective-permute-start | bytes 589832 | tf_op jit(solution)/shard_map/ppermute | solution.py:85
  405.3 16.3 %collective-permute-start.105 = (bf16[64,1536]{1,0:T(8,128)(2,1)S(1)}, bf16[64,1536]{1,0:T(8,128)(2,1)S(1)}, u32[]{:S(2)}, u32[]{:S(2)}) collective-permute-start(bf16[64,1536]{1,0:T(8,128)(2,1)S(1)} %get-tuple-element.266.refs_1_.refs_26_), channel_id=1, source_target_pairs={{0,1},{1,0},{2,3},{3,2},{4,5},{5,4},{6,7},{7,6},{8,9},{9,8},{10,11... | collective-permute-start | bytes 589832 | tf_op jit(solution)/shard_map/ppermute | solution.py:81
  405.3 19.5 %collective-permute-start.106 = (bf16[64,1536]{1,0:T(8,128)(2,1)S(1)}, bf16[64,1536]{1,0:T(8,128)(2,1)S(1)}, u32[]{:S(2)}, u32[]{:S(2)}) collective-permute-start(bf16[64,1536]{1,0:T(8,128)(2,1)S(1)} %get-tuple-element.267.refs_2_.refs_27_), channel_id=1, source_target_pairs={{0,1},{1,0},{2,3},{3,2},{4,5},{5,4},{6,7},{7,6},{8,9},{9,8},{10,11... | collective-permute-start | bytes 589832 | tf_op jit(solution)/shard_map/ppermute | solution.py:81
  461.3 28.7 %all-to-all-start.2 = ((bf16[8,208,512]{2,1,0:T(8,128)(2,1)}), bf16[8,208,512]{2,1,0:T(8,128)(2,1)S(1)}, u32[]{:S(2)}, u32[]{:S(2)}) async-start(bf16[8,208,512]{2,1,0:T(8,128)(2,1)} %attn_grad.1), calls=%async_computation.2 | async-start | bytes 3407872 | tf_op jit(solution)/shard_map/all_to_all | solution.py:804
  (200 other events, 2025.3 us)
Sparse Core Ops, SparseCore 0:
  10.5 45.8 all-gather.1
